TPU v7x, 32 devices: a whole 2x2x4 slice. The times are simulated.
32 devices in a mesh: ep: 8 (over z, y), tp: 4 (over x, core).
Axes of the slice: x: 2, y: 2, z: 4, core: 2. Of those that a mesh axis runs over, the one named last changes fastest.
Arguments:
- tokens: bfloat16 [4096, 2048], P('ep', 'tp'), may hold values from -6 to 6
- out_grad: bfloat16 [4096, 2048], P('ep', 'tp'), may hold values from -6 to 6
- first_gain: float32 [2048], replicated, may hold values from 0.5 to 1.5
- query_weight: bfloat16 [2048, 2048], P(None, 'tp'), may hold values from -0.125 to 0.125
- key_weight: bfloat16 [2048, 2048], P(None, 'tp'), may hold values from -0.125 to 0.125
- value_weight: bfloat16 [2048, 2048], P(None, 'tp'), may hold values from -0.125 to 0.125
- query_bias: float32 [2048], P('tp'), may hold values from -0.6 to 0.6
- key_bias: float32 [2048], P('tp'), may hold values from -0.6 to 0.6
- value_bias: float32 [2048], P('tp'), may hold values from -0.6 to 0.6
- output_weight: bfloat16 [2048, 2048], P('tp'), may hold values from -1.5 to 1.5
- second_gain: float32 [2048], replicated, may hold values from 0.5 to 1.5
- router_weight: bfloat16 [2048, 8], replicated, may hold values from -0.0625 to 0.0625
- shared_gate_weight: bfloat16 [2048, 5632], P(None, 'tp'), may hold values from -0.125 to 0.125
- shared_up_weight: bfloat16 [2048, 5632], P(None, 'tp'), may hold values from -0.125 to 0.125
- shared_down_weight: bfloat16 [5632, 2048], P('tp'), may hold values from -0.078125 to 0.078125
- switch_vector: bfloat16 [2048], replicated, may hold values from -0.125 to 0.125
- expert_gate_weight: bfloat16 [8, 2048, 1408], P('ep', None, 'tp'), may hold values from -0.125 to 0.125
- expert_up_weight: bfloat16 [8, 2048, 1408], P('ep', None, 'tp'), may hold values from -0.125 to 0.125
- expert_down_weight: bfloat16 [8, 1408, 2048], P('ep', 'tp'), may hold values from -0.625 to 0.625
- expert_ids: int32 [4096, 4], P('ep'), may hold values from 0 to 7, all different within a row
- pair_order: int32 [8, 2048], P('ep'), may hold values from 0 to 2047, each once within a row
Outputs:
- mixed: bfloat16 [4096, 2048], P('ep', 'tp')
- tokens_grad: bfloat16 [4096, 2048], P('ep', 'tp')
- first_gain_grad: float32 [2048], P('ep')
- query_weight_grad: float32 [2048, 2048], P('ep', 'tp')
- key_weight_grad: float32 [2048, 2048], P('ep', 'tp')
- value_weight_grad: float32 [2048, 2048], P('ep', 'tp')
- query_bias_grad: float32 [16, 128], P('tp', 'ep')
- key_bias_grad: float32 [16, 128], P('tp', 'ep')
- value_bias_grad: float32 [16, 128], P('tp', 'ep')
- output_weight_grad: float32 [2048, 2048], P('tp', 'ep')
- second_gain_grad: float32 [2048], P('ep')
- router_weight_grad: float32 [2048, 8], P('ep')
- shared_gate_grad: float32 [2048, 5632], P('ep', 'tp')
- shared_up_grad: float32 [2048, 5632], P('ep', 'tp')
- shared_down_grad: float32 [5632, 2048], P('tp', 'ep')
- switch_vector_grad: float32 [2048], P('ep')
- expert_gate_grad: float32 [8, 2048, 1408], P('ep', None, 'tp')
- expert_up_grad: float32 [8, 2048, 1408], P('ep', None, 'tp')
- expert_down_grad: float32 [8, 1408, 2048], P('ep', 'tp')
Inputs may be any that keep to these rules, and one draw needn't show every extreme that they name: `expert_ids`: each row names 4 different experts; every expert is named by some row. `pair_order`: each row holds every pair number t * 4 + k of its group of rows once.
All inputs are finite; a program needn't handle non-finite values.
Results may differ from a plain program's by a relative error of at most 0.024.
Values may be sent and summed in bfloat16 or wider, within the bound.
A program may use at most 320 MiB of HBM per device.

v0:
```python
import math

import jax
import jax.numpy as jnp
from jax import lax
from jax.sharding import PartitionSpec as P

HD = 128
BLOCK = 256
SPAN = 2


rope_theta = 1000000.0
norm_eps = 1e-06
masked_score = -1e30


def passed_along(value, axis, steps):
    count = lax.axis_size(axis)
    leading, last = (max(0, -steps), min(count, count - steps))
    return lax.ppermute(value, axis, [(source, source + steps) for source in range(leading, last)])


def rope_tables(row_count, head_dim, first_position):
    positions = jnp.arange(row_count, dtype=jnp.float32) + first_position.astype(jnp.float32)
    frequency = jnp.exp(
        jnp.arange(head_dim // 2, dtype=jnp.float32) * (-2.0 * math.log(rope_theta) / head_dim)
    )
    angles = positions[:, None] * frequency[None, :]
    return (jnp.cos(angles)[:, None, :], jnp.sin(angles)[:, None, :])


def rotate(values, cosine, sine_part):
    half_dim = values.shape[-1] // 2
    first_half = values[..., :half_dim]
    second_half = values[..., half_dim:]
    return jnp.concatenate(
        [
            first_half * cosine - second_half * sine_part,
            second_half * cosine + first_half * sine_part,
        ],
        axis=-1,
    )


def inner_rows(left_side, right_side):
    return lax.dot_general(
        left_side, right_side, (((0,), (0,)), ((), ())), preferred_element_type=jnp.float32
    )


def times_transpose(left_side, right_side):
    return lax.dot_general(
        left_side, right_side, (((1,), (1,)), ((), ())), preferred_element_type=jnp.float32
    )


def row_stats(values):
    inv_rms = lax.rsqrt(jnp.mean(values * values, axis=-1, keepdims=True) + norm_eps)
    return (values * inv_rms, inv_rms)


def norm_back(grad_rows, unit_rows, inv_rms, gain_vec):
    scaled = grad_rows * gain_vec
    return inv_rms * (scaled - unit_rows * jnp.mean(scaled * unit_rows, axis=-1, keepdims=True))


def softmax_rows(scores):
    row_max = jnp.max(scores, axis=-1, keepdims=True)
    powers = jnp.exp(scores - row_max)
    return powers / jnp.sum(powers, axis=-1, keepdims=True)


def to_experts(block_rows, local_count):
    sources, span_rows, col_count = block_rows.shape
    slot_count = span_rows // local_count
    shaped = block_rows.reshape(sources, local_count, slot_count, col_count)
    return shaped.swapaxes(0, 1).reshape(local_count, sources * slot_count, col_count)


def to_sources(block_rows, sources):
    local_count, rows_all, col_count = block_rows.shape
    slot_count = rows_all // sources
    shaped = block_rows.reshape(local_count, sources, slot_count, col_count)
    return shaped.swapaxes(0, 1).reshape(sources, local_count * slot_count, col_count)


def deliver(block_rows):
    arrived = lax.all_to_all(block_rows, "ep", split_axis=0, concat_axis=0, tiled=True)
    return arrived


def collect(block_rows):
    return lax.all_to_all(block_rows, "ep", split_axis=0, concat_axis=0, tiled=True)


def per_device(
    tokens,
    out_grad,
    first_gain,
    query_weight,
    key_weight,
    value_weight,
    query_bias,
    key_bias,
    value_bias,
    output_weight,
    second_gain,
    router_weight,
    shared_gate_weight,
    shared_up_weight,
    shared_down_weight,
    switch_vector,
    expert_gate_weight,
    expert_up_weight,
    expert_down_weight,
    expert_ids,
    pair_order,
):
    whole_in, whole_grad = (
        lax.all_gather(tokens, "tp", axis=1, tiled=True),
        lax.all_gather(out_grad, "tp", axis=1, tiled=True),
    )
    tok_count = whole_in.shape[0]
    model_dim = whole_in.shape[1]
    col_width = tokens.shape[1]
    col_start = lax.axis_index("tp") * col_width
    sources = lax.axis_size("ep")
    place_in_seq = lax.axis_index("ep") % SPAN
    has_earlier = place_in_seq > 0
    local_experts = expert_gate_weight.shape[0]
    expert_total = router_weight.shape[1]
    top_count = expert_ids.shape[1]
    pair_count = tok_count * top_count
    capacity = 9 * pair_count // (8 * expert_total)
    head_count = query_weight.shape[1] // HD
    score_scale = HD ** (-0.5)
    inputs_full = whole_in.astype(jnp.float32)
    unit_one, inv_one = row_stats(inputs_full)
    normed_one = (unit_one * first_gain).astype(jnp.bfloat16)
    query_lin = jnp.dot(normed_one, query_weight, preferred_element_type=jnp.float32) + query_bias
    key_lin = jnp.dot(normed_one, key_weight, preferred_element_type=jnp.float32) + key_bias
    value_lin = jnp.dot(normed_one, value_weight, preferred_element_type=jnp.float32) + value_bias
    cosine, sine_part = rope_tables(tok_count, HD, place_in_seq * tok_count)
    queries = rotate(query_lin.reshape(tok_count, head_count, HD), cosine, sine_part).astype(
        jnp.bfloat16
    )
    keys_rot = rotate(key_lin.reshape(tok_count, head_count, HD), cosine, sine_part).astype(
        jnp.bfloat16
    )
    values_all = value_lin.reshape(tok_count, head_count, HD).astype(jnp.bfloat16)
    earlier_keys, earlier_values = passed_along((keys_rot, values_all), "ep", 1)
    keys_both = jnp.concatenate([earlier_keys, keys_rot], axis=0)
    values_both = jnp.concatenate([earlier_values, values_all], axis=0)
    blocks = jnp.arange(tok_count) // BLOCK
    local_allowed = blocks[None, :] <= blocks[:, None]
    remote_allowed = jnp.broadcast_to(has_earlier, (tok_count, tok_count))
    allowed = jnp.concatenate([remote_allowed, local_allowed], axis=1)[None]

    def attention_scores():
        scored = (
            jnp.einsum("qhd,khd->hqk", queries, keys_both, preferred_element_type=jnp.float32)
            * score_scale
        )
        return jnp.where(allowed, scored, masked_score)

    scores = attention_scores()
    row_max = jnp.max(scores, axis=-1, keepdims=True)
    powers = jnp.exp(scores - row_max)
    totals = jnp.sum(powers, axis=-1, keepdims=True)
    log_total = row_max + jnp.log(totals)
    probs_low = (powers / totals).astype(jnp.bfloat16)
    context = jnp.einsum("hqk,khd->qhd", probs_low, values_both, preferred_element_type=jnp.float32)
    context = context.reshape(tok_count, head_count * HD).astype(jnp.bfloat16)
    attn_part = jnp.dot(context, output_weight, preferred_element_type=jnp.float32)
    attended = lax.psum(attn_part, "tp")
    hidden_one = inputs_full + attended
    unit_two, inv_two = row_stats(hidden_one)
    normed_two = (unit_two * second_gain).astype(jnp.bfloat16)
    logits = jnp.dot(normed_two, router_weight, preferred_element_type=jnp.float32)
    router_probs = softmax_rows(logits)
    gate_values = jnp.take_along_axis(router_probs, expert_ids, axis=1)
    switch = jax.nn.sigmoid(jnp.dot(normed_two, switch_vector, preferred_element_type=jnp.float32))
    flat_ids = expert_ids.reshape(-1)
    turn_order = pair_order.reshape(-1)
    in_turn = flat_ids[turn_order]
    onehot = (in_turn[:, None] == jnp.arange(expert_total, dtype=jnp.int32)[None, :]).astype(
        jnp.int32
    )
    earlier = jnp.cumsum(onehot, axis=0) - onehot
    turn_slot = jnp.sum(earlier * onehot, axis=1)
    slot_index = jnp.zeros((pair_count,), jnp.int32).at[turn_order].set(turn_slot)
    kept_pair = slot_index < capacity
    slot_rows = expert_total * capacity
    target = jnp.where(kept_pair, flat_ids * capacity + slot_index, slot_rows)
    pair_token = jnp.arange(pair_count, dtype=jnp.int32) // top_count
    slot_token = (
        jnp.full((slot_rows + 1,), tok_count, jnp.int32).at[target].set(pair_token)[:slot_rows]
    )
    slot_gate = (
        jnp.zeros((slot_rows + 1,), jnp.float32).at[target].set(gate_values.reshape(-1))[:slot_rows]
    )
    padded_two = jnp.concatenate([normed_two, jnp.zeros((1, model_dim), jnp.bfloat16)], axis=0)
    send_rows = padded_two[slot_token].reshape(sources, local_experts * capacity, model_dim)
    expert_rows = to_experts(deliver(send_rows), local_experts)
    gate_lin = jnp.einsum(
        "erd,edf->erf", expert_rows, expert_gate_weight, preferred_element_type=jnp.float32
    )
    up_lin = jnp.einsum(
        "erd,edf->erf", expert_rows, expert_up_weight, preferred_element_type=jnp.float32
    )
    gate_sig = jax.nn.sigmoid(gate_lin)
    gate_act = gate_lin * gate_sig
    expert_hidden = (gate_act * up_lin).astype(jnp.bfloat16)
    expert_part = jnp.einsum(
        "erf,efd->erd", expert_hidden, expert_down_weight, preferred_element_type=jnp.float32
    )
    shared_gate_lin = jnp.dot(normed_two, shared_gate_weight, preferred_element_type=jnp.float32)
    shared_up_lin = jnp.dot(normed_two, shared_up_weight, preferred_element_type=jnp.float32)
    shared_sig = jax.nn.sigmoid(shared_gate_lin)
    shared_act = shared_gate_lin * shared_sig
    shared_hidden = (shared_act * shared_up_lin).astype(jnp.bfloat16)
    shared_part = jnp.dot(shared_hidden, shared_down_weight, preferred_element_type=jnp.float32)
    expert_cols, shared_cols = (
        lax.psum_scatter(expert_part.reshape(-1, model_dim), "tp", scatter_dimension=1, tiled=True),
        lax.psum_scatter(shared_part, "tp", scatter_dimension=1, tiled=True),
    )
    returned = collect(
        to_sources(expert_cols.astype(jnp.bfloat16).reshape(local_experts, -1, col_width), sources)
    )
    back_flat = jnp.concatenate(
        [returned.reshape(slot_rows, col_width), jnp.zeros((1, col_width), jnp.bfloat16)], axis=0
    )
    pair_out = back_flat[target].astype(jnp.float32).reshape(tok_count, top_count, col_width)
    routed = jnp.sum(gate_values[:, :, None] * pair_out, axis=1)
    hidden_cols = lax.dynamic_slice_in_dim(hidden_one, col_start, col_width, 1)
    layer_out = (hidden_cols + switch[:, None] * shared_cols + routed).astype(jnp.bfloat16)
    grad_full = whole_grad.astype(jnp.float32)
    grad_cols = out_grad.astype(jnp.float32)
    gate_part = jnp.sum(pair_out * grad_cols[:, None, :], axis=-1)
    switch_part = jnp.sum(grad_cols * shared_cols, axis=-1)
    gate_grad, switch_grad = lax.psum((gate_part, switch_part), "tp")
    padded_grad = jnp.concatenate([whole_grad, jnp.zeros((1, model_dim), jnp.bfloat16)], axis=0)
    send_grads = (slot_gate[:, None] * padded_grad[slot_token].astype(jnp.float32)).astype(
        jnp.bfloat16
    )
    expert_grads = to_experts(
        deliver(send_grads.reshape(sources, local_experts * capacity, model_dim)), local_experts
    )
    hidden_grad = jnp.einsum(
        "erd,efd->erf", expert_grads, expert_down_weight, preferred_element_type=jnp.float32
    )
    gate_lin_grad = (hidden_grad * up_lin * gate_sig * (1.0 + gate_lin * (1.0 - gate_sig))).astype(
        jnp.bfloat16
    )
    up_lin_grad = (hidden_grad * gate_act).astype(jnp.bfloat16)
    expert_down_grad = jnp.einsum(
        "erf,erd->efd", expert_hidden, expert_grads, preferred_element_type=jnp.float32
    )
    expert_gate_grad = jnp.einsum(
        "erd,erf->edf", expert_rows, gate_lin_grad, preferred_element_type=jnp.float32
    )
    expert_up_grad = jnp.einsum(
        "erd,erf->edf", expert_rows, up_lin_grad, preferred_element_type=jnp.float32
    )
    rows_grad = jnp.einsum(
        "erf,edf->erd", gate_lin_grad, expert_gate_weight, preferred_element_type=jnp.float32
    )
    rows_grad = rows_grad + jnp.einsum(
        "erf,edf->erd", up_lin_grad, expert_up_weight, preferred_element_type=jnp.float32
    )
    rows_grad_cols = lax.psum_scatter(
        rows_grad.reshape(-1, model_dim), "tp", scatter_dimension=1, tiled=True
    )
    returned_grad = collect(
        to_sources(
            rows_grad_cols.astype(jnp.bfloat16).reshape(local_experts, -1, col_width), sources
        )
    )
    back_grad = jnp.concatenate(
        [returned_grad.reshape(slot_rows, col_width), jnp.zeros((1, col_width), jnp.bfloat16)],
        axis=0,
    )
    routed_grad = jnp.sum(
        back_grad[target].astype(jnp.float32).reshape(tok_count, top_count, col_width), axis=1
    )
    shared_out_grad = (switch[:, None] * grad_full).astype(jnp.bfloat16)
    shared_hidden_grad = times_transpose(shared_out_grad, shared_down_weight)
    shared_gate_lin_grad = (
        shared_hidden_grad
        * shared_up_lin
        * shared_sig
        * (1.0 + shared_gate_lin * (1.0 - shared_sig))
    ).astype(jnp.bfloat16)
    shared_up_lin_grad = (shared_hidden_grad * shared_act).astype(jnp.bfloat16)
    shared_down_grad = inner_rows(shared_hidden, shared_out_grad)
    shared_gate_grad = inner_rows(normed_two, shared_gate_lin_grad)
    shared_up_grad = inner_rows(normed_two, shared_up_lin_grad)
    normed_grad = times_transpose(shared_gate_lin_grad, shared_gate_weight) + times_transpose(
        shared_up_lin_grad, shared_up_weight
    )
    normed_grad = normed_grad + lax.dynamic_update_slice_in_dim(
        jnp.zeros_like(normed_grad), routed_grad, col_start, 1
    )
    normed_grad = lax.psum(normed_grad, "tp")
    picked = (
        expert_ids[:, :, None] == jnp.arange(expert_total, dtype=jnp.int32)[None, None, :]
    ).astype(jnp.float32)
    probs_grad = jnp.sum(picked * gate_grad[:, :, None], axis=1)
    logit_grad = (
        router_probs * (probs_grad - jnp.sum(router_probs * probs_grad, axis=-1, keepdims=True))
    ).astype(jnp.bfloat16)
    router_grad = inner_rows(normed_two, logit_grad)
    switch_lin_grad = switch_grad * switch * (1.0 - switch)
    switch_vector_grad = jnp.dot(switch_lin_grad, normed_two, preferred_element_type=jnp.float32)
    normed_grad = normed_grad + times_transpose(logit_grad, router_weight)
    normed_grad = (
        normed_grad + switch_lin_grad[:, None] * switch_vector.astype(jnp.float32)[None, :]
    )
    second_gain_grad = jnp.sum(normed_grad * unit_two, axis=0)
    hidden_grad_one = grad_full + norm_back(normed_grad, unit_two, inv_two, second_gain)
    attended_grad = hidden_grad_one.astype(jnp.bfloat16)
    output_grad = inner_rows(context, attended_grad)
    context_grad = (
        times_transpose(attended_grad, output_weight)
        .astype(jnp.bfloat16)
        .reshape(tok_count, head_count, HD)
    )
    scores = attention_scores()
    attn_probs = jnp.exp(scores - log_total)
    probs_again = attn_probs.astype(jnp.bfloat16)
    probs_grad_att = jnp.einsum(
        "qhd,khd->hqk", context_grad, values_both, preferred_element_type=jnp.float32
    )
    values_both_grad = jnp.einsum(
        "hqk,qhd->khd", probs_again, context_grad, preferred_element_type=jnp.float32
    )
    scores_grad = (
        attn_probs * (probs_grad_att - jnp.sum(attn_probs * probs_grad_att, axis=-1, keepdims=True))
    ).astype(jnp.bfloat16)
    queries_grad = (
        jnp.einsum("hqk,khd->qhd", scores_grad, keys_both, preferred_element_type=jnp.float32)
        * score_scale
    )
    keys_both_grad = (
        jnp.einsum("hqk,qhd->khd", scores_grad, queries, preferred_element_type=jnp.float32)
        * score_scale
    )
    later_keys_grad, later_values_grad = passed_along(
        (keys_both_grad[:tok_count], values_both_grad[:tok_count]), "ep", -1
    )
    keep_later = jnp.where(has_earlier, 0.0, 1.0).astype(jnp.float32)
    keys_grad = keys_both_grad[tok_count:] + keep_later * later_keys_grad
    values_grad = values_both_grad[tok_count:] + keep_later * later_values_grad
    value_lin_grad = values_grad.reshape(tok_count, head_count * HD).astype(jnp.bfloat16)
    query_lin_grad = (
        rotate(queries_grad, cosine, -sine_part)
        .reshape(tok_count, head_count * HD)
        .astype(jnp.bfloat16)
    )
    key_lin_grad = (
        rotate(keys_grad, cosine, -sine_part)
        .reshape(tok_count, head_count * HD)
        .astype(jnp.bfloat16)
    )
    query_grad = inner_rows(normed_one, query_lin_grad)
    key_grad = inner_rows(normed_one, key_lin_grad)
    value_grad = inner_rows(normed_one, value_lin_grad)
    query_bias_grad = jnp.sum(query_lin_grad.astype(jnp.float32), axis=0).reshape(head_count, HD)
    key_bias_grad = jnp.sum(key_lin_grad.astype(jnp.float32), axis=0).reshape(head_count, HD)
    value_bias_grad = jnp.sum(value_lin_grad.astype(jnp.float32), axis=0).reshape(head_count, HD)
    normed_one_grad = times_transpose(query_lin_grad, query_weight) + times_transpose(
        key_lin_grad, key_weight
    )
    normed_one_grad = normed_one_grad + times_transpose(value_lin_grad, value_weight)
    normed_one_grad = lax.psum(normed_one_grad.astype(jnp.bfloat16), "tp").astype(jnp.float32)
    first_gain_grad = jnp.sum(normed_one_grad * unit_one, axis=0)
    input_grad = hidden_grad_one + norm_back(normed_one_grad, unit_one, inv_one, first_gain)
    tokens_grad = lax.dynamic_slice_in_dim(input_grad, col_start, col_width, 1).astype(jnp.bfloat16)
    reduced = (
        lax.psum_scatter(
            first_gain_grad.astype(jnp.bfloat16), "ep", scatter_dimension=0, tiled=True
        ).astype(jnp.float32),
        lax.psum_scatter(
            query_grad.astype(jnp.bfloat16), "ep", scatter_dimension=0, tiled=True
        ).astype(jnp.float32),
        lax.psum_scatter(
            key_grad.astype(jnp.bfloat16), "ep", scatter_dimension=0, tiled=True
        ).astype(jnp.float32),
        lax.psum_scatter(
            value_grad.astype(jnp.bfloat16), "ep", scatter_dimension=0, tiled=True
        ).astype(jnp.float32),
        lax.psum_scatter(
            query_bias_grad.astype(jnp.bfloat16), "ep", scatter_dimension=1, tiled=True
        ).astype(jnp.float32),
        lax.psum_scatter(
            key_bias_grad.astype(jnp.bfloat16), "ep", scatter_dimension=1, tiled=True
        ).astype(jnp.float32),
        lax.psum_scatter(
            value_bias_grad.astype(jnp.bfloat16), "ep", scatter_dimension=1, tiled=True
        ).astype(jnp.float32),
        lax.psum_scatter(
            output_grad.astype(jnp.bfloat16), "ep", scatter_dimension=1, tiled=True
        ).astype(jnp.float32),
        lax.psum_scatter(
            second_gain_grad.astype(jnp.bfloat16), "ep", scatter_dimension=0, tiled=True
        ).astype(jnp.float32),
        lax.psum_scatter(
            router_grad.astype(jnp.bfloat16), "ep", scatter_dimension=0, tiled=True
        ).astype(jnp.float32),
        lax.psum_scatter(
            shared_gate_grad.astype(jnp.bfloat16), "ep", scatter_dimension=0, tiled=True
        ).astype(jnp.float32),
        lax.psum_scatter(
            shared_up_grad.astype(jnp.bfloat16), "ep", scatter_dimension=0, tiled=True
        ).astype(jnp.float32),
        lax.psum_scatter(
            shared_down_grad.astype(jnp.bfloat16), "ep", scatter_dimension=1, tiled=True
        ).astype(jnp.float32),
        lax.psum_scatter(
            switch_vector_grad.astype(jnp.bfloat16), "ep", scatter_dimension=0, tiled=True
        ).astype(jnp.float32),
    )
    return (
        layer_out,
        tokens_grad,
        reduced[0],
        reduced[1],
        reduced[2],
        reduced[3],
        reduced[4],
        reduced[5],
        reduced[6],
        reduced[7],
        reduced[8],
        reduced[9],
        reduced[10],
        reduced[11],
        reduced[12],
        reduced[13],
        expert_gate_grad,
        expert_up_grad,
        expert_down_grad,
    )


def solution(mesh):
    return jax.shard_map(
        per_device,
        mesh=mesh,
        in_specs=(
            P("ep", "tp"),
            P("ep", "tp"),
            P(),
            P(None, "tp"),
            P(None, "tp"),
            P(None, "tp"),
            P("tp"),
            P("tp"),
            P("tp"),
            P("tp", None),
            P(),
            P(),
            P(None, "tp"),
            P(None, "tp"),
            P("tp", None),
            P(),
            P("ep", None, "tp"),
            P("ep", None, "tp"),
            P("ep", "tp", None),
            P("ep", None),
            P("ep", None),
        ),
        out_specs=(
            P("ep", "tp"),
            P("ep", "tp"),
            P("ep"),
            P("ep", "tp"),
            P("ep", "tp"),
            P("ep", "tp"),
            P("tp", "ep"),
            P("tp", "ep"),
            P("tp", "ep"),
            P("tp", "ep"),
            P("ep"),
            P("ep", None),
            P("ep", "tp"),
            P("ep", "tp"),
            P("tp", "ep"),
            P("ep"),
            P("ep", None, "tp"),
            P("ep", None, "tp"),
            P("ep", "tp", None),
        ),
        check_vma=False,
    )
```

profile of v0, /device:TPU:9, one launch (start us, length us, event | category | flops | bytes accessed | tf_op | source)
XLA Modules:
  0.0 2032.5 jit_solution(17963663743530084487)
XLA Ops:
  9.9 23.9 %all-gather.3.cloned.1.call-done = bf16[512,2048]{1,0:T(8,128)(2,1)} async-done(((bf16[512,512]{1,0:T(8,128)(2,1)}), bf16[512,2048]{1,0:T(8,128)(2,1)}) %all-gather.3.cloned.1.call-update) | async-done | bytes 2097168 | tf_op jit(solution)/shard_map/all_gather | solution.py:121
  93.0 11.8 gather_fusion
  124.5 52.5 %all-reduce.14.cloned.1.call-done = f32[512,2048]{1,0:T(8,128)} async-done(((f32[512,2048]{1,0:T(8,128)}), f32[512,2048]{1,0:T(8,128)}) %all-reduce.14.cloned.1.call-update) | async-done | bytes 4194320 | tf_op jit(solution)/shard_map/psum | solution.py:176
  185.7 20.2 gather_fusion.1
  212.4 25.2 %all-gather.5.cloned.1.call-done = bf16[512,2048]{1,0:T(8,128)(2,1)} async-done(((bf16[512,512]{1,0:T(8,128)(2,1)}), bf16[512,2048]{1,0:T(8,128)(2,1)}) %all-gather.5.cloned.1.call-update) | async-done | bytes 2097168 | tf_op jit(solution)/shard_map/all_gather | solution.py:122
  240.8 20.2 gather_fusion.3
  264.5 12.5 gather_fusion.5
  294.8 120.4 %all-to-all-done = bf16[8,288,2048]{2,1,0:T(8,128)(2,1)} async-done(((bf16[8,288,2048]{2,1,0:T(8,128)(2,1)}), bf16[8,288,2048]{2,1,0:T(8,128)(2,1)}, u32[]{:S(2)}, u32[]{:S(2)}) %all-to-all-start) | async-done | bytes 9437216 | tf_op jit(solution)/shard_map/all_to_all | solution.py:89
  439.6 185.4 %all-to-all-done.2 = bf16[8,288,2048]{2,1,0:T(8,128)(2,1)} async-done(((bf16[8,288,2048]{2,1,0:T(8,128)(2,1)}), bf16[8,288,2048]{2,1,0:T(8,128)(2,1)}, u32[]{:S(2)}, u32[]{:S(2)}) %all-to-all-start.2) | async-done | bytes 9437216 | tf_op jit(solution)/shard_map/all_to_all | solution.py:89
  645.9 12.7 convolution_add_fusion
  660.0 14.2 fusion.17
  704.2 94.6 %reduce-scatter.25.cloned.1.call-done = f32[2304,512]{1,0:T(8,128)} async-done(((f32[2304,2048]{1,0:T(8,128)}), f32[2304,512]{1,0:T(8,128)}) %reduce-scatter.25.cloned.1.call-update) | async-done | bytes 4718608 | tf_op jit(solution)/shard_map/reduce_scatter | solution.py:272
  824.9 35.5 %all-to-all-done.3 = bf16[8,288,512]{2,1,0:T(8,128)(2,1)} async-done(((bf16[8,288,512]{2,1,0:T(8,128)(2,1)}), bf16[8,288,512]{2,1,0:T(8,128)(2,1)}, u32[]{:S(2)}, u32[]{:S(2)}) %all-to-all-start.3) | async-done | bytes 2359328 | tf_op jit(solution)/shard_map/all_to_all | solution.py:94
  911.9 28.8 %reduce-scatter.23.cloned.1.call-done = f32[2304,512]{1,0:T(8,128)} async-done(((f32[2304,2048]{1,0:T(8,128)}), f32[2304,512]{1,0:T(8,128)}) %reduce-scatter.23.cloned.1.call-update) | async-done | bytes 4718608 | tf_op jit(solution)/shard_map/reduce_scatter | solution.py:225
  951.5 51.0 %all-to-all-done.1 = bf16[8,288,512]{2,1,0:T(8,128)(2,1)} async-done(((bf16[8,288,512]{2,1,0:T(8,128)(2,1)}), bf16[8,288,512]{2,1,0:T(8,128)(2,1)}, u32[]{:S(2)}, u32[]{:S(2)}) %all-to-all-start.1) | async-done | bytes 2359328 | tf_op jit(solution)/shard_map/all_to_all | solution.py:94
  1031.8 15.7 all-reduce.8
  1047.8 29.3 %all-reduce.16.cloned.1.call-done = f32[512,2048]{1,0:T(8,128)} async-done(((f32[512,2048]{1,0:T(8,128)}), f32[512,2048]{1,0:T(8,128)}) %all-reduce.16.cloned.1.call-update) | async-done | bytes 4194320 | tf_op jit(solution)/shard_map/psum | solution.py:305
  1110.6 42.3 %collective-permute-done.2 = f32[512,4,128]{2,0,1:T(8,128)} collective-permute-done((f32[512,4,128]{2,0,1:T(8,128)}, f32[512,4,128]{2,0,1:T(8,128)}, u32[]{:S(2)}, u32[]{:S(2)}) %collective-permute-start.2) | collective-permute-done | bytes 1048608 | tf_op jit(solution)/shard_map/ppermute | solution.py:21
  1155.9 24.9 %collective-permute-done.3 = f32[512,4,128]{2,0,1:T(8,128)S(1)} collective-permute-done((f32[512,4,128]{2,0,1:T(8,128)S(1)}, f32[512,4,128]{2,0,1:T(8,128)S(1)}, u32[]{:S(2)}, u32[]{:S(2)}) %collective-permute-start.3) | collective-permute-done | bytes 1048608 | tf_op jit(solution)/shard_map/ppermute | solution.py:21
  1222.7 12.5 reduce-scatter.41.cloned.1.call-done
  1237.5 111.6 %reduce-scatter.39.cloned.1.call-done = bf16[256,1408]{1,0:T(8,128)(2,1)} async-done(((bf16[2048,1408]{1,0:T(8,128)(2,1)}), bf16[256,1408]{1,0:T(8,128)(2,1)}) %reduce-scatter.39.cloned.1.call-update) | async-done | bytes 720912 | tf_op jit(solution)/shard_map/reduce_scatter | solution.py:414
  1351.4 111.4 %reduce-scatter.37.cloned.1.call-done = bf16[256,1408]{1,0:T(8,128)(2,1)} async-done(((bf16[2048,1408]{1,0:T(8,128)(2,1)}), bf16[256,1408]{1,0:T(8,128)(2,1)}) %reduce-scatter.37.cloned.1.call-update) | async-done | bytes 720912 | tf_op jit(solution)/shard_map/reduce_scatter | solution.py:411
  1497.2 20.4 %reduce-scatter.35.cloned.1.call-done = bf16[256,8]{0,1:T(8,128)(2,1)} async-done(((bf16[2048,8]{0,1:T(8,128)(2,1)}), bf16[256,8]{0,1:T(8,128)(2,1)}) %reduce-scatter.35.cloned.1.call-update) | async-done | bytes 4112 | tf_op jit(solution)/shard_map/reduce_scatter | solution.py:408
  1518.8 55.2 %reduce-scatter.47.cloned.1.call-done = bf16[16,4]{1,0:T(8,128)(2,1)} async-done(((bf16[128,4]{1,0:T(8,128)(2,1)}), bf16[16,4]{1,0:T(8,128)(2,1)}) %reduce-scatter.47.cloned.1.call-update) | async-done | bytes 144
  1575.4 55.3 %reduce-scatter.45.cloned.1.call-done = bf16[16,4]{1,0:T(8,128)(2,1)} async-done(((bf16[128,4]{1,0:T(8,128)(2,1)}), bf16[16,4]{1,0:T(8,128)(2,1)}) %reduce-scatter.45.cloned.1.call-update) | async-done | bytes 144
  1632.1 55.2 %reduce-scatter.43.cloned.1.call-done = bf16[16,4]{1,0:T(8,128)(2,1)} async-done(((bf16[128,4]{1,0:T(8,128)(2,1)}), bf16[16,4]{1,0:T(8,128)(2,1)}) %reduce-scatter.43.cloned.1.call-update) | async-done | bytes 144
  1688.6 53.7 %all-reduce.18.cloned.1.call-done = bf16[512,2048]{1,0:T(8,128)(2,1)} async-done(((bf16[512,2048]{1,0:T(8,128)(2,1)}), bf16[512,2048]{1,0:T(8,128)(2,1)}) %all-reduce.18.cloned.1.call-update) | async-done | bytes 2097168 | tf_op jit(solution)/shard_map/psum | solution.py:376
  1749.2 27.7 %all-reduce.9 = (bf16[2048]{0:T(1024)(128)(2,1)S(1)}, bf16[2048]{0:T(1024)(128)(2,1)S(1)}, bf16[2048]{0:T(1024)(128)(2,1)S(1)}) all-reduce(bf16[2048]{0:T(1024)(128)(2,1)S(1)} %get-tuple-element.21, bf16[2048]{0:T(1024)(128)(2,1)S(1)} %get-tuple-element.19, ...), channel_id=5, replica_groups=mesh['ep'=8,'tp'=4] {'ep'}, use_global_device_ids=true, to_apply=%region_30.31.clone | all-reduce | flops 6144 | bytes 24576
  1781.7 31.1 %reduce-scatter.33.cloned.1.call-done = bf16[512,256]{1,0:T(8,128)(2,1)} async-done(((bf16[512,2048]{1,0:T(8,128)(2,1)}), bf16[512,256]{1,0:T(8,128)(2,1)}) %reduce-scatter.33.cloned.1.call-update) | async-done | bytes 262160 | tf_op jit(solution)/shard_map/reduce_scatter | solution.py:402
  1814.7 68.5 %reduce-scatter.27.cloned.1.call-done = bf16[256,512]{1,0:T(8,128)(2,1)} async-done(((bf16[2048,512]{1,0:T(8,128)(2,1)}), bf16[256,512]{1,0:T(8,128)(2,1)}) %reduce-scatter.27.cloned.1.call-update) | async-done | bytes 262160 | tf_op jit(solution)/shard_map/reduce_scatter | solution.py:384
  1885.0 68.7 %reduce-scatter.29.cloned.1.call-done = bf16[256,512]{1,0:T(8,128)(2,1)} async-done(((bf16[2048,512]{1,0:T(8,128)(2,1)}), bf16[256,512]{1,0:T(8,128)(2,1)}) %reduce-scatter.29.cloned.1.call-update) | async-done | bytes 262160 | tf_op jit(solution)/shard_map/reduce_scatter | solution.py:387
  1955.4 68.3 %reduce-scatter.31.cloned.1.call-done = bf16[256,512]{1,0:T(8,128)(2,1)} async-done(((bf16[2048,512]{1,0:T(8,128)(2,1)}), bf16[256,512]{1,0:T(8,128)(2,1)}) %reduce-scatter.31.cloned.1.call-update) | async-done | bytes 262160 | tf_op jit(solution)/shard_map/reduce_scatter | solution.py:390
  (366 shorter events, 455.5 us)
Async XLA Ops:
  7.2 81.6 %copy-start = (bf16[512,2048]{1,0:T(8,128)(2,1)S(1)}, bf16[512,2048]{1,0:T(8,128)(2,1)}, u32[]{:S(2)}) copy-start(bf16[512,2048]{1,0:T(8,128)(2,1)} %param.30) | copy-start | bytes 6291460
  7.2 26.6 %all-gather.3.cloned.1.call-start = ((), (), s32[]{:S(2)}) async-start(), calls=%async_computation.18 | async-start | bytes 2621440 | tf_op jit(solution)/shard_map/all_gather | solution.py:121
  8.0 169.0 %all-reduce.14.cloned.1.call-start = ((), (), s32[]{:S(2)}) async-start(), calls=%async_computation.19 | async-start | bytes 8388608 | tf_op jit(solution)/shard_map/psum | solution.py:176
  58.3 16.0 collective-permute-start.1
  65.6 20.0 collective-permute-start
  124.5 57.9 %copy-start.53 = (f32[2048]{0:T(1024)S(1)}, f32[2048]{0:T(1024)}, u32[]{:S(2)}) copy-start(f32[2048]{0:T(1024)} %param.31) | copy-start | bytes 24580
  205.8 209.3 %all-to-all-start = ((bf16[8,288,2048]{2,1,0:T(8,128)(2,1)}), bf16[8,288,2048]{2,1,0:T(8,128)(2,1)}, u32[]{:S(2)}, u32[]{:S(2)}) async-start(bf16[8,288,2048]{2,1,0:T(8,128)(2,1)} %bitcast.149), calls=%async_computation.1 | async-start | bytes 18874368 | tf_op jit(solution)/shard_map/all_to_all | solution.py:89
  211.3 26.3 %all-gather.5.cloned.1.call-start = ((), (), s32[]{:S(2)}) async-start(), calls=%async_computation.22 | async-start | bytes 2621440 | tf_op jit(solution)/shard_map/all_gather | solution.py:122
  415.2 209.8 %all-to-all-start.2 = ((bf16[8,288,2048]{2,1,0:T(8,128)(2,1)}), bf16[8,288,2048]{2,1,0:T(8,128)(2,1)}, u32[]{:S(2)}, u32[]{:S(2)}) async-start(bf16[8,288,2048]{2,1,0:T(8,128)(2,1)} %fusion), calls=%async_computation.4 | async-start | bytes 18874368 | tf_op jit(solution)/shard_map/all_to_all | solution.py:89
  420.9 377.9 %reduce-scatter.25.cloned.1.call-start = ((), (), s32[]{:S(2)}) async-start(), calls=%async_computation.23 | async-start | bytes 23592960 | tf_op jit(solution)/shard_map/reduce_scatter | solution.py:272
  658.7 282.0 %reduce-scatter.23.cloned.1.call-start = ((), (), s32[]{:S(2)}) async-start(), calls=%async_computation.21 | async-start | bytes 23592960 | tf_op jit(solution)/shard_map/reduce_scatter | solution.py:225
  674.2 354.5 %reduce-scatter.21.cloned.1.call-start = ((), (), s32[]{:S(2)}) async-start(), calls=%async_computation.20 | async-start | bytes 5242880 | tf_op jit(solution)/shard_map/reduce_scatter | solution.py:226
  802.8 57.6 %all-to-all-start.3 = ((bf16[8,288,512]{2,1,0:T(8,128)(2,1)}), bf16[8,288,512]{2,1,0:T(8,128)(2,1)}, u32[]{:S(2)}, u32[]{:S(2)}) async-start(bf16[8,288,512]{2,1,0:T(8,128)(2,1)} %bitcast.151), calls=%async_computation.6 | async-start | bytes 4718592 | tf_op jit(solution)/shard_map/all_to_all | solution.py:94
  808.3 268.7 %all-reduce.16.cloned.1.call-start = ((), (), s32[]{:S(2)}) async-start(), calls=%async_computation.24 | async-start | bytes 8388608 | tf_op jit(solution)/shard_map/psum | solution.py:305
  887.2 348.0 %reduce-scatter.41.cloned.1.call-start = ((), (), s32[]{:S(2)}) async-start(), calls=%async_computation.33 | async-start | bytes 6488064 | tf_op jit(solution)/shard_map/reduce_scatter | solution.py:417
  895.1 454.0 %reduce-scatter.39.cloned.1.call-start = ((), (), s32[]{:S(2)}) async-start(), calls=%async_computation.32 | async-start | bytes 6488064 | tf_op jit(solution)/shard_map/reduce_scatter | solution.py:414
  903.9 559.0 %reduce-scatter.37.cloned.1.call-start = ((), (), s32[]{:S(2)}) async-start(), calls=%async_computation.31 | async-start | bytes 6488064 | tf_op jit(solution)/shard_map/reduce_scatter | solution.py:411
  944.8 57.8 %all-to-all-start.1 = ((bf16[8,288,512]{2,1,0:T(8,128)(2,1)}), bf16[8,288,512]{2,1,0:T(8,128)(2,1)}, u32[]{:S(2)}, u32[]{:S(2)}) async-start(bf16[8,288,512]{2,1,0:T(8,128)(2,1)} %bitcast.152), calls=%async_computation.3 | async-start | bytes 4718592 | tf_op jit(solution)/shard_map/all_to_all | solution.py:94
  950.4 567.2 %reduce-scatter.35.cloned.1.call-start = ((), (), s32[]{:S(2)}) async-start(), calls=%async_computation.30 | async-start | bytes 36864 | tf_op jit(solution)/shard_map/reduce_scatter | solution.py:408
  1028.7 48.3 %copy-start.49 = (bf16[2048,8]{0,1:T(8,128)(2,1)S(1)}, bf16[2048,8]{0,1:T(8,128)(2,1)}, u32[]{:S(2)}) copy-start(bf16[2048,8]{0,1:T(8,128)(2,1)} %param.32) | copy-start | bytes 98308
  1028.7 48.3 %copy-start.54 = (f32[2048]{0:T(1024)S(1)}, f32[2048]{0:T(1024)}, u32[]{:S(2)}) copy-start(f32[2048]{0:T(1024)} %param.31) | copy-start | bytes 24580
  1095.2 57.6 %collective-permute-start.2 = (f32[512,4,128]{2,0,1:T(8,128)}, f32[512,4,128]{2,0,1:T(8,128)}, u32[]{:S(2)}, u32[]{:S(2)}) collective-permute-start(f32[512,4,128]{2,0,1:T(8,128)} %slice.86), channel_id=1, source_target_pairs={{4,0},{8,4},{12,8},{16,12},{20,16},{24,20},{28,24},{5,1},{9,5},{13... | collective-permute-start | bytes 3145736 | tf_op jit(solution)/shard_map/ppermute | solution.py:21
  1100.9 473.2 %reduce-scatter.47.cloned.1.call-start = ((), (), s32[]{:S(2)}) async-start(), calls=%async_computation.36 | async-start | bytes 36864
  1106.8 74.0 %collective-permute-start.3 = (f32[512,4,128]{2,0,1:T(8,128)S(1)}, f32[512,4,128]{2,0,1:T(8,128)S(1)}, u32[]{:S(2)}, u32[]{:S(2)}) collective-permute-start(f32[512,4,128]{2,0,1:T(8,128)S(1)} %slice.90), channel_id=1, source_target_pairs={{4,0},{8,4},{12,8},{16,12},{20,16},{24,20},{28,24},{5,1},{9,5},{13... | collective-permute-start | bytes 3145736 | tf_op jit(solution)/shard_map/ppermute | solution.py:21
  1188.1 442.7 %reduce-scatter.45.cloned.1.call-start = ((), (), s32[]{:S(2)}) async-start(), calls=%async_computation.35 | async-start | bytes 36864
  1192.3 495.0 %reduce-scatter.43.cloned.1.call-start = ((), (), s32[]{:S(2)}) async-start(), calls=%async_computation.34 | async-start | bytes 36864
  1200.0 542.2 %all-reduce.18.cloned.1.call-start = ((), (), s32[]{:S(2)}) async-start(), calls=%async_computation.25 | async-start | bytes 4194304 | tf_op jit(solution)/shard_map/psum | solution.py:376
  1207.0 605.9 %reduce-scatter.33.cloned.1.call-start = ((), (), s32[]{:S(2)}) async-start(), calls=%async_computation.29 | async-start | bytes 2359296 | tf_op jit(solution)/shard_map/reduce_scatter | solution.py:402
  1212.1 671.1 %reduce-scatter.27.cloned.1.call-start = ((), (), s32[]{:S(2)}) async-start(), calls=%async_computation.26 | async-start | bytes 2359296 | tf_op jit(solution)/shard_map/reduce_scatter | solution.py:384
  1216.7 737.0 %reduce-scatter.29.cloned.1.call-start = ((), (), s32[]{:S(2)}) async-start(), calls=%async_computation.27 | async-start | bytes 2359296 | tf_op jit(solution)/shard_map/reduce_scatter | solution.py:387
  1221.1 802.7 %reduce-scatter.31.cloned.1.call-start = ((), (), s32[]{:S(2)}) async-start(), calls=%async_computation.28 | async-start | bytes 2359296 | tf_op jit(solution)/shard_map/reduce_scatter | solution.py:390
  1222.7 242.5 %copy-start.28 = (bf16[512,4,128]{0,2,1:T(8,128)(2,1)S(1)}, bf16[512,4,128]{0,2,1:T(8,128)(2,1)}, u32[]{:S(2)}) copy-start(bf16[512,4,128]{0,2,1:T(8,128)(2,1)} %copy.155) | copy-start | bytes 1572868
  (78 other events, 826.3 us)
Sparse Core Ops, SparseCore 0:
  9.6 24.1 all-gather.2
  92.1 84.8 all-reduce.13
  213.8 23.7 all-gather.4
  658.8 139.9 reduce-scatter.24
  801.2 139.4 reduce-scatter.22
  943.3 44.5 reduce-scatter.20
  990.2 86.8 all-reduce.15
  1081.2 154.0 reduce-scatter.40
  1239.3 109.7 reduce-scatter.38
  1353.0 109.7 reduce-scatter.36
  1466.3 51.2 reduce-scatter.34
  1521.4 52.5 reduce-scatter.46
  1578.1 52.6 reduce-scatter.44
  1634.6 52.5 reduce-scatter.42
  1689.6 52.6 all-reduce.17
  1745.7 67.1 reduce-scatter.32
  1816.3 66.8 reduce-scatter.26
  1886.5 67.0 reduce-scatter.28
  1957.2 66.5 reduce-scatter.30
where the time goes:
time: 2040 us; the launch traced here: 2030 us
  waiting for transfers between devices  1440 us (71%)
  matrix products  237 us (12%)
  local copies, waits for them, and re-layouts  168 us (8%)
  other arithmetic  90.5 us (4%)
  blocking collectives  43.4 us (2%)
  starting transfers between devices  37.6 us (2%)
    all_to_all x2, waiting for transfers between devices, deliver(): lax.all_to_all(block_rows, 'ep', split_axis=0, concat_axis=0, tiled=True)  306 us
    unnamed x22, waiting for transfers between devices  167 us
    reduce_scatter x1, waiting for transfers between devices, per_device(): lax.psum_scatter(shared_up_grad.astype(jnp.bfloat16), 'ep', scatter_dimen...  112 us
    reduce_scatter x1, waiting for transfers between devices, per_device(): lax.psum_scatter(shared_gate_grad.astype(jnp.bfloat16), 'ep', scatter_dim...  111 us
    reduce_scatter x1, waiting for transfers between devices, per_device(): lax.psum_scatter(rows_grad.reshape(-1, model_dim), 'tp', scatter_dimensio...  94.6 us
    all_to_all x2, waiting for transfers between devices, collect(): lax.all_to_all(block_rows, 'ep', split_axis=0, concat_axis=0, tiled=True)  86.5 us
    ppermute x4, waiting for transfers between devices, passed_along(): lax.ppermute(value, axis, [(source, source + steps) for source in range(l...  79.6 us
    reduce_scatter x1, waiting for transfers between devices, per_device(): lax.psum_scatter(key_grad.astype(jnp.bfloat16), 'ep', scatter_dimension=0...  68.7 us
  transfers between devices with their start and end apart: 27, of which 26 were waited for; matrix products, arithmetic and copies ran while one was open for 19% of the time, Pallas kernels for 0%

commit v1 on v0

--- a/solution.py
+++ b/solution.py
@@ -3,6 +3,8 @@
 import jax
 import jax.numpy as jnp
 from jax import lax
+from jax.experimental import pallas as pl
+from jax.experimental.pallas import tpu as pltpu
 from jax.sharding import PartitionSpec as P
 
 HD = 128
@@ -94,7 +96,7 @@
     return lax.all_to_all(block_rows, "ep", split_axis=0, concat_axis=0, tiled=True)
 
 
-def per_device(
+def slot_plan(
     tokens,
     out_grad,
     first_gain,
@@ -444,9 +446,930 @@
     )
 
 
+MESH = pl.DeviceIdType.MESH
+Z_ORDER = (0, 3, 1, 2)
+
+
+def place():
+    ep, tp = lax.axis_index("ep"), lax.axis_index("tp")
+    return ep, tp, ep // 2, lax.rem(ep, 2), tp // 2, lax.rem(tp, 2)
+
+
+def greet(always, along_z=False):
+    barrier = pltpu.get_barrier_semaphore()
+    for device in always:
+        pl.semaphore_signal(barrier, inc=1, device_id=device, device_id_type=MESH)
+    count = len(always)
+    if along_z:
+        ep, tp, z, _, _, _ = place()
+
+        @pl.when(z < 3)
+        def _():
+            pl.semaphore_signal(barrier, inc=1, device_id=(ep + 2, tp), device_id_type=MESH)
+
+        @pl.when(z > 0)
+        def _():
+            pl.semaphore_signal(barrier, inc=1, device_id=(ep - 2, tp), device_id_type=MESH)
+
+        count = count + lax.min(z, 1) + lax.min(3 - z, 1)
+    pl.semaphore_wait(barrier, count)
+
+
+def remote(source, target, send_sem, recv_sem, device):
+    return pltpu.make_async_remote_copy(
+        src_ref=source,
+        dst_ref=target,
+        send_sem=send_sem,
+        recv_sem=recv_sem,
+        device_id=device,
+        device_id_type=MESH,
+    )
+
+
+def add_blocks(target, sources, rows):
+    step = 64
+
+    def body(i, carry):
+        span = pl.ds(pl.multiple_of(i * step, step), step)
+        total = target[span, :].astype(jnp.float32)
+        for source in sources:
+            total = total + source[span, :].astype(jnp.float32)
+        target[span, :] = total.astype(target.dtype)
+        return carry
+
+    lax.fori_loop(0, rows // step, body, 0)
+
+
+def gather_tp_kernel(x_ref, o_ref, send_sem, recv_sem, own_sem):
+    ep, tp, _, _, x, core = place()
+    cols = x_ref.shape[1]
+    sibling = (ep, tp + 1 - 2 * core)
+    across = (ep, tp + 2 - 4 * x)
+    greet([sibling, across])
+    mine = o_ref.at[:, pl.ds(pl.multiple_of(tp * cols, cols), cols)]
+    theirs = o_ref.at[:, pl.ds(pl.multiple_of((tp + 2 - 4 * x) * cols, cols), cols)]
+    out_x = remote(x_ref, mine, send_sem.at[0], recv_sem.at[0], across)
+    out_s = remote(x_ref, mine, send_sem.at[1], recv_sem.at[1], sibling)
+    own = pltpu.make_async_copy(x_ref, mine, own_sem)
+    out_x.start()
+    out_s.start()
+    own.start()
+    remote(x_ref, theirs, send_sem.at[0], recv_sem.at[0], across).wait_recv()
+    passing = remote(theirs, theirs, send_sem.at[2], recv_sem.at[2], sibling)
+    passing.start()
+    out_s.wait_recv()
+    passing.wait_recv()
+    own.wait()
+    out_x.wait_send()
+    out_s.wait_send()
+    passing.wait_send()
+
+
+def gather_tp(value, cid):
+    rows, cols = value.shape
+    return pl.pallas_call(
+        gather_tp_kernel,
+        out_shape=jax.ShapeDtypeStruct((rows, 4 * cols), value.dtype),
+        in_specs=[pl.BlockSpec(memory_space=pl.ANY)],
+        out_specs=pl.BlockSpec(memory_space=pl.ANY),
+        scratch_shapes=[
+            pltpu.SemaphoreType.DMA((3,)),
+            pltpu.SemaphoreType.DMA((3,)),
+            pltpu.SemaphoreType.DMA,
+        ],
+        compiler_params=pltpu.CompilerParams(collective_id=cid, has_side_effects=True),
+        name="gather_tp",
+    )(value)
+
+
+def scatter_tp_kernel(p_ref, o_ref, mine, from_sib, from_x, own_sem, send_sem, recv_sem):
+    ep, tp, _, _, x, core = place()
+    rows, cols = o_ref.shape
+    sibling = (ep, tp + 1 - 2 * core)
+    across = (ep, tp + 2 - 4 * x)
+    greet([sibling, across])
+
+    def part(x_at, core_at):
+        return p_ref.at[:, pl.ds(pl.multiple_of((x_at * 2 + core_at) * cols, cols), cols)]
+
+    sends, owns = [], []
+    for i, x_at in enumerate((1 - x, x)):
+        owns.append(pltpu.make_async_copy(part(x_at, core), mine.at[i], own_sem.at[i]))
+        sends.append(
+            remote(part(x_at, 1 - core), from_sib.at[i], send_sem.at[i], recv_sem.at[i], sibling)
+        )
+        sends[-1].start()
+        owns[-1].start()
+    owns[0].wait()
+    sends[0].wait_recv()
+    add_blocks(mine.at[0], [from_sib.at[0]], rows)
+    out_x = remote(mine.at[0], from_x, send_sem.at[2], recv_sem.at[2], across)
+    out_x.start()
+    owns[1].wait()
+    sends[1].wait_recv()
+    out_x.wait_recv()
+    o_ref[...] = jnp.zeros_like(o_ref)
+    add_blocks(o_ref, [mine.at[1], from_sib.at[1], from_x], rows)
+    out_x.wait_send()
+    sends[0].wait_send()
+    sends[1].wait_send()
+
+
+def scatter_tp(value, cid):
+    rows, cols = value.shape[0], value.shape[1] // 4
+    return pl.pallas_call(
+        scatter_tp_kernel,
+        out_shape=jax.ShapeDtypeStruct((rows, cols), jnp.float32),
+        in_specs=[pl.BlockSpec(memory_space=pl.ANY)],
+        out_specs=pl.BlockSpec(memory_space=pltpu.VMEM),
+        scratch_shapes=[
+            pltpu.VMEM((2, rows, cols), value.dtype),
+            pltpu.VMEM((2, rows, cols), value.dtype),
+            pltpu.VMEM((rows, cols), value.dtype),
+            pltpu.SemaphoreType.DMA((2,)),
+            pltpu.SemaphoreType.DMA((3,)),
+            pltpu.SemaphoreType.DMA((3,)),
+        ],
+        compiler_params=pltpu.CompilerParams(
+            collective_id=cid, has_side_effects=True, vmem_limit_bytes=32 * 2**20
+        ),
+        name="scatter_tp",
+    )(value)
+
+
+def lane_peers():
+    ep, tp, z, y, x, core = place()
+    to_y, to_x = 1 - 2 * y, 1 - 2 * x
+    peer_a = (ep + (1 - core) * to_y, tp + core * 2 * to_x)
+    peer_b = (ep + core * to_y, tp + (1 - core) * 2 * to_x)
+    sibling = (ep, tp + 1 - 2 * core)
+    above, below = (ep + 2, tp), (ep - 2, tp)
+    return peer_a, peer_b, sibling, above, below
+
+
+def lane_spot(z_at, da, db, core_at):
+    _, _, _, y, x, _ = place()
+    y_at = y + (1 - 2 * y) * ((1 - core_at) * da + core_at * db)
+    x_at = x + (1 - 2 * x) * (core_at * da + (1 - core_at) * db)
+    return z_at * 2 + y_at, x_at * 2 + core_at
+
+
+def gather_all_kernel(x_ref, o_ref, up_sem, down_sem, a_sem, b_sem, s_sem, recv_sem, sib_sem, own_sem):
+    ep, tp, z, y, x, core = place()
+    rows, cols = x_ref.shape
+    peer_a, peer_b, sibling, above, below = lane_peers()
+    greet([peer_a, peer_b, sibling], True)
+
+    def spot(z_at, da, db):
+        group, quarter = lane_spot(z_at, da, db, core)
+        return o_ref.at[
+            pl.ds(pl.multiple_of(group * rows, rows), rows),
+            pl.ds(pl.multiple_of(quarter * cols, cols), cols),
+        ]
+
+    def at(z_at, da, db):
+        return z_at * 4 + da * 2 + db
+
+    def arrived(z_at, da, db):
+        block = spot(z_at, da, db)
+        remote(block, block, s_sem.at[at(z_at, da, db)], recv_sem.at[at(z_at, da, db)], sibling).wait_recv()
+
+    def up(z_at, source):
+        return remote(source, spot(z_at, 0, 0), up_sem.at[z_at], recv_sem.at[at(z_at, 0, 0)], above)
+
+    def down(z_at, source):
+        return remote(source, spot(z_at, 0, 0), down_sem.at[z_at], recv_sem.at[at(z_at, 0, 0)], below)
+
+    def over_a(z_at, source):
+        return remote(source, spot(z_at, 0, 0), a_sem.at[z_at], recv_sem.at[at(z_at, 1, 0)], peer_a)
+
+    def over_b(z_at, da, source):
+        return remote(
+            source, spot(z_at, da, 0), b_sem.at[z_at * 2 + da], recv_sem.at[at(z_at, da, 1)], peer_b
+        )
+
+    def to_sibling(z_at, da, db, source):
+        n = at(z_at, da, db)
+        return remote(source, spot(z_at, da, db), s_sem.at[n], sib_sem.at[n], sibling)
+
+    own = pltpu.make_async_copy(x_ref, spot(z, 0, 0), own_sem)
+    over_b(z, 0, x_ref).start()
+    over_a(z, x_ref).start()
+
+    @pl.when(z < 3)
+    def _():
+        up(z, x_ref).start()
+
+    @pl.when(z > 0)
+    def _():
+        down(z, x_ref).start()
+
+    to_sibling(z, 0, 0, x_ref).start()
+    own.start()
+
+    def from_a(z_at):
+        arrived(z_at, 1, 0)
+        block = spot(z_at, 1, 0)
+        over_b(z_at, 1, block).start()
+        to_sibling(z_at, 1, 0, block).start()
+
+    def from_z(z_at, onward):
+        arrived(z_at, 0, 0)
+        block = spot(z_at, 0, 0)
+        onward(block)
+        over_a(z_at, block).start()
+        over_b(z_at, 0, block).start()
+        to_sibling(z_at, 0, 0, block).start()
+
+    def from_below(z_at):
+        def onward(block):
+            @pl.when(z < 3)
+            def _():
+                up(z_at, block).start()
+
+        from_z(z_at, onward)
+
+    def from_above(z_at):
+        def onward(block):
+            @pl.when(z > 0)
+            def _():
+                down(z_at, block).start()
+
+        from_z(z_at, onward)
+
+    for d in range(1, 4):
+
+        @pl.when(z >= d)
+        def _(d=d):
+            from_below(z - d)
+
+        @pl.when(z + d <= 3)
+        def _(d=d):
+            from_above(z + d)
+
+        if d == 1:
+            from_a(z)
+        else:
+
+            @pl.when(z >= d - 1)
+            def _(d=d):
+                from_a(z - d + 1)
+
+            @pl.when(z + d - 1 <= 3)
+            def _(d=d):
+                from_a(z + d - 1)
+
+    @pl.when(z >= 3)
+    def _():
+        from_a(z - 3)
+
+    @pl.when(z + 3 <= 3)
+    def _():
+        from_a(z + 3)
+
+    def from_b(z_at, da):
+        arrived(z_at, da, 1)
+        to_sibling(z_at, da, 1, spot(z_at, da, 1)).start()
+
+    for da in range(2):
+        from_b(z, da)
+    for d in range(1, 4):
+        for da in range(2):
+
+            @pl.when(z >= d)
+            def _(d=d, da=da):
+                from_b(z - d, da)
+
+            @pl.when(z + d <= 3)
+            def _(d=d, da=da):
+                from_b(z + d, da)
+
+    def finish_sibling(i, carry):
+        block = spot(0, 0, 0)
+        copy = remote(block, block, s_sem.at[i], sib_sem.at[i], sibling)
+        copy.wait_recv()
+        copy.wait_send()
+        return carry
+
+    lax.fori_loop(0, 16, finish_sibling, 0)
+
+    def finish_links(i, carry):
+        over_a(i, x_ref).wait_send()
+        over_b(i, 0, x_ref).wait_send()
+        over_b(i, 1, x_ref).wait_send()
+
+        @pl.when((z < 3) & (i <= z))
+        def _():
+            up(i, x_ref).wait_send()
+
+        @pl.when((z > 0) & (i >= z))
+        def _():
+            down(i, x_ref).wait_send()
+
+        return carry
+
+    lax.fori_loop(0, 4, finish_links, 0)
+    own.wait()
+
+
+def gather_all(value, cid):
+    rows, cols = value.shape
+    return pl.pallas_call(
+        gather_all_kernel,
+        out_shape=jax.ShapeDtypeStruct((8 * rows, 4 * cols), value.dtype),
+        in_specs=[pl.BlockSpec(memory_space=pl.ANY)],
+        out_specs=pl.BlockSpec(memory_space=pl.ANY),
+        scratch_shapes=[
+            pltpu.SemaphoreType.DMA((4,)),
+            pltpu.SemaphoreType.DMA((4,)),
+            pltpu.SemaphoreType.DMA((4,)),
+            pltpu.SemaphoreType.DMA((8,)),
+            pltpu.SemaphoreType.DMA((16,)),
+            pltpu.SemaphoreType.DMA((16,)),
+            pltpu.SemaphoreType.DMA((16,)),
+            pltpu.SemaphoreType.DMA,
+        ],
+        compiler_params=pltpu.CompilerParams(collective_id=cid, has_side_effects=True),
+        name="gather_all",
+    )(value)
+
+
+def z_chain(blocks, totals, from_below, from_above, up_send, up_recv, down_send, down_recv, rows, final):
+    ep, tp, z, _, _, _ = place()
+    above, below = (ep + 2, tp), (ep - 2, tp)
+
+    def up(z_at):
+        return remote(totals(z_at), from_below.at[z_at], up_send.at[z_at], up_recv.at[z_at], above)
+
+    def down(z_at):
+        return remote(totals(z_at), from_above.at[z_at], down_send.at[z_at], down_recv.at[z_at], below)
+
+    for z_at in Z_ORDER:
+        blocks(z_at)
+
+        @pl.when(z_at > z)
+        def _(z_at=z_at):
+            @pl.when(z > 0)
+            def _():
+                up(z_at).wait_recv()
+                add_blocks(totals(z_at), [from_below.at[z_at]], rows)
+
+            up(z_at).start()
+
+        @pl.when(z_at < z)
+        def _(z_at=z_at):
+            @pl.when(z < 3)
+            def _():
+                down(z_at).wait_recv()
+                add_blocks(totals(z_at), [from_above.at[z_at]], rows)
+
+            down(z_at).start()
+
+    for z_at in range(4):
+
+        @pl.when(z_at == z)
+        def _(z_at=z_at):
+            @pl.when(z > 0)
+            def _():
+                up(z_at).wait_recv()
+
+            @pl.when(z < 3)
+            def _():
+                down(z_at).wait_recv()
+
+            @pl.when(z == 0)
+            def _():
+                final(z_at, [from_above.at[z_at]])
+
+            @pl.when(z == 3)
+            def _():
+                final(z_at, [from_below.at[z_at]])
+
+            @pl.when((z > 0) & (z < 3))
+            def _():
+                final(z_at, [from_below.at[z_at], from_above.at[z_at]])
+
+    for z_at in range(4):
+
+        @pl.when(z_at > z)
+        def _(z_at=z_at):
+            up(z_at).wait_send()
+
+        @pl.when(z_at < z)
+        def _(z_at=z_at):
+            down(z_at).wait_send()
+
+
+def scatter_all_kernel(
+    p_ref,
+    o_ref,
+    mine,
+    from_sib,
+    from_b,
+    from_a,
+    from_below,
+    from_above,
+    own_sem,
+    s_send,
+    s_recv,
+    b_send,
+    b_recv,
+    a_send,
+    a_recv,
+    up_send,
+    up_recv,
+    down_send,
+    down_recv,
+):
+    ep, tp, z, y, x, core = place()
+    rows, cols = o_ref.shape
+    peer_a, peer_b, sibling, above, below = lane_peers()
+    greet([peer_a, peer_b, sibling], True)
+
+    def part(z_at, da, db, core_at):
+        group, quarter = lane_spot(z_at, da, db, core_at)
+        return p_ref.at[
+            pl.ds(pl.multiple_of(group * rows, rows), rows),
+            pl.ds(pl.multiple_of(quarter * cols, cols), cols),
+        ]
+
+    def at(z_at, da, db):
+        return z_at * 4 + da * 2 + db
+
+    def own(z_at, da, db):
+        n = at(z_at, da, db)
+        return pltpu.make_async_copy(part(z_at, da, db, core), mine.at[n], own_sem.at[n])
+
+    def to_sibling(z_at, da, db):
+        n = at(z_at, da, db)
+        return remote(
+            part(z_at, da, db, 1 - core), from_sib.at[n], s_send.at[n], s_recv.at[n], sibling
+        )
+
+    for da, db in ((1, 1), (0, 1), (1, 0), (0, 0)):
+        for z_at in Z_ORDER:
+            to_sibling(z_at, da, db).start()
+            own(z_at, da, db).start()
+
+    def here(z_at, da, db):
+        own(z_at, da, db).wait()
+        to_sibling(z_at, da, db).wait_recv()
+        return mine.at[at(z_at, da, db)], from_sib.at[at(z_at, da, db)]
+
+    def over_b(z_at, da):
+        n = z_at * 2 + da
+        return remote(mine.at[at(z_at, da, 1)], from_b.at[n], b_send.at[n], b_recv.at[n], peer_b)
+
+    def over_a(z_at):
+        return remote(mine.at[at(z_at, 1, 0)], from_a.at[z_at], a_send.at[z_at], a_recv.at[z_at], peer_a)
+
+    for da in (1, 0):
+        for z_at in Z_ORDER:
+            own_part, sib_part = here(z_at, da, 1)
+            add_blocks(own_part, [sib_part], rows)
+            over_b(z_at, da).start()
+    for z_at in Z_ORDER:
+        own_part, sib_part = here(z_at, 1, 0)
+        over_b(z_at, 1).wait_recv()
+        add_blocks(own_part, [sib_part, from_b.at[z_at * 2 + 1]], rows)
+        over_a(z_at).start()
+
+    def blocks(z_at):
+        own_part, sib_part = here(z_at, 0, 0)
+        over_b(z_at, 0).wait_recv()
+        over_a(z_at).wait_recv()
+        add_blocks(own_part, [sib_part, from_b.at[z_at * 2], from_a.at[z_at]], rows)
+
+    def final(z_at, others):
+        o_ref[...] = jnp.zeros_like(o_ref)
+        add_blocks(o_ref, [mine.at[at(z_at, 0, 0)], *others], rows)
+
+    z_chain(
+        blocks,
+        lambda z_at: mine.at[at(z_at, 0, 0)],
+        from_below,
+        from_above,
+        up_send,
+        up_recv,
+        down_send,
+        down_recv,
+        rows,
+        final,
+    )
+    for z_at in range(4):
+        over_a(z_at).wait_send()
+        for da in range(2):
+            over_b(z_at, da).wait_send()
+            for db in range(2):
+                to_sibling(z_at, da, db).wait_send()
+
+
+def scatter_all(value, cid):
+    rows, cols = value.shape[0] // 8, value.shape[1] // 4
+    dma = pltpu.SemaphoreType.DMA
+
+    def held(count):
+        return pltpu.VMEM((count, rows, cols), value.dtype)
+
+    return pl.pallas_call(
+        scatter_all_kernel,
+        out_shape=jax.ShapeDtypeStruct((rows, cols), jnp.float32),
+        in_specs=[pl.BlockSpec(memory_space=pl.ANY)],
+        out_specs=pl.BlockSpec(memory_space=pltpu.VMEM),
+        scratch_shapes=[held(16), held(16), held(8), held(4), held(4), held(4)]
+        + [dma((16,)), dma((16,)), dma((16,)), dma((8,)), dma((8,))]
+        + [dma((4,))] * 6,
+        compiler_params=pltpu.CompilerParams(
+            collective_id=cid, has_side_effects=True, vmem_limit_bytes=48 * 2**20
+        ),
+        name="scatter_all",
+    )(value)
+
+
+def scatter_ep_kernel(
+    p_ref, o_ref, mine, from_y, from_below, from_above, own_sem, y_send, y_recv, up_send, up_recv, down_send, down_recv
+):
+    ep, tp, z, y, _, _ = place()
+    rows, cols = o_ref.shape
+    across = (ep + 1 - 2 * y, tp)
+    above, below = (ep + 2, tp), (ep - 2, tp)
+    greet([across], True)
+
+    def part(z_at, y_at):
+        return p_ref.at[pl.ds(pl.multiple_of((z_at * 2 + y_at) * rows, rows), rows), :]
+
+    def own(z_at):
+        return pltpu.make_async_copy(part(z_at, y), mine.at[z_at], own_sem.at[z_at])
+
+    def over_y(z_at):
+        return remote(part(z_at, 1 - y), from_y.at[z_at], y_send.at[z_at], y_recv.at[z_at], across)
+
+    for z_at in Z_ORDER:
+        over_y(z_at).start()
+        own(z_at).start()
+
+    def blocks(z_at):
+        own(z_at).wait()
+        over_y(z_at).wait_recv()
+        add_blocks(mine.at[z_at], [from_y.at[z_at]], rows)
+
+    def final(z_at, others):
+        o_ref[...] = jnp.zeros_like(o_ref)
+        add_blocks(o_ref, [mine.at[z_at], *others], rows)
+
+    z_chain(
+        blocks,
+        lambda z_at: mine.at[z_at],
+        from_below,
+        from_above,
+        up_send,
+        up_recv,
+        down_send,
+        down_recv,
+        rows,
+        final,
+    )
+    for z_at in range(4):
+        over_y(z_at).wait_send()
+
+
+def scatter_ep(value, cid):
+    rows, cols = value.shape[0] // 8, value.shape[1]
+    dma = pltpu.SemaphoreType.DMA
+
+    def held():
+        return pltpu.VMEM((4, rows, cols), value.dtype)
+
+    return pl.pallas_call(
+        scatter_ep_kernel,
+        out_shape=jax.ShapeDtypeStruct((rows, cols), jnp.float32),
+        in_specs=[pl.BlockSpec(memory_space=pl.ANY)],
+        out_specs=pl.BlockSpec(memory_space=pltpu.VMEM),
+        scratch_shapes=[held(), held(), held(), held()] + [dma((4,))] * 7,
+        compiler_params=pltpu.CompilerParams(
+            collective_id=cid, has_side_effects=True, vmem_limit_bytes=40 * 2**20
+        ),
+        name="scatter_ep",
+    )(value)
+
+
+def tp_total(value):
+    return lax.psum(value, "tp")
+
+
+def kept_choice(expert_ids, pair_order, expert_total, capacity):
+    tok_count, top_count = expert_ids.shape
+    pair_count = tok_count * top_count
+    order = pair_order.reshape(-1)
+    pairs = jnp.arange(pair_count, dtype=jnp.int32)
+    turn = jnp.sum(jnp.where(order[None, :] == pairs[:, None], pairs[None, :], 0), axis=1)
+    turn = turn.reshape(tok_count, top_count)
+    picked = expert_ids[:, :, None] == jnp.arange(expert_total, dtype=jnp.int32)[None, None, :]
+    turn_of = jnp.sum(jnp.where(picked, turn[:, :, None], 0), axis=1)
+    named = jnp.any(picked, axis=1)
+    turn_of = jnp.where(named, turn_of, pair_count)
+    slot = jnp.sum((turn_of[None, :, :] < turn_of[:, None, :]).astype(jnp.int32), axis=1)
+    return (named & (slot < capacity)).astype(jnp.float32)
+
+
+def dense_plan(
+    tokens,
+    out_grad,
+    first_gain,
+    query_weight,
+    key_weight,
+    value_weight,
+    query_bias,
+    key_bias,
+    value_bias,
+    output_weight,
+    second_gain,
+    router_weight,
+    shared_gate_weight,
+    shared_up_weight,
+    shared_down_weight,
+    switch_vector,
+    expert_gate_weight,
+    expert_up_weight,
+    expert_down_weight,
+    expert_ids,
+    pair_order,
+):
+    ep, tp = lax.axis_index("ep"), lax.axis_index("tp")
+    tok_count, col_width = tokens.shape
+    model_dim = query_weight.shape[0]
+    sources = lax.axis_size("ep")
+    place_in_seq = ep % SPAN
+    has_earlier = place_in_seq > 0
+    expert_total = router_weight.shape[1]
+    capacity = 9 * tok_count * expert_ids.shape[1] // (8 * expert_total)
+    head_count = query_weight.shape[1] // HD
+    score_scale = HD ** (-0.5)
+    expert_width = expert_gate_weight.shape[2]
+    shared_width = shared_gate_weight.shape[1] // sources
+    width = expert_width + shared_width
+
+    def own_cols(vector):
+        return lax.dynamic_slice_in_dim(vector, tp * col_width, col_width, vector.ndim - 1)
+
+    grads_all = lax.all_gather(
+        lax.all_gather(out_grad, "ep", axis=0, tiled=True), "tp", axis=1, tiled=True
+    )
+    kept_own = kept_choice(expert_ids, pair_order, expert_total, capacity)
+    kept_all = lax.all_gather(kept_own, "ep", axis=0, tiled=True)
+
+    inputs_full = gather_tp(tokens, 0).astype(jnp.float32)
+    unit_one, inv_one = row_stats(inputs_full)
+    normed_one = (unit_one * first_gain).astype(jnp.bfloat16)
+    query_lin = jnp.dot(normed_one, query_weight, preferred_element_type=jnp.float32) + query_bias
+    key_lin = jnp.dot(normed_one, key_weight, preferred_element_type=jnp.float32) + key_bias
+    value_lin = jnp.dot(normed_one, value_weight, preferred_element_type=jnp.float32) + value_bias
+    cosine, sine_part = rope_tables(tok_count, HD, place_in_seq * tok_count)
+    queries = rotate(query_lin.reshape(tok_count, head_count, HD), cosine, sine_part).astype(
+        jnp.bfloat16
+    )
+    keys_rot = rotate(key_lin.reshape(tok_count, head_count, HD), cosine, sine_part).astype(
+        jnp.bfloat16
+    )
+    values_all = value_lin.reshape(tok_count, head_count, HD).astype(jnp.bfloat16)
+    earlier_keys, earlier_values = passed_along((keys_rot, values_all), "ep", 1)
+    keys_both = jnp.concatenate([earlier_keys, keys_rot], axis=0)
+    values_both = jnp.concatenate([earlier_values, values_all], axis=0)
+    blocks = jnp.arange(tok_count) // BLOCK
+    local_allowed = blocks[None, :] <= blocks[:, None]
+    remote_allowed = jnp.broadcast_to(has_earlier, (tok_count, tok_count))
+    allowed = jnp.concatenate([remote_allowed, local_allowed], axis=1)[None]
+
+    def attention_scores():
+        scored = (
+            jnp.einsum("qhd,khd->hqk", queries, keys_both, preferred_element_type=jnp.float32)
+            * score_scale
+        )
+        return jnp.where(allowed, scored, masked_score)
+
+    scores = attention_scores()
+    row_max = jnp.max(scores, axis=-1, keepdims=True)
+    powers = jnp.exp(scores - row_max)
+    totals = jnp.sum(powers, axis=-1, keepdims=True)
+    log_total = row_max + jnp.log(totals)
+    probs_low = (powers / totals).astype(jnp.bfloat16)
+    context = jnp.einsum("hqk,khd->qhd", probs_low, values_both, preferred_element_type=jnp.float32)
+    context = context.reshape(tok_count, head_count * HD).astype(jnp.bfloat16)
+    attn_part = jnp.dot(context, output_weight, preferred_element_type=jnp.float32)
+    attended = scatter_tp(attn_part.astype(jnp.bfloat16), 1)
+
+    hidden_cols = tokens.astype(jnp.float32) + attended
+    squares = tp_total(jnp.sum(hidden_cols * hidden_cols, axis=-1, keepdims=True))
+    inv_two = lax.rsqrt(squares / model_dim + norm_eps)
+    unit_two = hidden_cols * inv_two
+    second_cols = own_cols(second_gain)
+    normed_cols = (unit_two * second_cols).astype(jnp.bfloat16)
+    normed_all = gather_all(normed_cols, 2)
+
+    def hidden_rows(expert_part, shared_part):
+        cut = lax.dynamic_slice_in_dim(shared_part, ep * shared_width, shared_width, 1)
+        return jnp.concatenate([expert_part[0].T, cut.T], axis=0)
+
+    gate_rows = hidden_rows(expert_gate_weight, shared_gate_weight)
+    up_rows = hidden_rows(expert_up_weight, shared_up_weight)
+    down_rows = jnp.concatenate(
+        [
+            expert_down_weight[0],
+            lax.dynamic_slice_in_dim(shared_down_weight, ep * shared_width, shared_width, 0),
+        ],
+        axis=0,
+    )
+    both_rows = jnp.concatenate([gate_rows, up_rows], axis=0)
+    rows_in = jnp.concatenate([both_rows, router_weight.T, switch_vector[None, :]], axis=0)
+    lin_all = times_transpose(normed_all, rows_in)
+    gate_lin = lin_all[:, :width]
+    up_lin = lin_all[:, width : 2 * width]
+    logits = lin_all[:, 2 * width : 2 * width + expert_total]
+    router_probs = softmax_rows(logits)
+    gates_all = jnp.sum(
+        jnp.where(jnp.arange(expert_total)[None, :] == ep, router_probs * kept_all, 0.0),
+        axis=1,
+        keepdims=True,
+    )
+    switch_all = jax.nn.sigmoid(lin_all[:, 2 * width + expert_total :])
+    is_expert = jnp.arange(width)[None, :] < expert_width
+    scale = jnp.where(is_expert, gates_all, switch_all)
+    hidden_grad = times_transpose(grads_all, down_rows)
+    gate_sig = jax.nn.sigmoid(gate_lin)
+    gate_act = gate_lin * gate_sig
+    hidden = gate_act * up_lin
+    agreement = hidden * hidden_grad
+    gate_part = jnp.sum(jnp.where(is_expert, agreement, 0.0), axis=1)
+    switch_part = jnp.sum(jnp.where(is_expert, 0.0, agreement), axis=1)
+    scaled_hidden = (hidden * scale).astype(jnp.bfloat16)
+    scaled_grad = hidden_grad * scale
+    gate_lin_grad = (scaled_grad * up_lin * gate_sig * (1.0 + gate_lin * (1.0 - gate_sig))).astype(
+        jnp.bfloat16
+    )
+    up_lin_grad = (scaled_grad * gate_act).astype(jnp.bfloat16)
+    both_grad = jnp.concatenate([gate_lin_grad, up_lin_grad], axis=1)
+    normed_grad_part = jnp.dot(both_grad, both_rows, preferred_element_type=jnp.float32)
+    normed_grad = scatter_all(normed_grad_part.astype(jnp.bfloat16), 3)
+    out_part = jnp.dot(scaled_hidden, down_rows, preferred_element_type=jnp.float32)
+    ffn_cols = scatter_all(out_part.astype(jnp.bfloat16), 3)
+    layer_out = (hidden_cols + ffn_cols).astype(jnp.bfloat16)
+    down_grad = inner_rows(scaled_hidden, grads_all)
+    both_rows_grad = inner_rows(both_grad, normed_all)
+    expert_down_grad = down_grad[None, :expert_width]
+    expert_gate_grad = both_rows_grad[:expert_width].T[None]
+    expert_up_grad = both_rows_grad[width : width + expert_width].T[None]
+    shared_parts = jnp.stack(
+        [
+            both_rows_grad[expert_width:width],
+            both_rows_grad[width + expert_width :],
+            down_grad[expert_width:],
+        ]
+    ).astype(jnp.bfloat16)
+    shared_parts = shared_parts.reshape(3, shared_width, sources, -1).transpose(2, 0, 1, 3)
+    shared_parts = lax.all_to_all(shared_parts, "ep", split_axis=0, concat_axis=0, tiled=True)
+    shared_parts = shared_parts.transpose(1, 0, 2, 3).reshape(3, sources * shared_width, -1)
+    shared_parts = shared_parts.astype(jnp.float32)
+    shared_gate_grad = shared_parts[0].T
+    shared_up_grad = shared_parts[1].T
+    shared_down_grad = shared_parts[2]
+
+    scalar_parts = jnp.stack([gate_part, switch_part]).reshape(2, sources, tok_count).swapaxes(0, 1)
+    scalar_parts = lax.all_to_all(scalar_parts, "ep", split_axis=0, concat_axis=0, tiled=True)
+    scalar_sums = tp_total(
+        jnp.concatenate([scalar_parts[:, 0], jnp.sum(scalar_parts[:, 1], axis=0)[None]], axis=0)
+    )
+    probs_grad = scalar_sums[:sources].T * kept_own
+    switch_grad = scalar_sums[sources]
+    own_rows = lax.dynamic_slice_in_dim(lin_all, ep * tok_count, tok_count, 0)
+    probs_own = softmax_rows(own_rows[:, 2 * width : 2 * width + expert_total])
+    switch = jax.nn.sigmoid(own_rows[:, 2 * width + expert_total])
+    logit_grad = (
+        probs_own * (probs_grad - jnp.sum(probs_own * probs_grad, axis=-1, keepdims=True))
+    ).astype(jnp.bfloat16)
+    router_grad = inner_rows(normed_cols, logit_grad)
+    switch_lin_grad = switch_grad * switch * (1.0 - switch)
+    switch_vector_grad = jnp.dot(switch_lin_grad, normed_cols, preferred_element_type=jnp.float32)
+    router_cols = lax.dynamic_slice_in_dim(router_weight, tp * col_width, col_width, 0)
+    normed_grad = normed_grad + times_transpose(logit_grad, router_cols)
+    normed_grad = (
+        normed_grad
+        + switch_lin_grad[:, None] * own_cols(switch_vector).astype(jnp.float32)[None, :]
+    )
+    second_gain_grad = jnp.sum(normed_grad * unit_two, axis=0)
+    scaled_two = normed_grad * second_cols
+    mean_two = tp_total(jnp.sum(scaled_two * unit_two, axis=-1, keepdims=True)) / model_dim
+    hidden_grad_cols = out_grad.astype(jnp.float32) + inv_two * (scaled_two - unit_two * mean_two)
+
+    attended_grad = gather_tp(hidden_grad_cols.astype(jnp.bfloat16), 0)
+    output_grad = inner_rows(attended_grad, context)
+    output_grad = lax.psum_scatter(
+        output_grad.astype(jnp.bfloat16), "ep", scatter_dimension=0, tiled=True
+    )
+    output_grad = output_grad.astype(jnp.float32).T
+    context_grad = (
+        times_transpose(attended_grad, output_weight)
+        .astype(jnp.bfloat16)
+        .reshape(tok_count, head_count, HD)
+    )
+    scores = attention_scores()
+    attn_probs = jnp.exp(scores - log_total)
+    probs_again = attn_probs.astype(jnp.bfloat16)
+    probs_grad_att = jnp.einsum(
+        "qhd,khd->hqk", context_grad, values_both, preferred_element_type=jnp.float32
+    )
+    values_both_grad = jnp.einsum(
+        "hqk,qhd->khd", probs_again, context_grad, preferred_element_type=jnp.float32
+    )
+    scores_grad = (
+        attn_probs * (probs_grad_att - jnp.sum(attn_probs * probs_grad_att, axis=-1, keepdims=True))
+    ).astype(jnp.bfloat16)
+    queries_grad = (
+        jnp.einsum("hqk,khd->qhd", scores_grad, keys_both, preferred_element_type=jnp.float32)
+        * score_scale
+    )
+    keys_both_grad = (
+        jnp.einsum("hqk,qhd->khd", scores_grad, queries, preferred_element_type=jnp.float32)
+        * score_scale
+    )
+    later_keys_grad, later_values_grad = passed_along(
+        (
+            keys_both_grad[:tok_count].astype(jnp.bfloat16),
+            values_both_grad[:tok_count].astype(jnp.bfloat16),
+        ),
+        "ep",
+        -1,
+    )
+    keep_later = jnp.where(has_earlier, 0.0, 1.0).astype(jnp.float32)
+    keys_grad = keys_both_grad[tok_count:] + keep_later * later_keys_grad
+    values_grad = values_both_grad[tok_count:] + keep_later * later_values_grad
+    value_lin_grad = values_grad.reshape(tok_count, head_count * HD).astype(jnp.bfloat16)
+    query_lin_grad = (
+        rotate(queries_grad, cosine, -sine_part)
+        .reshape(tok_count, head_count * HD)
+        .astype(jnp.bfloat16)
+    )
+    key_lin_grad = (
+        rotate(keys_grad, cosine, -sine_part)
+        .reshape(tok_count, head_count * HD)
+        .astype(jnp.bfloat16)
+    )
+    lin_grads = jnp.concatenate([query_lin_grad, key_lin_grad, value_lin_grad], axis=1)
+    weight_grads = scatter_ep(inner_rows(normed_one, lin_grads).astype(jnp.bfloat16), 5)
+    lin_width = head_count * HD
+    normed_one_grad = times_transpose(query_lin_grad, query_weight) + times_transpose(
+        key_lin_grad, key_weight
+    )
+    normed_one_grad = normed_one_grad + times_transpose(value_lin_grad, value_weight)
+    normed_one_cols = scatter_tp(normed_one_grad.astype(jnp.bfloat16), 1)
+    unit_cols = tokens.astype(jnp.float32) * inv_one
+    first_cols = own_cols(first_gain)
+    first_gain_grad = jnp.sum(normed_one_cols * unit_cols, axis=0)
+    scaled_one = normed_one_cols * first_cols
+    mean_one = tp_total(jnp.sum(scaled_one * unit_cols, axis=-1, keepdims=True)) / model_dim
+    tokens_grad = (hidden_grad_cols + inv_one * (scaled_one - unit_cols * mean_one)).astype(
+        jnp.bfloat16
+    )
+    bias_grad = jnp.sum(lin_grads.astype(jnp.float32), axis=0)
+
+    by_cols = jnp.concatenate(
+        [first_gain_grad[None], second_gain_grad[None], switch_vector_grad[None], router_grad.T],
+        axis=0,
+    )
+    small = lax.psum(jnp.concatenate([by_cols, bias_grad.reshape(3, -1)], axis=0), "ep")
+    spread = lax.all_gather(small[: 3 + expert_total], "tp", axis=1, tiled=True)
+    share = model_dim // sources
+    spread = lax.dynamic_slice_in_dim(spread, ep * share, share, 1)
+    bias_width = HD // sources
+    bias_sums = lax.dynamic_slice_in_dim(
+        small[3 + expert_total :].reshape(3, head_count, HD), ep * bias_width, bias_width, 2
+    )
+    return (
+        layer_out,
+        tokens_grad,
+        spread[0],
+        weight_grads[:, :lin_width],
+        weight_grads[:, lin_width : 2 * lin_width],
+        weight_grads[:, 2 * lin_width :],
+        bias_sums[0],
+        bias_sums[1],
+        bias_sums[2],
+        output_grad,
+        spread[1],
+        spread[3:].T,
+        shared_gate_grad,
+        shared_up_grad,
+        shared_down_grad,
+        spread[2],
+        expert_gate_grad,
+        expert_up_grad,
+        expert_down_grad,
+    )
+
+
 def solution(mesh):
+    plan = dense_plan if dict(mesh.shape) == {"ep": 8, "tp": 4} else slot_plan
     return jax.shard_map(
-        per_device,
+        plan,
         mesh=mesh,
         in_specs=(
             P("ep", "tp"),

time: 2040 us -> 998 us (0.49)
  waiting for transfers between devices: 1440 us -> 79.4 us
  Pallas kernels: 0 us -> 472 us
  local copies, waits for them, and re-layouts: 168 us -> 64 us
  matrix products: 237 us -> 187 us
  blocking collectives: 43.4 us -> 86.7 us
  other arithmetic: 90.5 us -> 59.9 us
    reduce_scatter x11 -> x1, waiting for transfers between devices: 616 us -> 0.01 us  [dense_plan(): lax.psum_scatter(output_grad.astype(jnp.bfloat16), 'ep', scatter_dimensio...]
    pallas_call x0 -> x8, Pallas kernels: none -> 472 us  [the longest x2 249 us: scatter_all(): pl.pallas_call(scatter_all_kernel, out_shape=jax.ShapeDtypeStruct((rows,...]
    all_to_all x4 -> x2, waiting for transfers between devices: 392 us -> 3.55 us  [the longest x1 3.54 us: dense_plan(): lax.all_to_all(scalar_parts, 'ep', split_axis=0, concat_axis=0, tiled=True)]
    unnamed x22 -> x3, waiting for transfers between devices: 167 us -> 0.71 us
    psum x3 -> x0, waiting for transfers between devices: 135 us -> none  [the longest x1 53.7 us: per_device(): lax.psum(normed_one_grad.astype(jnp.bfloat16), 'tp').astype(jnp.float32)]
    gather x10 -> x0, local copies, waits for them, and re-layouts: 88 us -> none  [the longest x1 20.2 us: per_device(): padded_grad[slot_token].astype(jnp.float32)]
    ppermute x4, waiting for transfers between devices: 79.6 us -> 0.01 us  [passed_along(): lax.ppermute(value, axis, [(source, source + steps) for source in range(l...]
    dot_general x24 -> x12, matrix products: 146 us -> 79 us  [the longest x1 26.7 us: dense_plan(): jnp.dot(both_grad, both_rows, preferred_element_type=jnp.float32)]
  transfers between devices with their start and end apart: 27 -> 9, of which waited for: 26 -> 2; matrix products, arithmetic and copies ran while one was open for 19% -> 16% of each run, Pallas kernels for 0% -> 34%
where the time goes in v1:
time: 998 us; the launch traced here: 987 us
  Pallas kernels  472 us (47%)
  matrix products  187 us (19%)
  blocking collectives  86.7 us (9%)
  waiting for transfers between devices  79.4 us (8%)
  local copies, waits for them, and re-layouts  64 us (6%)
  other arithmetic  59.9 us (6%)
  starting transfers between devices  23.2 us (2%)
  between operations  15.4 us (2%)
    pallas_call x2, Pallas kernels, scatter_all(): pl.pallas_call(scatter_all_kernel, out_shape=jax.ShapeDtypeStruct((rows,...  249 us
    pallas_call x1, Pallas kernels, scatter_ep(): pl.pallas_call(scatter_ep_kernel, out_shape=jax.ShapeDtypeStruct((rows, c...  77 us
    pallas_call x1, Pallas kernels, gather_all(): pl.pallas_call(gather_all_kernel, out_shape=jax.ShapeDtypeStruct((8 * row...  75.3 us
    all_gather x1, waiting for transfers between devices, dense_plan(): lax.all_gather(out_grad, 'ep', axis=0, tiled=True)  75.1 us
    dot_general x7, matrix products, times_transpose(): lax.dot_general(left_side, right_side, (((1,), (1,)), ((), ())), preferre...  56.1 us
    dot_general x5, matrix products, inner_rows(): lax.dot_general(left_side, right_side, (((0,), (0,)), ((), ())), preferre...  48.7 us
    pallas_call x2, Pallas kernels, gather_tp(): pl.pallas_call(gather_tp_kernel, out_shape=jax.ShapeDtypeStruct((rows, 4...  36.6 us
    psum x4, blocking collectives, tp_total(): return lax.psum(value, 'tp')  35.5 us
  transfers between devices with their start and end apart: 9, of which 2 were waited for; matrix products, arithmetic and copies ran while one was open for 16% of the time, Pallas kernels for 34%

profile of v1, /device:TPU:9, one launch (start us, length us, event | category | flops | bytes accessed | tf_op | source)
XLA Modules:
  0.0 987.3 jit_solution(11642639834671694741)
XLA Ops:
  8.0 75.1 %all-gather.3.cloned.1.call-done = bf16[4096,512]{1,0:T(8,128)(2,1)} async-done(((bf16[512,512]{1,0:T(8,128)(2,1)}), bf16[4096,512]{1,0:T(8,128)(2,1)}) %all-gather.3.cloned.1.call-update) | async-done | bytes 4194320 | tf_op jit(solution)/shard_map/all_gather | solution.py:1116
  83.1 18.8 %gather_tp.2 = bf16[512,2048]{1,0:T(8,128)(2,1)} custom-call(bf16[512,512]{1,0:T(8,128)(2,1)} %x_ref.1), custom_call_target="tpu_custom_call" | custom-call | tf_op jit(solution)/shard_map/gather_tp/pallas_call | solution.py:530
  104.2 4.5 fusion.29
  145.3 9.4 convert_reduce_fusion
  181.6 18.4 %scatter_tp.2 = f32[512,512]{1,0:T(8,128)S(1)} custom-call(bf16[512,2048]{1,0:T(8,128)(2,1)S(1)} %convolution_convert_fusion.4.p_ref), custom_call_target="tpu_custom_call" | custom-call | tf_op jit(solution)/shard_map/scatter_tp/pallas_call | solution.py:580
  200.3 5.4 psum.35
  206.6 75.3 %gather_all.1 = bf16[4096,2048]{1,0:T(8,128)(2,1)} custom-call(bf16[512,512]{1,0:T(8,128)(2,1)} %multiply_convert_fusion.3.x_ref), custom_call_target="tpu_custom_call" | custom-call | tf_op jit(solution)/shard_map/gather_all/pallas_call | solution.py:777
  281.9 22.7 %fusion.81 = f32[4096,1065]{0,1:T(8,128)S(1)} fusion(bf16[4096,2048]{1,0:T(8,128)(2,1)} %gather_all.1, bf16[1065,2048]{1,0:T(8,128)(2,1)} %copy-done.37), kind=kOutput, calls=%fused_computation.194 | convolution fusion | flops 17867735040 | bytes 38588416 | tf_op jit(solution)/shard_map/dot_general | solution.py:55
  305.5 5.2 copy-done.5
  310.8 24.2 %select_reduce_fusion.2 = (f32[4096]{0:T(1024)S(1)}, f32[4096]{0:T(1024)S(1)}, f32[4096,528]{0,1:T(8,128)}, f32[528,4096]{1,0:T(8,128)}) fusion(pred[528]{0:T(1024)(128)(4,1)S(1)} %copy-done.51, f32[4096,1065]{0,1:T(8,128)} %copy-done.5, bf16[4096,2048]{1,0:T(8,128)(2,1)} %all-gather.5.cloned.1.call-done, ...), kind=kOutput, calls=%fused_computation.10 | convolution fusion | flops 8884314112 | bytes 53576208 | tf_op jit(solution)/shard_map/dot_general | solution.py:55
  335.6 4.9 all-to-all-start
  344.8 11.2 %psum.36 = f32[9,512]{1,0:T(8,128)S(1)} all-reduce(f32[9,512]{1,0:T(8,128)S(1)} %pad_maximum_fusion.17), channel_id=1, replica_groups=mesh['ep'=8,'tp'=4] {'tp'}, use_global_device_ids=true, to_apply=%region_17.18 | all-reduce | flops 4608 | bytes 36864 | tf_op jit(solution)/shard_map/psum | solution.py:1057
  360.2 22.9 %all_gather.12 = f32[4096,8]{0,1:T(8,128)S(1)} all-gather(f32[512,8]{0,1:T(8,128)S(1)} %convert_element_type.144), channel_id=1, replica_groups=mesh['ep'=8,'tp'=4] {'ep'}, dimensions={0}, use_global_device_ids=true | all-gather | bytes 147456 | tf_op jit(solution)/shard_map/all_gather | solution.py:1119
  384.1 10.3 %multiply_convert_fusion.1 = (bf16[4096,528]{0,1:T(8,128)(2,1)S(1)}, bf16[4096,528]{0,1:T(8,128)(2,1)S(1)}) fusion(f32[4096,1065]{0,1:T(8,128)} %copy-done.5, f32[528,4096]{1,0:T(8,128)} %get-tuple-element.151, f32[4096]{0:T(1024)S(1)} %bitcast.180, f32[4096]{0:T(1024)S(1)} %select_reduce_fusion.3, pred[528]{0:T(1024)(128)(4,1)S(1)} %copy-done.51), kind=kLoop, calls=%fused_computation.12 | loop fusion | flops 32440320 | bytes 34636304 | tf_op jit(solution)/shard_map/convert_element_type | solution.py:1206
  394.4 24.3 %fusion.80 = (bf16[1056,2048]{1,0:T(8,128)(2,1)}, f32[1056,2048]{1,0:T(8,128)}) fusion(bf16[4096,2048]{1,0:T(8,128)(2,1)} %gather_all.1, bf16[4096,528]{0,1:T(8,128)(2,1)S(1)} %get-tuple-element.109, bf16[4096,528]{0,1:T(8,128)(2,1)S(1)} %get-tuple-element.108), kind=kOutput, calls=%fused_computation.193 | convolution fusion | flops 17736204288 | bytes 38404096 | tf_op jit(solution)/shard_map/dot_general | solution.py:49
  418.8 26.7 %convolution_convert_fusion.p_ref = bf16[4096,2048]{1,0:T(8,128)(2,1)} fusion(bf16[4096,528]{0,1:T(8,128)(2,1)} %copy-done.10, bf16[4096,528]{0,1:T(8,128)(2,1)S(1)} %get-tuple-element.108, bf16[176,2048]{1,0:T(8,128)(2,1)S(1)} %bitcast.163, bf16[352,2048]{1,0:T(8,128)(2,1)} %bitcast.174, bf16[176,2048]{1,0:T(8,128)(2,1)S(1)} %bitcast.164, ...), kind=kOutput, calls=%fused_computation.2 | convolution fusion | flops 17759731712 | bytes 29753344 | tf_op jit(solution)/shard_map/dot_general | solution.py:1211
  445.5 117.8 %scatter_all.3 = f32[512,512]{1,0:T(8,128)S(1)} custom-call(bf16[4096,2048]{1,0:T(8,128)(2,1)} %convolution_convert_fusion.p_ref), custom_call_target="tpu_custom_call" | custom-call | tf_op jit(solution)/shard_map/scatter_all/pallas_call | solution.py:974
  565.4 6.1 psum.37
  574.0 17.8 %gather_tp.3 = bf16[512,2048]{1,0:T(8,128)(2,1)} custom-call(bf16[512,512]{1,0:T(8,128)(2,1)} %fusion.64.x_ref), custom_call_target="tpu_custom_call" | custom-call | tf_op jit(solution)/shard_map/gather_tp/pallas_call | solution.py:530
  600.1 20.0 %convolution_convert_fusion.1.p_ref = bf16[4096,2048]{1,0:T(8,128)(2,1)} fusion(bf16[176,2048]{1,0:T(8,128)(2,1)S(1)} %copy-done.35, bf16[352,2048]{1,0:T(8,128)(2,1)S(1)} %bitcast.206, f32[4096,528]{0,1:T(8,128)} %get-tuple-element.105, f32[4096]{0:T(1024)S(1)} %bitcast.181, f32[4096]{0:T(1024)S(1)} %select_reduce_fusion.3, pred[528]{0:T(1024)(128)(4,1)S(1)} %copy-done.51), kind=kOutput, calls=%fused_computation.3 | convolution fusion | flops 8877572096 | bytes 27623952 | tf_op jit(solution)/shard_map/dot_general | solution.py:1213
  620.1 14.5 %fusion.65 = f32[528,2048]{1,0:T(8,128)S(1)} fusion(bf16[4096,2048]{1,0:T(8,128)(2,1)} %all-gather.5.cloned.1.call-done, f32[4096,528]{0,1:T(8,128)} %get-tuple-element.105, f32[4096]{0:T(1024)S(1)} %bitcast.182, f32[4096]{0:T(1024)S(1)} %select_reduce_fusion.3, pred[528]{0:T(1024)(128)(4,1)S(1)} %copy-done.51), kind=kOutput, calls=%fused_computation.184 | convolution fusion | flops 8864858112 | bytes 29786640 | tf_op jit(solution)/shard_map/dot_general | solution.py:49
  638.7 5.8 all-to-all-start.1
  644.8 5.9 slice_bitcast_fusion.1
  650.8 5.5 fusion.19
  659.7 5.1 multiply_reduce_fusion
  670.8 131.3 %scatter_all.2 = f32[512,512]{1,0:T(8,128)S(1)} custom-call(bf16[4096,2048]{1,0:T(8,128)(2,1)} %convolution_convert_fusion.1.p_ref), custom_call_target="tpu_custom_call" | custom-call | tf_op jit(solution)/shard_map/scatter_all/pallas_call | solution.py:974
  817.1 5.3 convolution_convert_fusion.2.p_ref
  822.5 77.0 %scatter_ep.1 = f32[256,1536]{1,0:T(8,128)S(1)} custom-call(bf16[2048,1536]{1,0:T(8,128)(2,1)S(1)} %convolution_convert_fusion.2.p_ref), custom_call_target="tpu_custom_call" | custom-call | tf_op jit(solution)/shard_map/scatter_ep/pallas_call | solution.py:1043
  904.9 15.2 %scatter_tp.3 = f32[512,512]{1,0:T(8,128)S(1)} custom-call(bf16[512,2048]{1,0:T(8,128)(2,1)S(1)} %add_convert_fusion.p_ref), custom_call_target="tpu_custom_call" | custom-call | tf_op jit(solution)/shard_map/scatter_tp/pallas_call | solution.py:580
  920.8 22.4 %psum.39 = f32[14,512]{1,0:T(8,128)S(1)} all-reduce(f32[14,512]{1,0:T(8,128)S(1)} %concatenate.63), channel_id=1, replica_groups=mesh['ep'=8,'tp'=4] {'ep'}, use_global_device_ids=true, to_apply=%region_27.28 | all-reduce | flops 7168 | bytes 57344 | tf_op jit(solution)/shard_map/psum | solution.py:1338
  943.2 12.7 %psum.38 = f32[512,1]{0,1:T(1,128)S(1)} all-reduce(f32[512,1]{0,1:T(1,128)S(1)} %bitcast.195), channel_id=1, replica_groups=mesh['ep'=8,'tp'=4] {'tp'}, use_global_device_ids=true, to_apply=%region_23.24 | all-reduce | flops 512 | bytes 4096 | tf_op jit(solution)/shard_map/psum | solution.py:1057
  955.9 5.9 all_gather.15
  (261 shorter events, 144.3 us)
Async XLA Ops:
  7.2 173.1 %copy-start = (bf16[512,2048]{1,0:T(8,128)(2,1)S(1)}, bf16[512,2048]{1,0:T(8,128)(2,1)}, u32[]{:S(2)}) copy-start(bf16[512,2048]{1,0:T(8,128)(2,1)} %param.30) | copy-start | bytes 6291460
  7.2 75.9 %all-gather.3.cloned.1.call-start = ((), (), s32[]{:S(2)}) async-start(), calls=%async_computation.3 | async-start | bytes 4718592 | tf_op jit(solution)/shard_map/all_gather | solution.py:1116
  7.9 302.8 %all-gather.5.cloned.1.call-start = ((), (), s32[]{:S(2)}) async-start(), calls=%async_computation.4 | async-start | bytes 20971520 | tf_op jit(solution)/shard_map/all_gather | solution.py:1115
  83.1 21.1 %copy-start.52 = (f32[2048]{0:T(1024)S(1)}, f32[2048]{0:T(1024)}, u32[]{:S(2)}) copy-start(f32[2048]{0:T(1024)} %param.23) | copy-start | bytes 24580
  83.1 21.1 %copy-start.56 = (f32[512]{0:T(512)S(1)}, f32[512]{0:T(512)}, u32[]{:S(2)}) copy-start(f32[512]{0:T(512)} %param.29) | copy-start | bytes 6148
  104.2 15.4 %copy-start.46 = (f32[512]{0:T(512)}, f32[512]{0:T(512)S(1)}, u32[]{:S(2)}) copy-start(f32[512]{0:T(512)S(1)} %add_rsqrt_fusion.1) | copy-start | bytes 6148
  108.7 67.6 %collective-permute-start = (bf16[512,4,128]{0,2,1:T(8,128)(2,1)}, bf16[512,4,128]{0,2,1:T(8,128)(2,1)}, u32[]{:S(2)}, u32[]{:S(2)}) collective-permute-start(bf16[512,4,128]{0,2,1:T(8,128)(2,1)} %bitcast), channel_id=1, source_target_pairs={{0,4},{4,8},{8,12},{12,16},{16,20},{20,24},{24,28},{1,5},{5,9},{9,... | collective-permute-start | bytes 1572872 | tf_op jit(solution)/shard_map/ppermute | solution.py:23
  136.1 34.7 %collective-permute-start.1 = (bf16[512,4,128]{2,0,1:T(8,128)(2,1)}, bf16[512,4,128]{2,0,1:T(8,128)(2,1)}, u32[]{:S(2)}, u32[]{:S(2)}) collective-permute-start(bf16[512,4,128]{2,0,1:T(8,128)(2,1)} %pad_maximum_fusion.12), channel_id=1, source_target_pairs={{0,4},{4,8},{8,12},{12,16},{16,20},{20,24},{24,28},{1,5},{5,9},{9,... | collective-permute-start | bytes 1572872 | tf_op jit(solution)/shard_map/ppermute | solution.py:23
  180.3 19.7 %copy-start.59 = (bf16[4,128,512]{2,1,0:T(8,128)(2,1)}, bf16[4,128,512]{2,1,0:T(8,128)(2,1)S(1)}, u32[]{:S(2)}) copy-start(bf16[4,128,512]{2,1,0:T(8,128)(2,1)S(1)} %fusion.28) | copy-start | bytes 1572868
  180.3 19.7 %copy-start.7 = (bf16[512,512]{1,0:T(8,128)(2,1)S(1)}, bf16[512,512]{1,0:T(8,128)(2,1)}, u32[]{:S(2)}) copy-start(bf16[512,512]{1,0:T(8,128)(2,1)} %x_ref.1) | copy-start | bytes 1572868
  181.6 24.1 %copy-start.42 = (f32[512]{0:T(512)S(1)}, f32[512]{0:T(512)}, u32[]{:S(2)}) copy-start(f32[512]{0:T(512)} %dynamic_slice.30) | copy-start | bytes 6148
  200.3 371.3 %copy-start.4 = (f32[512,512]{1,0:T(8,128)}, f32[512,512]{1,0:T(8,128)S(1)}, u32[]{:S(2)}) copy-start(f32[512,512]{1,0:T(8,128)S(1)} %get-tuple-element.107) | copy-start | bytes 3145732
  281.9 28.8 %copy-start.51 = (pred[528]{0:T(1024)(128)(4,1)S(1)}, pred[528]{0:T(1024)(128)(4,1)}, u32[]{:S(2)}) copy-start(pred[528]{0:T(1024)(128)(4,1)} %iota_compare_fusion.2) | copy-start | bytes 1588
  310.8 45.3 %copy-start.44 = (pred[512,8]{0,1:T(8,128)(4,1)S(1)}, pred[512,8]{0,1:T(8,128)(4,1)}, u32[]{:S(2)}) copy-start(pred[512,8]{0,1:T(8,128)(4,1)} %copy-done.43) | copy-start | bytes 12292
  335.6 9.2 all-to-all-start
  356.1 38.3 %copy-start.38 = (f32[9,512]{1,0:T(8,128)}, f32[9,512]{1,0:T(8,128)S(1)}, u32[]{:S(2)}) copy-start(f32[9,512]{1,0:T(8,128)S(1)} %psum.36) | copy-start | bytes 55300
  394.4 24.4 %copy-start.10 = (bf16[4096,528]{0,1:T(8,128)(2,1)}, bf16[4096,528]{0,1:T(8,128)(2,1)S(1)}, u32[]{:S(2)}) copy-start(bf16[4096,528]{0,1:T(8,128)(2,1)S(1)} %get-tuple-element.109) | copy-start | bytes 12976132
  394.4 24.4 %copy-start.13 = (bf16[2048,176]{0,1:T(8,128)(2,1)S(1)}, bf16[2048,176]{0,1:T(8,128)(2,1)}, u32[]{:S(2)}) copy-start(bf16[2048,176]{0,1:T(8,128)(2,1)} %copy.151) | copy-start | bytes 2162692
  394.4 24.4 %copy-start.15 = (bf16[2048,176]{0,1:T(8,128)(2,1)S(1)}, bf16[2048,176]{0,1:T(8,128)(2,1)}, u32[]{:S(2)}) copy-start(bf16[2048,176]{0,1:T(8,128)(2,1)} %copy.150) | copy-start | bytes 2162692
  394.4 24.3 %copy-start.32 = (bf16[1,2048,352]{1,2,0:T(8,128)(2,1)S(1)}, bf16[1,2048,352]{1,2,0:T(8,128)(2,1)}, u32[]{:S(2)}) copy-start(bf16[1,2048,352]{1,2,0:T(8,128)(2,1)} %param.37) | copy-start | bytes 4325380
  445.5 117.8 %copy-start.49 = (f32[512]{0:T(512)S(1)}, f32[512]{0:T(512)}, u32[]{:S(2)}) copy-start(f32[512]{0:T(512)} %dynamic-slice_convert_fusion) | copy-start | bytes 6148
  638.7 331.2 %all-to-all-start.1 = ((bf16[8,3,176,256]{3,2,1,0:T(8,128)(2,1)}), bf16[8,3,176,256]{3,2,1,0:T(8,128)(2,1)}, u32[]{:S(2)}, u32[]{:S(2)}) async-start(bf16[8,3,176,256]{3,2,1,0:T(8,128)(2,1)} %maximum_bitcast_fusion), calls=%async_computation.2 | async-start | bytes 4325376 | tf_op jit(solution)/shard_map/all_to_all | solution.py:1229
  644.6 333.9 %reduce-scatter.2.cloned.1.call-start = ((), (), s32[]{:S(2)}) async-start(), calls=%async_computation.5 | async-start | bytes 2359296 | tf_op jit(solution)/shard_map/reduce_scatter | solution.py:1265
  650.7 14.1 %slice-start = ((s8[8388608]{0:T(1024)(128)(4,1)}), s8[4194304]{0:T(1024)(128)(4,1)S(1)}, s32[]{:S(2)}) async-start(s8[8388608]{0:T(1024)(128)(4,1)} %bitcast.150), calls=%async_computation.6 | async-start | bytes 8388608
  656.4 154.1 %collective-permute-start.3 = (bf16[512,4,128]{2,0,1:T(8,128)(2,1)S(1)}, bf16[512,4,128]{2,0,1:T(8,128)(2,1)S(1)}, u32[]{:S(2)}, u32[]{:S(2)}) collective-permute-start(bf16[512,4,128]{2,0,1:T(8,128)(2,1)S(1)} %slice.260), channel_id=1, source_target_pairs={{4,0},{8,4},{12,8},{16,12},{20,16},{24,20},{28,24},{5,1},{9,5},{13... | collective-permute-start | bytes 1572872 | tf_op jit(solution)/shard_map/ppermute | solution.py:23
  668.5 133.6 %copy-start.28 = (bf16[512,4,64]{2,0,1:T(8,128)(2,1)S(1)}, bf16[512,4,64]{2,0,1:T(8,128)(2,1)}, u32[]{:S(2)}) copy-start(bf16[512,4,64]{2,0,1:T(8,128)(2,1)} %copy-done.26) | copy-start | bytes 786436
  668.5 133.6 %copy-start.31 = (bf16[512,4,64]{2,0,1:T(8,128)(2,1)S(1)}, bf16[512,4,64]{2,0,1:T(8,128)(2,1)}, u32[]{:S(2)}) copy-start(bf16[512,4,64]{2,0,1:T(8,128)(2,1)} %copy-done.29) | copy-start | bytes 786436
  668.5 140.1 %collective-permute-start.2 = (bf16[512,4,128]{2,0,1:T(8,128)(2,1)S(1)}, bf16[512,4,128]{2,0,1:T(8,128)(2,1)S(1)}, u32[]{:S(2)}, u32[]{:S(2)}) collective-permute-start(bf16[512,4,128]{2,0,1:T(8,128)(2,1)S(1)} %slice.261), channel_id=1, source_target_pairs={{4,0},{8,4},{12,8},{16,12},{20,16},{24,20},{28,24},{5,1},{9,5},{13... | collective-permute-start | bytes 1572872 | tf_op jit(solution)/shard_map/ppermute | solution.py:23
  822.4 77.1 %copy-start.24 = (bf16[2048,512]{1,0:T(8,128)(2,1)S(1)}, bf16[2048,512]{1,0:T(8,128)(2,1)}, u32[]{:S(2)}) copy-start(bf16[2048,512]{1,0:T(8,128)(2,1)} %param.24) | copy-start | bytes 6291460
  903.5 16.7 %copy-start.8 = (bf16[512,512]{1,0:T(8,128)(2,1)S(1)}, bf16[512,512]{1,0:T(8,128)(2,1)}, u32[]{:S(2)}) copy-start(bf16[512,512]{1,0:T(8,128)(2,1)} %x_ref.1) | copy-start | bytes 1572868
  903.5 16.7 %copy-start.48 = (f32[512]{0:T(512)S(1)}, f32[512]{0:T(512)}, u32[]{:S(2)}) copy-start(f32[512]{0:T(512)} %dynamic_slice.37) | copy-start | bytes 6148
  904.9 15.7 %copy-start.40 = (f32[8,512]{1,0:T(8,128)S(1)}, f32[8,512]{1,0:T(8,128)}, u32[]{:S(2)}) copy-start(f32[8,512]{1,0:T(8,128)} %fusion.85) | copy-start | bytes 49156
  (41 other events, 162.9 us)
Sparse Core Ops, SparseCore 0:
  10.2 72.8 all-gather.2
  84.6 107.6 all-gather.4
  650.9 121.7 reduce-scatter.1

commit v2 on v1

--- a/solution.py
+++ b/solution.py
@@ -1,3 +1,4 @@
+import functools
 import math
 
 import jax
@@ -487,10 +488,10 @@
 
 
 def add_blocks(target, sources, rows):
-    step = 64
+    step = next(size for size in (64, 48, 16) if rows % size == 0)
 
     def body(i, carry):
-        span = pl.ds(pl.multiple_of(i * step, step), step)
+        span = pl.ds(pl.multiple_of(i * step, 16), step)
         total = target[span, :].astype(jnp.float32)
         for source in sources:
             total = total + source[span, :].astype(jnp.float32)
@@ -987,35 +988,55 @@
 
 
 def scatter_ep_kernel(
-    p_ref, o_ref, mine, from_y, from_below, from_above, own_sem, y_send, y_recv, up_send, up_recv, down_send, down_recv
+    p_ref, e_ref, o_ref, mine, from_y, from_below, from_above, own_sem, y_send, y_recv, up_send, up_recv, down_send, down_recv
 ):
     ep, tp, z, y, _, _ = place()
-    rows, cols = o_ref.shape
+    rows, extra = p_ref.shape[0] // 8, e_ref.shape[0]
+    tall = rows + extra
     across = (ep + 1 - 2 * y, tp)
-    above, below = (ep + 2, tp), (ep - 2, tp)
     greet([across], True)
 
     def part(z_at, y_at):
         return p_ref.at[pl.ds(pl.multiple_of((z_at * 2 + y_at) * rows, rows), rows), :]
 
     def own(z_at):
-        return pltpu.make_async_copy(part(z_at, y), mine.at[z_at], own_sem.at[z_at])
+        return (
+            pltpu.make_async_copy(part(z_at, y), mine.at[z_at, pl.ds(0, rows)], own_sem.at[z_at]),
+            pltpu.make_async_copy(e_ref, mine.at[z_at, pl.ds(rows, extra)], own_sem.at[4 + z_at]),
+        )
 
     def over_y(z_at):
-        return remote(part(z_at, 1 - y), from_y.at[z_at], y_send.at[z_at], y_recv.at[z_at], across)
+        return (
+            remote(
+                part(z_at, 1 - y),
+                from_y.at[z_at, pl.ds(0, rows)],
+                y_send.at[z_at],
+                y_recv.at[z_at],
+                across,
+            ),
+            remote(
+                e_ref,
+                from_y.at[z_at, pl.ds(rows, extra)],
+                y_send.at[4 + z_at],
+                y_recv.at[4 + z_at],
+                across,
+            ),
+        )
 
     for z_at in Z_ORDER:
-        over_y(z_at).start()
-        own(z_at).start()
+        for copy in over_y(z_at) + own(z_at):
+            copy.start()
 
     def blocks(z_at):
-        own(z_at).wait()
-        over_y(z_at).wait_recv()
-        add_blocks(mine.at[z_at], [from_y.at[z_at]], rows)
+        for copy in own(z_at):
+            copy.wait()
+        for copy in over_y(z_at):
+            copy.wait_recv()
+        add_blocks(mine.at[z_at], [from_y.at[z_at]], tall)
 
     def final(z_at, others):
         o_ref[...] = jnp.zeros_like(o_ref)
-        add_blocks(o_ref, [mine.at[z_at], *others], rows)
+        add_blocks(o_ref, [mine.at[z_at], *others], tall)
 
     z_chain(
         blocks,
@@ -1026,31 +1047,616 @@
         up_recv,
         down_send,
         down_recv,
-        rows,
+        tall,
         final,
     )
     for z_at in range(4):
-        over_y(z_at).wait_send()
-
-
-def scatter_ep(value, cid):
+        for copy in over_y(z_at):
+            copy.wait_send()
+
+
+def scatter_ep(value, extra, cid):
     rows, cols = value.shape[0] // 8, value.shape[1]
+    tall = rows + extra.shape[0]
     dma = pltpu.SemaphoreType.DMA
 
     def held():
-        return pltpu.VMEM((4, rows, cols), value.dtype)
+        return pltpu.VMEM((4, tall, cols), value.dtype)
 
     return pl.pallas_call(
         scatter_ep_kernel,
-        out_shape=jax.ShapeDtypeStruct((rows, cols), jnp.float32),
-        in_specs=[pl.BlockSpec(memory_space=pl.ANY)],
+        out_shape=jax.ShapeDtypeStruct((tall, cols), jnp.float32),
+        in_specs=[pl.BlockSpec(memory_space=pl.ANY)] * 2,
         out_specs=pl.BlockSpec(memory_space=pltpu.VMEM),
-        scratch_shapes=[held(), held(), held(), held()] + [dma((4,))] * 7,
+        scratch_shapes=[held(), held(), held(), held()] + [dma((8,))] * 3 + [dma((4,))] * 4,
         compiler_params=pltpu.CompilerParams(
             collective_id=cid, has_side_effects=True, vmem_limit_bytes=40 * 2**20
         ),
         name="scatter_ep",
-    )(value)
+    )(value, extra)
+
+
+def experts_kernel(
+    expert_width,
+    shared_width,
+    expert_total,
+    x_ref,
+    g_ref,
+    kept_ref,
+    expert_gate_ref,
+    shared_gate_ref,
+    extra_ref,
+    expert_up_ref,
+    shared_up_ref,
+    expert_down_ref,
+    shared_down_ref,
+    all_ref,
+    hidden_ref,
+    both_ref,
+    out_ref,
+    grad_ref,
+    logit_ref,
+    in_ref,
+    down_ref,
+    scalars,
+    kept_held,
+    x_held,
+    g_held,
+    lin,
+    hidden_grad,
+    hidden_held,
+    both_held,
+    out_held,
+    kept_cols,
+    staged,
+    mine,
+    from_sib,
+    from_b,
+    from_a,
+    from_below,
+    from_above,
+    up_sem,
+    down_sem,
+    a_sem,
+    b_sem,
+    s_sem,
+    recv_sem,
+    sib_sem,
+    own_sem,
+    load_sem,
+    store_sem,
+    weight_sem,
+    kept_send,
+    kept_recv,
+    rs_send,
+    rs_recv,
+    rb_send,
+    rb_recv,
+    ra_send,
+    ra_recv,
+    ru_send,
+    ru_recv,
+    rd_send,
+    rd_recv,
+):
+    ep, tp, z, y, x, core = place()
+    rows, cols = x_ref.shape
+    width = down_ref.shape[0]
+    peer_a, peer_b, sibling, above, below = lane_peers()
+    sources = kept_held.shape[0]
+    others = [(lax.rem(ep + i, sources), tp) for i in range(1, sources)]
+    x_peer = (ep, tp + 2 - 4 * x)
+    greet([x_peer, sibling] + others)
+
+    def spot(z_at, da, db):
+        group, quarter = lane_spot(z_at, da, db, core)
+        return all_ref.at[
+            pl.ds(pl.multiple_of(group * rows, rows), rows),
+            pl.ds(pl.multiple_of(quarter * cols, cols), cols),
+        ]
+
+    def at(z_at, da, db):
+        return z_at * 4 + da * 2 + db
+
+    turns = (
+        z,
+        1 + lax.rem(z, 2),
+        jnp.where(z == 0, 2, jnp.where(z == 1, 0, jnp.where(z == 2, 3, 1))),
+        3 * (1 - z // 2),
+    )
+    edge = (z == 0) | (z == 3)
+
+    def arrived(z_at, da, db):
+        block, n = spot(z_at, da, db), at(z_at, da, db)
+        remote(block, block, s_sem.at[n], recv_sem.at[n], sibling).wait_recv()
+        return block
+
+    def up(z_at, source):
+        return remote(source, spot(z_at, 0, 0), up_sem.at[z_at], recv_sem.at[at(z_at, 0, 0)], above)
+
+    def down(z_at, source):
+        return remote(source, spot(z_at, 0, 0), down_sem.at[z_at], recv_sem.at[at(z_at, 0, 0)], below)
+
+    def over_a(z_at, source):
+        return remote(source, spot(z_at, 0, 0), a_sem.at[z_at], recv_sem.at[at(z_at, 1, 0)], peer_a)
+
+    def over_b(z_at, da, source):
+        return remote(
+            source, spot(z_at, da, 0), b_sem.at[z_at * 2 + da], recv_sem.at[at(z_at, da, 1)], peer_b
+        )
+
+    def to_sibling(z_at, da, db, source):
+        n = at(z_at, da, db)
+        return remote(source, spot(z_at, da, db), s_sem.at[n], sib_sem.at[n], sibling)
+
+    def pass_z(k):
+        z_at = turns[k]
+        block = arrived(z_at, 0, 0)
+
+        @pl.when((z_at > z) & (z > 0))
+        def _():
+            down(z_at, block).start()
+
+        @pl.when((z_at < z) & (z < 3))
+        def _():
+            up(z_at, block).start()
+
+        over_a(z_at, block).start()
+        over_b(z_at, 0, block).start()
+        to_sibling(z_at, 0, 0, block).start()
+
+    def pass_a(k):
+        block = arrived(turns[k], 1, 0)
+        over_b(turns[k], 1, block).start()
+        to_sibling(turns[k], 1, 0, block).start()
+
+    def pass_b(k, da):
+        block = arrived(turns[k], da, 1)
+        to_sibling(turns[k], da, 1, block).start()
+
+    def sibling_blocks(k, dy):
+        for dx in range(2):
+            da, db = core * dy + (1 - core) * dx, core * dx + (1 - core) * dy
+            n = at(turns[k], da, db)
+            block = spot(0, 0, 0)
+            remote(block, block, s_sem.at[n], sib_sem.at[n], sibling).wait_recv()
+
+    def group_rows(k, dy):
+        group = turns[k] * 2 + y + (1 - 2 * y) * dy
+        return group, pl.ds(pl.multiple_of(group * rows, rows), rows)
+
+    def load_x(k, dy):
+        _, span = group_rows(k, dy)
+        return pltpu.make_async_copy(all_ref.at[span, :], x_held.at[dy], load_sem.at[dy])
+
+    def load_g(k, dy):
+        _, span = group_rows(k, dy)
+        return pltpu.make_async_copy(g_ref.at[span, :], g_held.at[dy], load_sem.at[2 + dy])
+
+    def project(k, dy):
+        def body(i, carry):
+            cut = pl.ds(pl.multiple_of(i * width, width), width)
+            lin[:, cut] = times_transpose(x_held[dy], in_ref[cut, :])
+            return carry
+
+        lax.fori_loop(0, 2, body, 0)
+
+    def project_grad(k, dy):
+        hidden_grad[...] = times_transpose(g_held[dy], down_ref[...])
+
+    def stores(k, dy):
+        _, span = group_rows(k, dy)
+        return (
+            pltpu.make_async_copy(hidden_held.at[dy], hidden_ref.at[span, :], store_sem.at[dy]),
+            pltpu.make_async_copy(both_held.at[dy], both_ref.at[span, :], store_sem.at[2 + dy]),
+            pltpu.make_async_copy(out_held.at[dy], out_ref.at[span, :], store_sem.at[4 + dy]),
+        )
+
+    step = 64
+    tile_start = width - 128
+    logit_at = expert_width + shared_width - tile_start
+
+    def activate(k, dy):
+        group, _ = group_rows(k, dy)
+        lane = lax.broadcasted_iota(jnp.int32, (1, width), 1)
+        near = lax.broadcasted_iota(jnp.int32, (1, 128), 1)
+        is_logit = (near >= logit_at) & (near < logit_at + expert_total)
+        kept_cols[:, :16] = kept_held[group].astype(jnp.float32).T
+
+        def body(i, carry):
+            span = pl.ds(pl.multiple_of(i * step, step), step)
+            gate_lin, up_lin = lin[span, :width], lin[span, width:]
+            grad = hidden_grad[span, :]
+            tail = lin[span, tile_start:width]
+            if k == 0 and dy == 0:
+                logit_ref[span, :] = tail
+            most = jnp.max(jnp.where(is_logit, tail, -1e30), axis=1, keepdims=True)
+            powers = jnp.where(is_logit, jnp.exp(jnp.minimum(tail - most, 0.0)), 0.0)
+            kept = jnp.sum(jnp.where(near == ep, kept_cols[span, :], 0.0), axis=1, keepdims=True)
+            gate = jnp.sum(jnp.where(near == logit_at + ep, powers, 0.0), axis=1, keepdims=True)
+            gate = gate / jnp.sum(powers, axis=1, keepdims=True) * kept
+            switch = jax.nn.sigmoid(
+                jnp.sum(
+                    jnp.where(near == logit_at + expert_total, tail, 0.0), axis=1, keepdims=True
+                )
+            )
+            scale = jnp.where(lane < expert_width, gate, switch)
+            sig = jax.nn.sigmoid(gate_lin)
+            act = gate_lin * sig
+            hidden = act * up_lin
+            agreement = hidden * grad
+            gate_part = jnp.sum(jnp.where(lane < expert_width, agreement, 0.0), axis=1, keepdims=True)
+            switch_part = jnp.sum(
+                jnp.where(lane < expert_width, 0.0, agreement), axis=1, keepdims=True
+            )
+            scaled = grad * scale
+            hidden_held[dy, span, :] = (hidden * scale).astype(jnp.bfloat16)
+            both_held[dy, span, :width] = (
+                scaled * up_lin * sig * (1.0 + gate_lin * (1.0 - sig))
+            ).astype(jnp.bfloat16)
+            both_held[dy, span, width:] = (scaled * act).astype(jnp.bfloat16)
+            scalars[span, :] = jnp.where(
+                near == ep, gate_part, jnp.where(near == expert_total, switch_part, 0.0)
+            )
+            return carry
+
+        lax.fori_loop(0, rows // step, body, 0)
+
+    def out_rows(k, dy):
+        def body(i, carry):
+            cut = pl.ds(pl.multiple_of(i * cols, cols), cols)
+            out_held[dy, :, cut] = jnp.dot(
+                hidden_held[dy], down_ref[:, cut], preferred_element_type=jnp.float32
+            ).astype(jnp.bfloat16)
+            return carry
+
+        lax.fori_loop(0, 4, body, 0)
+
+    tall = mine.shape[1]
+
+    def lane_at(k, dx, dy, core_at):
+        da, db = (1 - core_at) * dy + core_at * dx, (1 - core_at) * dx + core_at * dy
+        return at(turns[k], da, db)
+
+    def rs_sibling(k, dx, dy):
+        n = lane_at(k, dx, dy, 1 - core)
+        return remote(
+            staged.at[dy * 2 + dx], from_sib.at[n], rs_send.at[n], rs_recv.at[n], sibling
+        )
+
+    def grad_rows(k, dy):
+        sums = scalars[...].T[:16, :].astype(jnp.bfloat16)
+
+        def body(dx, carry):
+            x_at = x + (1 - 2 * x) * dx
+            theirs = pl.ds(pl.multiple_of((x_at * 2 + 1 - core) * cols, cols), cols)
+            ours = pl.ds(pl.multiple_of((x_at * 2 + core) * cols, cols), cols)
+            staged[dy * 2 + dx, :rows, :] = jnp.dot(
+                both_held[dy], in_ref[:, theirs], preferred_element_type=jnp.float32
+            ).astype(jnp.bfloat16)
+            staged[dy * 2 + dx, rows:, :] = sums
+            rs_sibling(k, dx, dy).start()
+            ours_at = lane_at(k, dx, dy, core)
+            mine[ours_at, :rows, :] = jnp.dot(
+                both_held[dy], in_ref[:, ours], preferred_element_type=jnp.float32
+            ).astype(jnp.bfloat16)
+            mine[ours_at, rows:, :] = sums
+            return carry
+
+        lax.fori_loop(0, 2, body, 0)
+
+    def staged_free(k, dy):
+        for dx in range(2):
+            rs_sibling(k, dx, dy).wait_send()
+
+    def rs_over_b(k, da):
+        n = turns[k] * 2 + da
+        return remote(
+            mine.at[at(turns[k], da, 1)], from_b.at[n], rb_send.at[n], rb_recv.at[n], peer_b
+        )
+
+    def rs_over_a(k):
+        z_at = turns[k]
+        return remote(
+            mine.at[at(z_at, 1, 0)], from_a.at[z_at], ra_send.at[z_at], ra_recv.at[z_at], peer_a
+        )
+
+    def rs_up(z_at):
+        return remote(
+            mine.at[at(z_at, 0, 0)], from_below.at[z_at], ru_send.at[z_at], ru_recv.at[z_at], above
+        )
+
+    def rs_down(z_at):
+        return remote(
+            mine.at[at(z_at, 0, 0)], from_above.at[z_at], rd_send.at[z_at], rd_recv.at[z_at], below
+        )
+
+    def reduce_sibling(k, dy):
+        for dx in range(2):
+            n = lane_at(k, dx, dy, core)
+            remote(staged.at[0], from_sib.at[n], rs_send.at[n], rs_recv.at[n], sibling).wait_recv()
+            add_blocks(mine.at[n], [from_sib.at[n]], tall)
+
+        @pl.when(core == 0)
+        def _():
+            rs_over_b(k, dy).start()
+
+        if dy == 1:
+
+            @pl.when(core == 1)
+            def _():
+                rs_over_b(k, 0).start()
+                rs_over_b(k, 1).start()
+
+    def reduce_b(k):
+        rs_over_b(k, 1).wait_recv()
+        add_blocks(mine.at[at(turns[k], 1, 0)], [from_b.at[turns[k] * 2 + 1]], tall)
+        rs_over_a(k).start()
+
+    def reduce_a(k):
+        z_at = turns[k]
+        rs_over_b(k, 0).wait_recv()
+        rs_over_a(k).wait_recv()
+        add_blocks(mine.at[at(z_at, 0, 0)], [from_b.at[z_at * 2], from_a.at[z_at]], tall)
+        if k > 0:
+
+            @pl.when(z == 0)
+            def _():
+                rs_up(z_at).start()
+
+            @pl.when(z == 3)
+            def _():
+                rs_down(z_at).start()
+
+    def chain(z_at):
+        @pl.when(z_at > z)
+        def _():
+            rs_up(z_at).wait_recv()
+            add_blocks(mine.at[at(z_at, 0, 0)], [from_below.at[z_at]], tall)
+            rs_up(z_at).start()
+
+        @pl.when(z_at < z)
+        def _():
+            rs_down(z_at).wait_recv()
+            add_blocks(mine.at[at(z_at, 0, 0)], [from_above.at[z_at]], tall)
+            rs_down(z_at).start()
+
+    own = pltpu.make_async_copy(x_ref, spot(z, 0, 0), own_sem)
+    over_b(z, 0, x_ref).start()
+    over_a(z, x_ref).start()
+
+    @pl.when(z < 3)
+    def _():
+        up(z, x_ref).start()
+
+    @pl.when(z > 0)
+    def _():
+        down(z, x_ref).start()
+
+    to_sibling(z, 0, 0, x_ref).start()
+    own.start()
+    load_g(0, 0).start()
+
+    def kept_to(i):
+        return remote(
+            kept_ref, kept_held.at[ep], kept_send.at[i - 1], kept_recv.at[i - 1], others[i - 1]
+        )
+
+    for i in range(1, sources):
+        kept_to(i).start()
+    own_kept = pltpu.make_async_copy(kept_ref, kept_held.at[ep], weight_sem.at[7])
+    own_kept.start()
+    pieces = [
+        (expert_gate_ref, in_ref, 0),
+        (shared_gate_ref, in_ref, expert_width),
+        (extra_ref, in_ref, expert_width + shared_width),
+        (expert_up_ref, in_ref, width),
+        (shared_up_ref, in_ref, width + expert_width),
+        (expert_down_ref, down_ref, 0),
+    ]
+    weight_copies = [
+        pltpu.make_async_copy(piece, target.at[pl.ds(at_row, piece.shape[0]), :], weight_sem.at[i])
+        for i, (piece, target, at_row) in enumerate(pieces)
+    ]
+    weight_copies.append(
+        pltpu.make_async_copy(
+            shared_down_ref.at[pl.ds(pl.multiple_of(ep * shared_width, 16), shared_width), :],
+            down_ref.at[pl.ds(expert_width, shared_width), :],
+            weight_sem.at[6],
+        )
+    )
+    for copy in weight_copies:
+        copy.start()
+    filled = expert_width + shared_width
+    for target, first, last_row in (
+        (in_ref, filled + 16, width),
+        (in_ref, width + filled, 2 * width),
+        (down_ref, filled, width),
+    ):
+        target[first:last_row, :] = jnp.zeros((last_row - first, target.shape[1]), target.dtype)
+    for copy in weight_copies:
+        copy.wait()
+    own_kept.wait()
+    for i in range(1, sources):
+        kept_to(i).wait_recv()
+    own.wait()
+
+    def ready(k, dy):
+        if dy == 0:
+            pass_a(k)
+            pass_b(k, 0)
+        else:
+            pass_b(k, 1)
+        sibling_blocks(k, dy)
+        load_x(k, dy).start()
+
+    order = [(k, dy) for k in range(4) for dy in range(2)]
+    ready(0, 0)
+    for s, (k, dy) in enumerate(order):
+        following = order[s + 1] if s < 7 else None
+        load_x(k, dy).wait()
+        load_g(k, dy).wait()
+        if following is not None:
+            load_g(*following).start()
+        project(k, dy)
+        if s == 0:
+            pass_z(1)
+        if s >= 1:
+            reduce_sibling(*order[s - 1])
+        project_grad(k, dy)
+        if s == 0:
+            pass_z(2)
+        if s == 1:
+            pass_z(3)
+        if dy == 1 and k >= 1:
+            reduce_b(k - 1)
+        if s >= 2:
+            for copy in stores(*order[s - 2]):
+                copy.wait()
+        activate(k, dy)
+        if following is not None:
+            ready(*following)
+        if dy == 0 and k >= 2:
+            reduce_a(k - 2)
+        if s >= 2:
+            staged_free(*order[s - 2])
+        grad_rows(k, dy)
+        out_rows(k, dy)
+        for copy in stores(k, dy):
+            copy.start()
+    reduce_sibling(3, 1)
+    reduce_a(2)
+    reduce_b(3)
+    for s in (6, 7):
+        for copy in stores(*order[s]):
+            copy.wait()
+    reduce_a(3)
+
+    @pl.when(z == 1)
+    def _():
+        for z_at in (2, 3, 0):
+            chain(z_at)
+
+    @pl.when(z == 2)
+    def _():
+        for z_at in (1, 0, 3):
+            chain(z_at)
+
+    last = mine.at[at(z, 0, 0)]
+
+    @pl.when(z > 0)
+    def _():
+        rs_up(z).wait_recv()
+
+    @pl.when(z < 3)
+    def _():
+        rs_down(z).wait_recv()
+
+    grad_ref[...] = jnp.zeros_like(grad_ref)
+
+    @pl.when(z == 0)
+    def _():
+        add_blocks(grad_ref, [last, from_above.at[0]], tall)
+
+    @pl.when(z == 3)
+    def _():
+        add_blocks(grad_ref, [last, from_below.at[3]], tall)
+
+    @pl.when((z > 0) & (z < 3))
+    def _():
+        add_blocks(grad_ref, [last, from_below.at[z], from_above.at[z]], tall)
+
+    for i in range(1, sources):
+        kept_to(i).wait_send()
+    staged_free(3, 0)
+    staged_free(3, 1)
+
+    def finish(i, carry):
+        over_a(i, x_ref).wait_send()
+        over_b(i, 0, x_ref).wait_send()
+        over_b(i, 1, x_ref).wait_send()
+        remote(mine.at[0], from_a.at[0], ra_send.at[i], ra_recv.at[i], peer_a).wait_send()
+        for da in range(2):
+            n = i * 2 + da
+            remote(mine.at[0], from_b.at[0], rb_send.at[n], rb_recv.at[n], peer_b).wait_send()
+        for n in range(4):
+            block = spot(0, 0, 0)
+            remote(block, block, s_sem.at[i * 4 + n], sib_sem.at[i * 4 + n], sibling).wait_send()
+
+        @pl.when((z < 3) & (i <= z))
+        def _():
+            up(i, x_ref).wait_send()
+
+        @pl.when((z > 0) & (i >= z))
+        def _():
+            down(i, x_ref).wait_send()
+
+        @pl.when(i > z)
+        def _():
+            rs_up(i).wait_send()
+
+        @pl.when(i < z)
+        def _():
+            rs_down(i).wait_send()
+
+        return carry
+
+    lax.fori_loop(0, 4, finish, 0)
+
+
+def experts(x_cols, grads_all, kept_rows, weights, expert_total, cid):
+    rows, cols = x_cols.shape
+    total, model_dim = grads_all.shape
+    expert_width, shared_width = weights[0].shape[0], weights[1].shape[0]
+    width = -(-(expert_width + shared_width + expert_total + 1) // 128) * 128
+    low, dma = jnp.bfloat16, pltpu.SemaphoreType.DMA
+    vmem, hbm = pl.BlockSpec(memory_space=pltpu.VMEM), pl.BlockSpec(memory_space=pl.ANY)
+
+    def held(count):
+        return pltpu.VMEM((count, rows + 16, cols), low)
+
+    return pl.pallas_call(
+        functools.partial(experts_kernel, expert_width, shared_width, expert_total),
+        out_shape=[
+            jax.ShapeDtypeStruct((total, model_dim), low),
+            jax.ShapeDtypeStruct((total, width), low),
+            jax.ShapeDtypeStruct((total, 2 * width), low),
+            jax.ShapeDtypeStruct((total, model_dim), low),
+            jax.ShapeDtypeStruct((rows + 16, cols), jnp.float32),
+            jax.ShapeDtypeStruct((rows, 128), jnp.float32),
+        ],
+        in_specs=[hbm] * 10,
+        out_specs=[hbm, hbm, hbm, hbm, vmem, vmem],
+        scratch_shapes=[
+            pltpu.VMEM((2 * width, model_dim), low),
+            pltpu.VMEM((width, model_dim), low),
+            pltpu.VMEM((rows, 128), jnp.float32),
+            pltpu.VMEM((total // rows, 16, rows), low),
+            pltpu.VMEM((2, rows, model_dim), low),
+            pltpu.VMEM((2, rows, model_dim), low),
+            pltpu.VMEM((rows, 2 * width), jnp.float32),
+            pltpu.VMEM((rows, width), jnp.float32),
+            pltpu.VMEM((2, rows, width), low),
+            pltpu.VMEM((2, rows, 2 * width), low),
+            pltpu.VMEM((2, rows, model_dim), low),
+            pltpu.VMEM((rows, 128), jnp.float32),
+            held(4),
+            held(16),
+            held(16),
+            held(8),
+            held(4),
+            held(4),
+            held(4),
+        ]
+        + [dma((4,)), dma((4,)), dma((4,)), dma((8,)), dma((16,)), dma((16,)), dma((16,)), dma]
+        + [dma((4,)), dma((6,)), dma((8,)), dma((7,)), dma((7,))]
+        + [dma((16,)), dma((16,)), dma((8,)), dma((8,))]
+        + [dma((4,))] * 6,
+        compiler_params=pltpu.CompilerParams(
+            collective_id=cid, has_side_effects=True, vmem_limit_bytes=63 * 2**20
+        ),
+        name="experts",
+    )(x_cols, grads_all, kept_rows, *weights)
 
 
 def tp_total(value):
@@ -1112,11 +1718,8 @@
     def own_cols(vector):
         return lax.dynamic_slice_in_dim(vector, tp * col_width, col_width, vector.ndim - 1)
 
-    grads_all = lax.all_gather(
-        lax.all_gather(out_grad, "ep", axis=0, tiled=True), "tp", axis=1, tiled=True
-    )
     kept_own = kept_choice(expert_ids, pair_order, expert_total, capacity)
-    kept_all = lax.all_gather(kept_own, "ep", axis=0, tiled=True)
+    grads_all = gather_all(out_grad, 2)
 
     inputs_full = gather_tp(tokens, 0).astype(jnp.float32)
     unit_one, inv_one = row_stats(inputs_full)
@@ -1164,64 +1767,47 @@
     unit_two = hidden_cols * inv_two
     second_cols = own_cols(second_gain)
     normed_cols = (unit_two * second_cols).astype(jnp.bfloat16)
-    normed_all = gather_all(normed_cols, 2)
-
-    def hidden_rows(expert_part, shared_part):
-        cut = lax.dynamic_slice_in_dim(shared_part, ep * shared_width, shared_width, 1)
-        return jnp.concatenate([expert_part[0].T, cut.T], axis=0)
-
-    gate_rows = hidden_rows(expert_gate_weight, shared_gate_weight)
-    up_rows = hidden_rows(expert_up_weight, shared_up_weight)
-    down_rows = jnp.concatenate(
+
+    def shared_rows(weight):
+        return lax.dynamic_slice_in_dim(weight, ep * shared_width, shared_width, 1).T
+
+    extra_rows = jnp.concatenate([router_weight.T, switch_vector[None, :]], axis=0)
+    extra_rows = jnp.pad(extra_rows, ((0, 16 - extra_rows.shape[0]), (0, 0)))
+    kept_rows = jnp.pad(kept_own.T, ((0, 16 - expert_total), (0, 0))).astype(jnp.bfloat16)
+    normed_all, hidden_all, both_all, out_part, reduced, logit_tile = experts(
+        normed_cols,
+        grads_all,
+        kept_rows,
         [
+            expert_gate_weight[0].T,
+            shared_rows(shared_gate_weight),
+            extra_rows,
+            expert_up_weight[0].T,
+            shared_rows(shared_up_weight),
             expert_down_weight[0],
-            lax.dynamic_slice_in_dim(shared_down_weight, ep * shared_width, shared_width, 0),
+            shared_down_weight,
         ],
-        axis=0,
-    )
-    both_rows = jnp.concatenate([gate_rows, up_rows], axis=0)
-    rows_in = jnp.concatenate([both_rows, router_weight.T, switch_vector[None, :]], axis=0)
-    lin_all = times_transpose(normed_all, rows_in)
-    gate_lin = lin_all[:, :width]
-    up_lin = lin_all[:, width : 2 * width]
-    logits = lin_all[:, 2 * width : 2 * width + expert_total]
-    router_probs = softmax_rows(logits)
-    gates_all = jnp.sum(
-        jnp.where(jnp.arange(expert_total)[None, :] == ep, router_probs * kept_all, 0.0),
-        axis=1,
-        keepdims=True,
-    )
-    switch_all = jax.nn.sigmoid(lin_all[:, 2 * width + expert_total :])
-    is_expert = jnp.arange(width)[None, :] < expert_width
-    scale = jnp.where(is_expert, gates_all, switch_all)
-    hidden_grad = times_transpose(grads_all, down_rows)
-    gate_sig = jax.nn.sigmoid(gate_lin)
-    gate_act = gate_lin * gate_sig
-    hidden = gate_act * up_lin
-    agreement = hidden * hidden_grad
-    gate_part = jnp.sum(jnp.where(is_expert, agreement, 0.0), axis=1)
-    switch_part = jnp.sum(jnp.where(is_expert, 0.0, agreement), axis=1)
-    scaled_hidden = (hidden * scale).astype(jnp.bfloat16)
-    scaled_grad = hidden_grad * scale
-    gate_lin_grad = (scaled_grad * up_lin * gate_sig * (1.0 + gate_lin * (1.0 - gate_sig))).astype(
-        jnp.bfloat16
-    )
-    up_lin_grad = (scaled_grad * gate_act).astype(jnp.bfloat16)
-    both_grad = jnp.concatenate([gate_lin_grad, up_lin_grad], axis=1)
-    normed_grad_part = jnp.dot(both_grad, both_rows, preferred_element_type=jnp.float32)
-    normed_grad = scatter_all(normed_grad_part.astype(jnp.bfloat16), 3)
-    out_part = jnp.dot(scaled_hidden, down_rows, preferred_element_type=jnp.float32)
-    ffn_cols = scatter_all(out_part.astype(jnp.bfloat16), 3)
-    layer_out = (hidden_cols + ffn_cols).astype(jnp.bfloat16)
-    down_grad = inner_rows(scaled_hidden, grads_all)
-    both_rows_grad = inner_rows(both_grad, normed_all)
+        expert_total,
+        4,
+    )
+    padded = hidden_all.shape[1]
+    ffn_cols = lax.psum_scatter(
+        lax.psum_scatter(out_part, "tp", scatter_dimension=1, tiled=True),
+        "ep",
+        scatter_dimension=0,
+        tiled=True,
+    )
+    layer_out = (hidden_cols + ffn_cols.astype(jnp.float32)).astype(jnp.bfloat16)
+    down_grad = inner_rows(hidden_all[:, :width], grads_all)
+    gate_rows_grad = inner_rows(both_all[:, :width], normed_all)
+    up_rows_grad = inner_rows(both_all[:, padded : padded + width], normed_all)
     expert_down_grad = down_grad[None, :expert_width]
-    expert_gate_grad = both_rows_grad[:expert_width].T[None]
-    expert_up_grad = both_rows_grad[width : width + expert_width].T[None]
+    expert_gate_grad = gate_rows_grad[:expert_width].T[None]
+    expert_up_grad = up_rows_grad[:expert_width].T[None]
     shared_parts = jnp.stack(
         [
-            both_rows_grad[expert_width:width],
-            both_rows_grad[width + expert_width :],
+            gate_rows_grad[expert_width:],
+            up_rows_grad[expert_width:],
             down_grad[expert_width:],
         ]
     ).astype(jnp.bfloat16)
@@ -1233,16 +1819,12 @@
     shared_up_grad = shared_parts[1].T
     shared_down_grad = shared_parts[2]
 
-    scalar_parts = jnp.stack([gate_part, switch_part]).reshape(2, sources, tok_count).swapaxes(0, 1)
-    scalar_parts = lax.all_to_all(scalar_parts, "ep", split_axis=0, concat_axis=0, tiled=True)
-    scalar_sums = tp_total(
-        jnp.concatenate([scalar_parts[:, 0], jnp.sum(scalar_parts[:, 1], axis=0)[None]], axis=0)
-    )
-    probs_grad = scalar_sums[:sources].T * kept_own
-    switch_grad = scalar_sums[sources]
-    own_rows = lax.dynamic_slice_in_dim(lin_all, ep * tok_count, tok_count, 0)
-    probs_own = softmax_rows(own_rows[:, 2 * width : 2 * width + expert_total])
-    switch = jax.nn.sigmoid(own_rows[:, 2 * width + expert_total])
+    normed_grad = reduced[:tok_count]
+    probs_grad = reduced[tok_count : tok_count + expert_total].T * kept_own
+    switch_grad = reduced[tok_count + expert_total]
+    logit_at = width - (padded - 128)
+    probs_own = softmax_rows(logit_tile[:, logit_at : logit_at + expert_total])
+    switch = jax.nn.sigmoid(logit_tile[:, logit_at + expert_total])
     logit_grad = (
         probs_own * (probs_grad - jnp.sum(probs_own * probs_grad, axis=-1, keepdims=True))
     ).astype(jnp.bfloat16)
@@ -1314,7 +1896,6 @@
         .astype(jnp.bfloat16)
     )
     lin_grads = jnp.concatenate([query_lin_grad, key_lin_grad, value_lin_grad], axis=1)
-    weight_grads = scatter_ep(inner_rows(normed_one, lin_grads).astype(jnp.bfloat16), 5)
     lin_width = head_count * HD
     normed_one_grad = times_transpose(query_lin_grad, query_weight) + times_transpose(
         key_lin_grad, key_weight
@@ -1329,20 +1910,27 @@
     tokens_grad = (hidden_grad_cols + inv_one * (scaled_one - unit_cols * mean_one)).astype(
         jnp.bfloat16
     )
-    bias_grad = jnp.sum(lin_grads.astype(jnp.float32), axis=0)
-
-    by_cols = jnp.concatenate(
+
+    small = jnp.concatenate(
         [first_gain_grad[None], second_gain_grad[None], switch_vector_grad[None], router_grad.T],
         axis=0,
     )
-    small = lax.psum(jnp.concatenate([by_cols, bias_grad.reshape(3, -1)], axis=0), "ep")
-    spread = lax.all_gather(small[: 3 + expert_total], "tp", axis=1, tiled=True)
+    small_rows = small.shape[0]
+    small = jnp.concatenate([jnp.sum(lin_grads.astype(jnp.float32), axis=0), small.reshape(-1)])
+    small = jnp.pad(small, (0, 16 * 3 * lin_width - small.shape[0])).reshape(16, 3 * lin_width)
+    weight_grads = scatter_ep(
+        inner_rows(normed_one, lin_grads).astype(jnp.bfloat16), small.astype(jnp.bfloat16), 5
+    )
     share = model_dim // sources
-    spread = lax.dynamic_slice_in_dim(spread, ep * share, share, 1)
+    small = weight_grads[share:].reshape(-1)
+    weight_grads = weight_grads[:share]
     bias_width = HD // sources
     bias_sums = lax.dynamic_slice_in_dim(
-        small[3 + expert_total :].reshape(3, head_count, HD), ep * bias_width, bias_width, 2
-    )
+        small[: 3 * lin_width].reshape(3, head_count, HD), ep * bias_width, bias_width, 2
+    )
+    small = small[3 * lin_width : 3 * lin_width + small_rows * col_width]
+    spread = lax.all_gather(small.reshape(small_rows, col_width), "tp", axis=1, tiled=True)
+    spread = lax.dynamic_slice_in_dim(spread, ep * share, share, 1)
     return (
         layer_out,
         tokens_grad,

time: 998 us -> 842 us (0.84)
  matrix products: 187 us -> 103 us
  Pallas kernels: 472 us -> 541 us
  blocking collectives: 86.7 us -> 24.5 us
  waiting for transfers between devices: 79.4 us -> 21.2 us
  other arithmetic: 59.9 us -> 47.3 us
    all_gather x2 -> x0, waiting for transfers between devices: 75.1 us -> none  [the longest x1 75.1 us: dense_plan(): lax.all_gather(out_grad, 'ep', axis=0, tiled=True)]
    pallas_call x3 -> x2, Pallas kernels: 326 us -> 384 us  [the longest x1 224 us: experts(): pl.pallas_call(functools.partial(experts_kernel, expert_width, shared_wid...]
    dot_general x2 -> x0, matrix products: 46.7 us -> none  [the longest x1 26.7 us: dense_plan(): jnp.dot(both_grad, both_rows, preferred_element_type=jnp.float32)]
    dot_general x7 -> x5, matrix products: 56.1 us -> 12.1 us  [times_transpose(): lax.dot_general(left_side, right_side, (((1,), (1,)), ((), ())), preferre...]
    all_gather x2 -> x1, blocking collectives: 28.8 us -> 5.89 us  [dense_plan(): lax.all_gather(small.reshape(small_rows, col_width), 'tp', axis=1, tiled=...]
    psum x1 -> x0, blocking collectives: 22.4 us -> none  [dense_plan(): lax.psum(jnp.concatenate([by_cols, bias_grad.reshape(3, -1)], axis=0), 'ep')]
    psum x4 -> x3, blocking collectives: 35.5 us -> 18.6 us  [tp_total(): return lax.psum(value, 'tp')]
    ppermute x4, waiting for transfers between devices: 0.01 us -> 13.6 us  [passed_along(): lax.ppermute(value, axis, [(source, source + steps) for source in range(l...]
  transfers between devices with their start and end apart: 9 -> 8, of which waited for: 2 -> 2; matrix products, arithmetic and copies ran while one was open for 16% -> 22% of each run, Pallas kernels for 34% -> 34%
where the time goes in v2:
time: 842 us; the launch traced here: 833 us
  Pallas kernels  541 us (64%)
  matrix products  103 us (12%)
  local copies, waits for them, and re-layouts  56 us (7%)
  other arithmetic  47.3 us (6%)
  starting transfers between devices  25.3 us (3%)
  blocking collectives  24.5 us (3%)
  waiting for transfers between devices  21.2 us (3%)
  between operations  15.3 us (2%)
    pallas_call x1, Pallas kernels, experts(): pl.pallas_call(functools.partial(experts_kernel, expert_width, shared_wid...  224 us
    pallas_call x1, Pallas kernels, scatter_ep(): pl.pallas_call(scatter_ep_kernel, out_shape=jax.ShapeDtypeStruct((tall, c...  160 us
    pallas_call x1, Pallas kernels, gather_all(): pl.pallas_call(gather_all_kernel, out_shape=jax.ShapeDtypeStruct((8 * row...  74.5 us
    dot_general x6, matrix products, inner_rows(): lax.dot_general(left_side, right_side, (((0,), (0,)), ((), ())), preferre...  53.9 us
    pallas_call x2, Pallas kernels, gather_tp(): pl.pallas_call(gather_tp_kernel, out_shape=jax.ShapeDtypeStruct((rows, 4...  46.2 us
    pallas_call x2, Pallas kernels, scatter_tp(): pl.pallas_call(scatter_tp_kernel, out_shape=jax.ShapeDtypeStruct((rows, c...  36 us
    unnamed x134, local copies, waits for them, and re-layouts  27.2 us
    ppermute x4, starting transfers between devices, passed_along(): lax.ppermute(value, axis, [(source, source + steps) for source in range(l...  20.7 us
  transfers between devices with their start and end apart: 8, of which 2 were waited for; matrix products, arithmetic and copies ran while one was open for 22% of the time, Pallas kernels for 34%

profile of v2, /device:TPU:9, one launch (start us, length us, event | category | flops | bytes accessed | tf_op | source)
XLA Modules:
  0.0 832.9 jit_solution(14122635459563167121)
XLA Ops:
  7.3 18.3 %gather_tp.2 = bf16[512,2048]{1,0:T(8,128)(2,1)} custom-call(bf16[512,512]{1,0:T(8,128)(2,1)} %x_ref.2), custom_call_target="tpu_custom_call" | custom-call | tf_op jit(solution)/shard_map/gather_tp/pallas_call | solution.py:531
  27.7 4.6 fusion.24
  62.6 9.4 %convert_reduce_fusion = s32[512,8]{1,0:T(8,128)S(1)} fusion(s32[512,8]{1,0:T(8,128)S(1)} %copy.149, s32[512,8]{0,1:T(8,128)S(1)} %broadcast_select_fusion), kind=kLoop, calls=%fused_computation.5 | loop fusion | flops 6287360 | bytes 49152 | tf_op jit(solution)/shard_map/reduce_sum | solution.py:1677
  77.5 74.5 %gather_all.1.g_ref = bf16[4096,2048]{1,0:T(8,128)(2,1)} custom-call(bf16[512,512]{1,0:T(8,128)(2,1)} %x_ref.3), custom_call_target="tpu_custom_call" | custom-call | tf_op jit(solution)/shard_map/gather_all/pallas_call | solution.py:778
  154.7 3.4 fusion.67
  161.4 3.5 fusion.23
  166.2 16.6 %scatter_tp.2 = f32[512,512]{1,0:T(8,128)S(1)} custom-call(bf16[512,2048]{1,0:T(8,128)(2,1)S(1)} %convolution_convert_fusion.2.p_ref), custom_call_target="tpu_custom_call" | custom-call | tf_op jit(solution)/shard_map/scatter_tp/pallas_call | solution.py:581
  183.0 6.2 psum.21
  190.2 223.9 %experts.1 = (bf16[4096,2048]{1,0:T(8,128)(2,1)}, bf16[4096,640]{1,0:T(8,128)(2,1)}, bf16[4096,1280]{1,0:T(8,128)(2,1)}, bf16[4096,2048]{1,0:T(8,128)(2,1)}, f32[528,512]{1,0:T(8,128)}, /*index=5*/f32[512,128]{1,0:T(8,128)}) custom-call(bf16[512,512]{1,0:T(8,128)(2,1)} %multiply_convert_fusion.1.x_ref, bf16[4096,2048]{1,0:T(8,128)(2,1)} %gather_all.1.g_ref, ...), custom_call_target="tpu_custom_call" | custom-call | tf_op jit(solution)/shard_map/experts/pallas_call | solution.py:1618
  421.0 15.1 %fusion.2 = f32[528,2048]{1,0:T(8,128)S(1)} fusion(bf16[4096,2048]{1,0:T(8,128)(2,1)} %gather_all.1.g_ref, bf16[4096,640]{1,0:T(8,128)(2,1)} %get-tuple-element.30), kind=kOutput, calls=%fused_computation.14 | convolution fusion | flops 8858370048 | bytes 26345472 | tf_op jit(solution)/shard_map/dot_general | solution.py:50
  440.0 5.1 psum.22
  447.5 28.0 %gather_tp.3 = bf16[512,2048]{1,0:T(8,128)(2,1)} custom-call(bf16[512,512]{1,0:T(8,128)(2,1)} %fusion.56.x_ref), custom_call_target="tpu_custom_call" | custom-call | tf_op jit(solution)/shard_map/gather_tp/pallas_call | solution.py:531
  475.5 3.5 convolution_convert_fusion.3
  479.1 5.1 fusion.15
  485.2 9.8 %collective-permute-start.3 = (bf16[512,4,128]{2,0,1:T(8,128)(2,1)}, bf16[512,4,128]{2,0,1:T(8,128)(2,1)}, u32[]{:S(2)}, u32[]{:S(2)}) collective-permute-start(bf16[512,4,128]{2,0,1:T(8,128)(2,1)} %slice.260), channel_id=1, source_target_pairs={{4,0},{8,4},{12,8},{16,12},{20,16},{24,20},{28,24},{5,1},{9,5},{13... | collective-permute-start | bytes 1572872 | tf_op jit(solution)/shard_map/ppermute | solution.py:24
  497.7 13.8 %fusion.6 = f32[528,2048]{1,0:T(8,128)S(1)} fusion(bf16[4096,2048]{1,0:T(8,128)(2,1)} %get-tuple-element.29, bf16[4096,1280]{1,0:T(8,128)(2,1)} %get-tuple-element.28), kind=kOutput, calls=%fused_computation.18 | convolution fusion | flops 8858370048 | bytes 26345472 | tf_op jit(solution)/shard_map/dot_general | solution.py:50
  511.9 14.9 %fusion.4 = f32[528,2048]{1,0:T(8,128)S(1)} fusion(bf16[4096,2048]{1,0:T(8,128)(2,1)} %get-tuple-element.29, bf16[4096,1280]{1,0:T(8,128)(2,1)} %get-tuple-element.28), kind=kOutput, calls=%fused_computation.16 | convolution fusion | flops 8858370048 | bytes 26345472 | tf_op jit(solution)/shard_map/dot_general | solution.py:50
  530.8 4.5 all-to-all-start
  535.3 5.2 multiply_reduce_fusion
  540.5 5.8 multiply_convert_fusion
  546.3 7.5 reduce-scatter.4.cloned.1.call-done
  553.8 4.3 multiply_bitcast_fusion
  559.0 4.4 collective-permute-start.2
  563.4 3.7 slice_bitcast_fusion
  567.2 3.7 slice_bitcast_fusion.2
  574.4 3.4 fusion.18
  582.0 13.6 %collective-permute-done.2 = bf16[512,4,128]{2,0,1:T(8,128)(2,1)} collective-permute-done((bf16[512,4,128]{2,0,1:T(8,128)(2,1)}, bf16[512,4,128]{2,0,1:T(8,128)(2,1)}, u32[]{:S(2)}, u32[]{:S(2)}) %collective-permute-start.2) | collective-permute-done | bytes 524320 | tf_op jit(solution)/shard_map/ppermute | solution.py:24
  605.7 19.5 %scatter_tp.3 = f32[512,512]{1,0:T(8,128)S(1)} custom-call(bf16[512,2048]{1,0:T(8,128)(2,1)S(1)} %add_convert_fusion.p_ref), custom_call_target="tpu_custom_call" | custom-call | tf_op jit(solution)/shard_map/scatter_tp/pallas_call | solution.py:581
  626.1 6.5 convolution_convert_fusion.p_ref
  632.6 160.1 %scatter_ep.1 = f32[272,1536]{1,0:T(8,128)S(1)} custom-call(bf16[2048,1536]{1,0:T(8,128)(2,1)S(1)} %convolution_convert_fusion.p_ref, bf16[16,1536]{1,0:T(8,128)(2,1)S(1)} %convert_element_type.167.e_ref), custom_call_target="tpu_custom_call" | custom-call | tf_op jit(solution)/shard_map/scatter_ep/pallas_call | solution.py:1066
  792.8 7.3 psum.23
  800.1 5.9 all_gather.3
  (243 shorter events, 106.9 us)
Async XLA Ops:
  7.2 20.4 %copy-start.50 = (f32[2048]{0:T(1024)S(1)}, f32[2048]{0:T(1024)}, u32[]{:S(2)}) copy-start(f32[2048]{0:T(1024)} %param.23) | copy-start | bytes 24580
  7.2 20.4 %copy-start.54 = (f32[512]{0:T(512)S(1)}, f32[512]{0:T(512)}, u32[]{:S(2)}) copy-start(f32[512]{0:T(512)} %param.29) | copy-start | bytes 6148
  7.2 546.6 %reduce-scatter.4.cloned.1.call-start = ((), (), s32[]{:S(2)}) async-start(), calls=%async_computation.4 | async-start | bytes 20971520 | tf_op jit(solution)/shard_map/reduce_scatter | solution.py:1795
  27.6 15.6 %copy-start.43 = (f32[512]{0:T(512)}, f32[512]{0:T(512)S(1)}, u32[]{:S(2)}) copy-start(f32[512]{0:T(512)S(1)} %add_rsqrt_fusion.1) | copy-start | bytes 6148
  32.2 127.7 %collective-permute-start = (bf16[512,4,128]{0,2,1:T(8,128)(2,1)}, bf16[512,4,128]{0,2,1:T(8,128)(2,1)}, u32[]{:S(2)}, u32[]{:S(2)}) collective-permute-start(bf16[512,4,128]{0,2,1:T(8,128)(2,1)} %bitcast), channel_id=1, source_target_pairs={{0,4},{4,8},{8,12},{12,16},{16,20},{20,24},{24,28},{1,5},{5,9},{9,... | collective-permute-start | bytes 1572872 | tf_op jit(solution)/shard_map/ppermute | solution.py:24
  56.7 98.0 %collective-permute-start.1 = (bf16[512,4,128]{2,0,1:T(8,128)(2,1)S(1)}, bf16[512,4,128]{2,0,1:T(8,128)(2,1)}, u32[]{:S(2)}, u32[]{:S(2)}) collective-permute-start(bf16[512,4,128]{2,0,1:T(8,128)(2,1)S(1)} %pad_maximum_fusion.6), channel_id=1, source_target_pairs={{0,4},{4,8},{8,12},{12,16},{16,20},{20,24},{24,28},{1,5},{5,9},{9,... | collective-permute-start | bytes 1572872 | tf_op jit(solution)/shard_map/ppermute | solution.py:24
  77.5 76.5 %copy-start.41 = (bf16[2048,8]{0,1:T(8,128)(2,1)S(1)}, bf16[2048,8]{0,1:T(8,128)(2,1)}, u32[]{:S(2)}) copy-start(bf16[2048,8]{0,1:T(8,128)(2,1)} %param.32) | copy-start | bytes 98308
  77.5 77.2 %copy-start.21 = (bf16[512,4,64]{2,0,1:T(8,128)(2,1)S(1)}, bf16[512,4,64]{2,0,1:T(8,128)(2,1)}, u32[]{:S(2)}) copy-start(bf16[512,4,64]{2,0,1:T(8,128)(2,1)} %get-tuple-element.137) | copy-start | bytes 786436
  77.5 77.2 %copy-start.22 = (bf16[512,4,64]{2,0,1:T(8,128)(2,1)S(1)}, bf16[512,4,64]{2,0,1:T(8,128)(2,1)}, u32[]{:S(2)}) copy-start(bf16[512,4,64]{2,0,1:T(8,128)(2,1)} %get-tuple-element.138) | copy-start | bytes 786436
  77.5 77.2 %copy-start.26 = (bf16[512,4,64]{2,0,1:T(8,128)(2,1)S(1)}, bf16[512,4,64]{2,0,1:T(8,128)(2,1)}, u32[]{:S(2)}) copy-start(bf16[512,4,64]{2,0,1:T(8,128)(2,1)} %copy-done.25) | copy-start | bytes 786436
  77.5 77.2 %copy-start.29 = (bf16[512,4,64]{2,0,1:T(8,128)(2,1)S(1)}, bf16[512,4,64]{2,0,1:T(8,128)(2,1)}, u32[]{:S(2)}) copy-start(bf16[512,4,64]{2,0,1:T(8,128)(2,1)} %copy-done.28) | copy-start | bytes 786436
  164.8 17.9 %copy-start.57 = (bf16[4,128,512]{2,1,0:T(8,128)(2,1)}, bf16[4,128,512]{2,1,0:T(8,128)(2,1)S(1)}, u32[]{:S(2)}) copy-start(bf16[4,128,512]{2,1,0:T(8,128)(2,1)S(1)} %fusion.23) | copy-start | bytes 1572868
  164.9 17.9 %copy-start.7 = (bf16[512,512]{1,0:T(8,128)(2,1)S(1)}, bf16[512,512]{1,0:T(8,128)(2,1)}, u32[]{:S(2)}) copy-start(bf16[512,512]{1,0:T(8,128)(2,1)} %x_ref.2) | copy-start | bytes 1572868
  166.2 23.0 %copy-start.37 = (f32[512]{0:T(512)S(1)}, f32[512]{0:T(512)}, u32[]{:S(2)}) copy-start(f32[512]{0:T(512)} %dynamic_slice.24) | copy-start | bytes 6148
  189.2 255.9 %copy-start.39 = (f32[512,1]{0,1:T(1,128)}, f32[512,1]{0,1:T(1,128)S(1)}, u32[]{:S(2)}) copy-start(f32[512,1]{0,1:T(1,128)S(1)} %add_rsqrt_fusion) | copy-start | bytes 6148
  414.1 405.2 %reduce-scatter.8.cloned.1.call-start = ((), (), s32[]{:S(2)}) async-start(), calls=%async_computation.6 | async-start | bytes 2359296 | tf_op jit(solution)/shard_map/reduce_scatter | solution.py:1847
  415.0 210.1 %copy-start.45 = (f32[512]{0:T(512)}, f32[512]{0:T(512)S(1)}, u32[]{:S(2)}) copy-start(f32[512]{0:T(512)S(1)} %dynamic_slice.29) | copy-start | bytes 6148
  415.9 20.2 %copy-start.34 = (f32[512,128]{0,1:T(8,128)}, f32[512,128]{0,1:T(8,128)S(1)}, u32[]{:S(2)}) copy-start(f32[512,128]{0,1:T(8,128)S(1)} %copy.153) | copy-start | bytes 786436
  445.1 33.9 %copy-start.47 = (f32[512,1]{0,1:T(1,128)}, f32[512,1]{0,1:T(1,128)S(1)}, u32[]{:S(2)}) copy-start(f32[512,1]{0,1:T(1,128)S(1)} %broadcast_multiply_fusion.1) | copy-start | bytes 6148
  479.0 15.9 %copy-start.23 = (bf16[512,2048]{1,0:T(8,128)(2,1)S(1)}, bf16[512,2048]{1,0:T(8,128)(2,1)}, u32[]{:S(2)}) copy-start(bf16[512,2048]{1,0:T(8,128)(2,1)} %gather_tp.3) | copy-start | bytes 6291460
  479.0 15.9 %copy-start.58 = (bf16[4,128,512]{2,1,0:T(8,128)(2,1)S(1)}, bf16[4,128,512]{2,1,0:T(8,128)(2,1)}, u32[]{:S(2)}) copy-start(bf16[4,128,512]{2,1,0:T(8,128)(2,1)} %copy-done.57) | copy-start | bytes 1572868
  484.2 13.5 %copy-start.8 = (f32[1024,4,128]{2,0,1:T(8,128)}, f32[1024,4,128]{2,0,1:T(8,128)S(1)}, u32[]{:S(2)}) copy-start(f32[1024,4,128]{2,0,1:T(8,128)S(1)} %fusion.15) | copy-start | bytes 6291460
  485.2 93.6 %collective-permute-start.3 = (bf16[512,4,128]{2,0,1:T(8,128)(2,1)}, bf16[512,4,128]{2,0,1:T(8,128)(2,1)}, u32[]{:S(2)}, u32[]{:S(2)}) collective-permute-start(bf16[512,4,128]{2,0,1:T(8,128)(2,1)} %slice.260), channel_id=1, source_target_pairs={{4,0},{8,4},{12,8},{16,12},{20,16},{24,20},{28,24},{5,1},{9,5},{13... | collective-permute-start | bytes 1572872 | tf_op jit(solution)/shard_map/ppermute | solution.py:24
  511.5 15.3 %copy-start.17 = (f32[528,2048]{1,0:T(8,128)}, f32[528,2048]{1,0:T(8,128)S(1)}, u32[]{:S(2)}) copy-start(f32[528,2048]{1,0:T(8,128)S(1)} %fusion.6) | copy-start | bytes 12976132
  530.8 278.3 %all-to-all-start = ((bf16[8,3,176,256]{3,2,1,0:T(8,128)(2,1)}), bf16[8,3,176,256]{3,2,1,0:T(8,128)(2,1)}, u32[]{:S(2)}, u32[]{:S(2)}) async-start(bf16[8,3,176,256]{3,2,1,0:T(8,128)(2,1)} %maximum_bitcast_fusion), calls=%async_computation.3 | async-start | bytes 4325376 | tf_op jit(solution)/shard_map/all_to_all | solution.py:1815
  535.3 287.9 %reduce-scatter.6.cloned.1.call-start = ((), (), s32[]{:S(2)}) async-start(), calls=%async_computation.5 | async-start | bytes 4718592 | tf_op jit(solution)/shard_map/reduce_scatter | solution.py:1794
  559.0 36.6 %collective-permute-start.2 = (bf16[512,4,128]{2,0,1:T(8,128)(2,1)}, bf16[512,4,128]{2,0,1:T(8,128)(2,1)}, u32[]{:S(2)}, u32[]{:S(2)}) collective-permute-start(bf16[512,4,128]{2,0,1:T(8,128)(2,1)} %slice.261), channel_id=1, source_target_pairs={{4,0},{8,4},{12,8},{16,12},{20,16},{24,20},{28,24},{5,1},{9,5},{13... | collective-permute-start | bytes 1572872 | tf_op jit(solution)/shard_map/ppermute | solution.py:24
  582.0 22.0 %copy-start.10 = (bf16[512,4,128]{0,2,1:T(8,128)(2,1)}, bf16[512,4,128]{0,2,1:T(8,128)(2,1)S(1)}, u32[]{:S(2)}) copy-start(bf16[512,4,128]{0,2,1:T(8,128)(2,1)S(1)} %copy.167) | copy-start | bytes 1572868
  582.0 14.8 %copy-start.14 = (f32[512,4,128]{2,0,1:T(8,128)S(1)}, f32[512,4,128]{2,0,1:T(8,128)}, u32[]{:S(2)}) copy-start(f32[512,4,128]{2,0,1:T(8,128)} %fusion.18) | copy-start | bytes 3145732
  605.7 19.5 %copy-start.44 = (f32[512]{0:T(512)S(1)}, f32[512]{0:T(512)}, u32[]{:S(2)}) copy-start(f32[512]{0:T(512)} %copy-done.43) | copy-start | bytes 6148
  605.7 20.0 %copy-start.11 = (bf16[512,4,128]{0,2,1:T(8,128)(2,1)S(1)}, bf16[512,4,128]{0,2,1:T(8,128)(2,1)}, u32[]{:S(2)}) copy-start(bf16[512,4,128]{0,2,1:T(8,128)(2,1)} %copy-done.10) | copy-start | bytes 1572868
  605.7 20.4 %copy-start.51 = (f32[2048]{0:T(1024)S(1)}, f32[2048]{0:T(1024)}, u32[]{:S(2)}) copy-start(f32[2048]{0:T(1024)} %param.23) | copy-start | bytes 24580
  (37 other events, 209.3 us)
Sparse Core Ops, SparseCore 0:
  414.2 139.5 reduce-scatter.3
  557.7 88.0 reduce-scatter.7
  649.9 130.6 reduce-scatter.5

commit v3 on v2

--- a/solution.py
+++ b/solution.py
@@ -488,14 +488,14 @@
 
 
 def add_blocks(target, sources, rows):
-    step = next(size for size in (64, 48, 16) if rows % size == 0)
+    step = next(size for size in (80, 64, 48, 16) if rows % size == 0)
 
     def body(i, carry):
         span = pl.ds(pl.multiple_of(i * step, 16), step)
-        total = target[span, :].astype(jnp.float32)
+        total = target[span, :]
         for source in sources:
-            total = total + source[span, :].astype(jnp.float32)
-        target[span, :] = total.astype(target.dtype)
+            total = total + source[span, :].astype(target.dtype)
+        target[span, :] = total
         return carry
 
     lax.fori_loop(0, rows // step, body, 0)
@@ -1090,12 +1090,17 @@
     shared_up_ref,
     expert_down_ref,
     shared_down_ref,
+    grad_ref,
+    ffn_ref,
+    logit_ref,
+    expert_grads_ref,
+    shared_grads_ref,
     all_ref,
-    hidden_ref,
-    both_ref,
-    out_ref,
-    grad_ref,
-    logit_ref,
+    from_sib,
+    from_b,
+    from_a,
+    from_below,
+    from_above,
     in_ref,
     down_ref,
     scalars,
@@ -1104,17 +1109,16 @@
     g_held,
     lin,
     hidden_grad,
-    hidden_held,
-    both_held,
-    out_held,
+    hidden_all,
+    both_all,
     kept_cols,
     staged,
     mine,
-    from_sib,
-    from_b,
-    from_a,
-    from_below,
-    from_above,
+    landed,
+    x_tile,
+    g_tile,
+    tile_out,
+    shared_out,
     up_sem,
     down_sem,
     a_sem,
@@ -1124,6 +1128,7 @@
     sib_sem,
     own_sem,
     load_sem,
+    fetch_sem,
     store_sem,
     weight_sem,
     kept_send,
@@ -1142,11 +1147,14 @@
     ep, tp, z, y, x, core = place()
     rows, cols = x_ref.shape
     width = down_ref.shape[0]
+    filled = expert_width + shared_width
+    tall = mine.shape[1]
+    out_at = rows + 16
+    cuts = ((0, out_at), (out_at, tall - out_at))
     peer_a, peer_b, sibling, above, below = lane_peers()
     sources = kept_held.shape[0]
     others = [(lax.rem(ep + i, sources), tp) for i in range(1, sources)]
-    x_peer = (ep, tp + 2 - 4 * x)
-    greet([x_peer, sibling] + others)
+    greet([(ep, tp + 2 - 4 * x), sibling] + others)
 
     def spot(z_at, da, db):
         group, quarter = lane_spot(z_at, da, db, core)
@@ -1158,13 +1166,13 @@
     def at(z_at, da, db):
         return z_at * 4 + da * 2 + db
 
-    turns = (
-        z,
-        1 + lax.rem(z, 2),
-        jnp.where(z == 0, 2, jnp.where(z == 1, 0, jnp.where(z == 2, 3, 1))),
-        3 * (1 - z // 2),
-    )
-    edge = (z == 0) | (z == 3)
+    def choose(*values):
+        return jnp.where(
+            z == 0, values[0], jnp.where(z == 1, values[1], jnp.where(z == 2, values[2], values[3]))
+        )
+
+    coming = (z, choose(1, 0, 3, 2), choose(2, 2, 1, 1), choose(3, 3, 0, 0))
+    turns = (z, choose(2, 0, 3, 1), choose(3, 3, 0, 0), choose(1, 2, 1, 2))
 
     def arrived(z_at, da, db):
         block, n = spot(z_at, da, db), at(z_at, da, db)
@@ -1189,8 +1197,7 @@
         n = at(z_at, da, db)
         return remote(source, spot(z_at, da, db), s_sem.at[n], sib_sem.at[n], sibling)
 
-    def pass_z(k):
-        z_at = turns[k]
+    def pass_z(z_at):
         block = arrived(z_at, 0, 0)
 
         @pl.when((z_at > z) & (z > 0))
@@ -1205,14 +1212,14 @@
         over_b(z_at, 0, block).start()
         to_sibling(z_at, 0, 0, block).start()
 
-    def pass_a(k):
-        block = arrived(turns[k], 1, 0)
-        over_b(turns[k], 1, block).start()
-        to_sibling(turns[k], 1, 0, block).start()
-
-    def pass_b(k, da):
-        block = arrived(turns[k], da, 1)
-        to_sibling(turns[k], da, 1, block).start()
+    def pass_a(z_at):
+        block = arrived(z_at, 1, 0)
+        over_b(z_at, 1, block).start()
+        to_sibling(z_at, 1, 0, block).start()
+
+    def pass_b(z_at, da):
+        block = arrived(z_at, da, 1)
+        to_sibling(z_at, da, 1, block).start()
 
     def sibling_blocks(k, dy):
         for dx in range(2):
@@ -1227,34 +1234,26 @@
 
     def load_x(k, dy):
         _, span = group_rows(k, dy)
-        return pltpu.make_async_copy(all_ref.at[span, :], x_held.at[dy], load_sem.at[dy])
+        return pltpu.make_async_copy(all_ref.at[span, :], x_held, load_sem.at[0])
 
     def load_g(k, dy):
         _, span = group_rows(k, dy)
-        return pltpu.make_async_copy(g_ref.at[span, :], g_held.at[dy], load_sem.at[2 + dy])
-
-    def project(k, dy):
+        return pltpu.make_async_copy(g_ref.at[span, :], g_held, load_sem.at[1])
+
+    def project():
         def body(i, carry):
             cut = pl.ds(pl.multiple_of(i * width, width), width)
-            lin[:, cut] = times_transpose(x_held[dy], in_ref[cut, :])
+            lin[:, cut] = times_transpose(x_held[...], in_ref[cut, :])
             return carry
 
         lax.fori_loop(0, 2, body, 0)
 
-    def project_grad(k, dy):
-        hidden_grad[...] = times_transpose(g_held[dy], down_ref[...])
-
-    def stores(k, dy):
-        _, span = group_rows(k, dy)
-        return (
-            pltpu.make_async_copy(hidden_held.at[dy], hidden_ref.at[span, :], store_sem.at[dy]),
-            pltpu.make_async_copy(both_held.at[dy], both_ref.at[span, :], store_sem.at[2 + dy]),
-            pltpu.make_async_copy(out_held.at[dy], out_ref.at[span, :], store_sem.at[4 + dy]),
-        )
+    def project_grad():
+        hidden_grad[...] = times_transpose(g_held[...], down_ref[...])
 
     step = 64
     tile_start = width - 128
-    logit_at = expert_width + shared_width - tile_start
+    logit_at = filled - tile_start
 
     def activate(k, dy):
         group, _ = group_rows(k, dy)
@@ -1265,6 +1264,7 @@
 
         def body(i, carry):
             span = pl.ds(pl.multiple_of(i * step, step), step)
+            whole = pl.ds(pl.multiple_of(group * rows + i * step, step), step)
             gate_lin, up_lin = lin[span, :width], lin[span, width:]
             grad = hidden_grad[span, :]
             tail = lin[span, tile_start:width]
@@ -1290,11 +1290,11 @@
                 jnp.where(lane < expert_width, 0.0, agreement), axis=1, keepdims=True
             )
             scaled = grad * scale
-            hidden_held[dy, span, :] = (hidden * scale).astype(jnp.bfloat16)
-            both_held[dy, span, :width] = (
+            hidden_all[whole, :] = (hidden * scale).astype(jnp.bfloat16)
+            both_all[whole, :width] = (
                 scaled * up_lin * sig * (1.0 + gate_lin * (1.0 - sig))
             ).astype(jnp.bfloat16)
-            both_held[dy, span, width:] = (scaled * act).astype(jnp.bfloat16)
+            both_all[whole, width:] = (scaled * act).astype(jnp.bfloat16)
             scalars[span, :] = jnp.where(
                 near == ep, gate_part, jnp.where(near == expert_total, switch_part, 0.0)
             )
@@ -1302,45 +1302,38 @@
 
         lax.fori_loop(0, rows // step, body, 0)
 
-    def out_rows(k, dy):
-        def body(i, carry):
-            cut = pl.ds(pl.multiple_of(i * cols, cols), cols)
-            out_held[dy, :, cut] = jnp.dot(
-                hidden_held[dy], down_ref[:, cut], preferred_element_type=jnp.float32
+    def hold(k, da, db):
+        slot = 2 if k == 0 else k % 2
+        return db * (7 + slot * 2 + da) + (1 - db) * (da * (4 + slot) + (1 - da) * k)
+
+    def lane_offsets(dx, dy, core_at):
+        return (1 - core_at) * dy + core_at * dx, (1 - core_at) * dx + core_at * dy
+
+    def rs_sibling(k, dx, dy):
+        n = at(turns[k], *lane_offsets(dx, dy, 1 - core))
+        return remote(staged.at[dx], from_sib.at[n], rs_send.at[n], rs_recv.at[n], sibling)
+
+    def block_rows(k, dy):
+        sums = scalars[...].T[:16, :].astype(jnp.bfloat16)
+        _, span = group_rows(k, dy)
+
+        def fill(target, cut):
+            target[:rows, :] = jnp.dot(
+                both_all[span, :], in_ref[:, cut], preferred_element_type=jnp.float32
             ).astype(jnp.bfloat16)
-            return carry
-
-        lax.fori_loop(0, 4, body, 0)
-
-    tall = mine.shape[1]
-
-    def lane_at(k, dx, dy, core_at):
-        da, db = (1 - core_at) * dy + core_at * dx, (1 - core_at) * dx + core_at * dy
-        return at(turns[k], da, db)
-
-    def rs_sibling(k, dx, dy):
-        n = lane_at(k, dx, dy, 1 - core)
-        return remote(
-            staged.at[dy * 2 + dx], from_sib.at[n], rs_send.at[n], rs_recv.at[n], sibling
-        )
-
-    def grad_rows(k, dy):
-        sums = scalars[...].T[:16, :].astype(jnp.bfloat16)
+            target[rows:out_at, :] = sums
+            target[out_at:, :] = jnp.dot(
+                hidden_all[span, :], down_ref[:, cut], preferred_element_type=jnp.float32
+            ).astype(jnp.bfloat16)
 
         def body(dx, carry):
             x_at = x + (1 - 2 * x) * dx
-            theirs = pl.ds(pl.multiple_of((x_at * 2 + 1 - core) * cols, cols), cols)
-            ours = pl.ds(pl.multiple_of((x_at * 2 + core) * cols, cols), cols)
-            staged[dy * 2 + dx, :rows, :] = jnp.dot(
-                both_held[dy], in_ref[:, theirs], preferred_element_type=jnp.float32
-            ).astype(jnp.bfloat16)
-            staged[dy * 2 + dx, rows:, :] = sums
+            fill(staged.at[dx], pl.ds(pl.multiple_of((x_at * 2 + 1 - core) * cols, cols), cols))
             rs_sibling(k, dx, dy).start()
-            ours_at = lane_at(k, dx, dy, core)
-            mine[ours_at, :rows, :] = jnp.dot(
-                both_held[dy], in_ref[:, ours], preferred_element_type=jnp.float32
-            ).astype(jnp.bfloat16)
-            mine[ours_at, rows:, :] = sums
+            fill(
+                mine.at[hold(k, *lane_offsets(dx, dy, core))],
+                pl.ds(pl.multiple_of((x_at * 2 + core) * cols, cols), cols),
+            )
             return carry
 
         lax.fori_loop(0, 2, body, 0)
@@ -1351,31 +1344,47 @@
 
     def rs_over_b(k, da):
         n = turns[k] * 2 + da
-        return remote(
-            mine.at[at(turns[k], da, 1)], from_b.at[n], rb_send.at[n], rb_recv.at[n], peer_b
-        )
+        return remote(mine.at[hold(k, da, 1)], from_b.at[n], rb_send.at[n], rb_recv.at[n], peer_b)
 
     def rs_over_a(k):
         z_at = turns[k]
         return remote(
-            mine.at[at(z_at, 1, 0)], from_a.at[z_at], ra_send.at[z_at], ra_recv.at[z_at], peer_a
+            mine.at[hold(k, 1, 0)], from_a.at[z_at], ra_send.at[z_at], ra_recv.at[z_at], peer_a
         )
 
-    def rs_up(z_at):
+    def rs_up(k, z_at, half):
+        first, count = cuts[half]
+        n = z_at * 2 + half
+        span = pl.ds(first, count)
         return remote(
-            mine.at[at(z_at, 0, 0)], from_below.at[z_at], ru_send.at[z_at], ru_recv.at[z_at], above
+            mine.at[k, span], from_below.at[z_at, span], ru_send.at[n], ru_recv.at[n], above
         )
 
-    def rs_down(z_at):
+    def rs_down(k, z_at, half):
+        first, count = cuts[half]
+        n = z_at * 2 + half
+        span = pl.ds(first, count)
         return remote(
-            mine.at[at(z_at, 0, 0)], from_above.at[z_at], rd_send.at[z_at], rd_recv.at[z_at], below
+            mine.at[k, span], from_above.at[z_at, span], rd_send.at[n], rd_recv.at[n], below
         )
 
+    def fetch(source, i):
+        return pltpu.make_async_copy(source, landed.at[i], fetch_sem.at[i])
+
+    def fetch_part(source, half, i):
+        span = pl.ds(*cuts[half])
+        return pltpu.make_async_copy(source.at[span], landed.at[i, span], fetch_sem.at[i])
+
     def reduce_sibling(k, dy):
+        spots = []
         for dx in range(2):
-            n = lane_at(k, dx, dy, core)
+            n = at(turns[k], *lane_offsets(dx, dy, core))
             remote(staged.at[0], from_sib.at[n], rs_send.at[n], rs_recv.at[n], sibling).wait_recv()
-            add_blocks(mine.at[n], [from_sib.at[n]], tall)
+            fetch(from_sib.at[n], dx).start()
+            spots.append(n)
+        for dx in range(2):
+            fetch(from_sib.at[spots[dx]], dx).wait()
+            add_blocks(mine.at[hold(k, *lane_offsets(dx, dy, core))], [landed.at[dx]], tall)
 
         @pl.when(core == 0)
         def _():
@@ -1390,36 +1399,88 @@
 
     def reduce_b(k):
         rs_over_b(k, 1).wait_recv()
-        add_blocks(mine.at[at(turns[k], 1, 0)], [from_b.at[turns[k] * 2 + 1]], tall)
+        source = from_b.at[turns[k] * 2 + 1]
+        fetch(source, 0).start()
+        fetch(source, 0).wait()
+        add_blocks(mine.at[hold(k, 1, 0)], [landed.at[0]], tall)
         rs_over_a(k).start()
 
     def reduce_a(k):
         z_at = turns[k]
         rs_over_b(k, 0).wait_recv()
+        fetch(from_b.at[z_at * 2], 0).start()
         rs_over_a(k).wait_recv()
-        add_blocks(mine.at[at(z_at, 0, 0)], [from_b.at[z_at * 2], from_a.at[z_at]], tall)
+        fetch(from_a.at[z_at], 1).start()
+        fetch(from_b.at[z_at * 2], 0).wait()
+        fetch(from_a.at[z_at], 1).wait()
+        add_blocks(mine.at[k], [landed.at[0], landed.at[1]], tall)
         if k > 0:
-
-            @pl.when(z == 0)
-            def _():
-                rs_up(z_at).start()
-
-            @pl.when(z == 3)
-            def _():
-                rs_down(z_at).start()
-
-    def chain(z_at):
-        @pl.when(z_at > z)
+            for half in range(2):
+
+                @pl.when(z == 0)
+                def _(half=half):
+                    rs_up(k, z_at, half).start()
+
+                @pl.when(z == 3)
+                def _(half=half):
+                    rs_down(k, z_at, half).start()
+
+    def chain(k):
+        z_at = turns[k]
+        first, count = cuts[0]
+        for half, (first, count) in enumerate(cuts):
+            span = pl.ds(first, count)
+
+            @pl.when((z > 0) & (z < 3) & (z_at > z))
+            def _(half=half, span=span, count=count):
+                rs_up(k, z_at, half).wait_recv()
+                fetch_part(from_below.at[z_at], half, half).start()
+                fetch_part(from_below.at[z_at], half, half).wait()
+                add_blocks(mine.at[k, span], [landed.at[half, span]], count)
+                rs_up(k, z_at, half).start()
+
+            @pl.when((z > 0) & (z < 3) & (z_at < z))
+            def _(half=half, span=span, count=count):
+                rs_down(k, z_at, half).wait_recv()
+                fetch_part(from_above.at[z_at], half, half).start()
+                fetch_part(from_above.at[z_at], half, half).wait()
+                add_blocks(mine.at[k, span], [landed.at[half, span]], count)
+                rs_down(k, z_at, half).start()
+
+    tile = x_tile.shape[1]
+
+    def load_tile(source, target, t, sem):
+        cut = pl.ds(pl.multiple_of(t * tile, tile), tile)
+        return pltpu.make_async_copy(source.at[:, cut], target, load_sem.at[sem])
+
+    def tile_stores(t, kind):
+        cut = pl.ds(pl.multiple_of(t * tile, tile), tile)
+        return (
+            pltpu.make_async_copy(
+                tile_out.at[kind, pl.ds(0, expert_width)],
+                expert_grads_ref.at[kind, :, cut],
+                store_sem.at[kind],
+            ),
+            pltpu.make_async_copy(
+                shared_out.at[kind], shared_grads_ref.at[t, kind], store_sem.at[3 + kind]
+            ),
+        )
+
+    def weight_tile(t, kind):
+        @pl.when(t > 0)
         def _():
-            rs_up(z_at).wait_recv()
-            add_blocks(mine.at[at(z_at, 0, 0)], [from_below.at[z_at]], tall)
-            rs_up(z_at).start()
-
-        @pl.when(z_at < z)
-        def _():
-            rs_down(z_at).wait_recv()
-            add_blocks(mine.at[at(z_at, 0, 0)], [from_above.at[z_at]], tall)
-            rs_down(z_at).start()
+            for copy in tile_stores(t - 1, kind):
+                copy.wait()
+
+        if kind == 0:
+            left, right = hidden_all[:, :filled], g_tile[...]
+        else:
+            left, right = both_all[:, (kind - 1) * width : (kind - 1) * width + filled], x_tile[...]
+        result = inner_rows(left, right)
+        tile_out[kind] = result
+        shared_out[kind] = result[expert_width:, :].astype(jnp.bfloat16)
+        for copy in tile_stores(t, kind):
+            copy.start()
 
     own = pltpu.make_async_copy(x_ref, spot(z, 0, 0), own_sem)
     over_b(z, 0, x_ref).start()
@@ -1447,27 +1508,24 @@
     own_kept = pltpu.make_async_copy(kept_ref, kept_held.at[ep], weight_sem.at[7])
     own_kept.start()
     pieces = [
+        (expert_down_ref, down_ref, 0),
+        (
+            shared_down_ref.at[pl.ds(pl.multiple_of(ep * shared_width, 16), shared_width), :],
+            down_ref,
+            expert_width,
+        ),
         (expert_gate_ref, in_ref, 0),
         (shared_gate_ref, in_ref, expert_width),
-        (extra_ref, in_ref, expert_width + shared_width),
+        (extra_ref, in_ref, filled),
         (expert_up_ref, in_ref, width),
         (shared_up_ref, in_ref, width + expert_width),
-        (expert_down_ref, down_ref, 0),
     ]
     weight_copies = [
         pltpu.make_async_copy(piece, target.at[pl.ds(at_row, piece.shape[0]), :], weight_sem.at[i])
         for i, (piece, target, at_row) in enumerate(pieces)
     ]
-    weight_copies.append(
-        pltpu.make_async_copy(
-            shared_down_ref.at[pl.ds(pl.multiple_of(ep * shared_width, 16), shared_width), :],
-            down_ref.at[pl.ds(expert_width, shared_width), :],
-            weight_sem.at[6],
-        )
-    )
     for copy in weight_copies:
         copy.start()
-    filled = expert_width + shared_width
     for target, first, last_row in (
         (in_ref, filled + 16, width),
         (in_ref, width + filled, 2 * width),
@@ -1476,109 +1534,155 @@
         target[first:last_row, :] = jnp.zeros((last_row - first, target.shape[1]), target.dtype)
     for copy in weight_copies:
         copy.wait()
+    load_g(0, 0).wait()
+    project_grad()
     own_kept.wait()
     for i in range(1, sources):
         kept_to(i).wait_recv()
     own.wait()
 
     def ready(k, dy):
-        if dy == 0:
-            pass_a(k)
-            pass_b(k, 0)
-        else:
-            pass_b(k, 1)
+        if k > 0:
+            pass_b(turns[k], dy)
         sibling_blocks(k, dy)
         load_x(k, dy).start()
 
-    order = [(k, dy) for k in range(4) for dy in range(2)]
+    order = [(0, 0)] + [(k, dy) for k in range(1, 4) for dy in range(2)] + [(0, 1)]
+    pass_a(z)
+    pass_b(z, 0)
     ready(0, 0)
     for s, (k, dy) in enumerate(order):
         following = order[s + 1] if s < 7 else None
         load_x(k, dy).wait()
-        load_g(k, dy).wait()
+        project()
+        if s == 0:
+            pass_z(coming[1])
+        if s >= 1:
+            load_g(k, dy).wait()
+            project_grad()
         if following is not None:
             load_g(*following).start()
-        project(k, dy)
         if s == 0:
-            pass_z(1)
+            pass_z(coming[2])
+            pass_b(z, 1)
+            pass_a(coming[1])
+        if s == 1:
+            pass_z(coming[3])
         if s >= 1:
             reduce_sibling(*order[s - 1])
-        project_grad(k, dy)
+        if s in (4, 6):
+            reduce_b(s // 2 - 1)
+        activate(k, dy)
         if s == 0:
-            pass_z(2)
-        if s == 1:
-            pass_z(3)
-        if dy == 1 and k >= 1:
-            reduce_b(k - 1)
-        if s >= 2:
-            for copy in stores(*order[s - 2]):
-                copy.wait()
-        activate(k, dy)
+            pass_a(coming[2])
+        if s == 2:
+            pass_a(coming[3])
         if following is not None:
             ready(*following)
-        if dy == 0 and k >= 2:
-            reduce_a(k - 2)
-        if s >= 2:
-            staged_free(*order[s - 2])
-        grad_rows(k, dy)
-        out_rows(k, dy)
-        for copy in stores(k, dy):
-            copy.start()
-    reduce_sibling(3, 1)
-    reduce_a(2)
-    reduce_b(3)
-    for s in (6, 7):
-        for copy in stores(*order[s]):
+        if s in (5, 7):
+            reduce_a((s - 3) // 2)
+        if s >= 1:
+            staged_free(*order[s - 1])
+        if s == 5:
+            for da in range(2):
+                rs_over_b(1, da).wait_send()
+            rs_over_a(1).wait_send()
+        block_rows(k, dy)
+
+    load_tile(g_ref, g_tile, 0, 2).start()
+    load_tile(all_ref, x_tile, 0, 3).start()
+    tiles = shared_grads_ref.shape[0]
+    services = {
+        (0, 1): lambda: reduce_sibling(0, 1),
+        (0, 2): lambda: chain(2),
+        (1, 1): lambda: reduce_b(3),
+        (1, 2): lambda: reduce_b(0),
+        (2, 0): lambda: chain(1),
+        (3, 0): lambda: reduce_a(3),
+        (4, 0): lambda: chain(3),
+        (5, 1): lambda: reduce_a(0),
+    }
+
+    def tile_step(t, carry):
+        for kind in range(3):
+            if kind == 0:
+                load_tile(g_ref, g_tile, t, 2).wait()
+            if kind == 1:
+                load_tile(all_ref, x_tile, t, 3).wait()
+            weight_tile(t, kind)
+
+            @pl.when(t + 1 < tiles)
+            def _(kind=kind):
+                if kind == 0:
+                    load_tile(g_ref, g_tile, t + 1, 2).start()
+                if kind == 2:
+                    load_tile(all_ref, x_tile, t + 1, 3).start()
+
+            for (at_tile, at_kind), service in services.items():
+                if at_kind == kind:
+                    pl.when(t == at_tile)(service)
+        return carry
+
+    lax.fori_loop(0, tiles, tile_step, 0)
+    for kind in range(3):
+        for copy in tile_stores(tiles - 1, kind):
             copy.wait()
-    reduce_a(3)
-
-    @pl.when(z == 1)
-    def _():
-        for z_at in (2, 3, 0):
-            chain(z_at)
-
-    @pl.when(z == 2)
-    def _():
-        for z_at in (1, 0, 3):
-            chain(z_at)
-
-    last = mine.at[at(z, 0, 0)]
-
-    @pl.when(z > 0)
-    def _():
-        rs_up(z).wait_recv()
-
-    @pl.when(z < 3)
-    def _():
-        rs_down(z).wait_recv()
-
-    grad_ref[...] = jnp.zeros_like(grad_ref)
+
+    for half in range(2):
+
+        @pl.when(z > 0)
+        def _(half=half):
+            rs_up(0, z, half).wait_recv()
+            fetch_part(from_below.at[z], half, 0).start()
+            fetch_part(from_below.at[z], half, 0).wait()
+
+        @pl.when(z < 3)
+        def _(half=half):
+            rs_down(0, z, half).wait_recv()
+            fetch_part(from_above.at[z], half, 1).start()
+            fetch_part(from_above.at[z], half, 1).wait()
+
+    def total(parts):
+        def body(i, carry):
+            for target, first in ((grad_ref, 0), (ffn_ref, out_at)):
+                span = pl.ds(pl.multiple_of(i * 16, 16), 16)
+                source = pl.ds(pl.multiple_of(first + i * 16, 16), 16)
+                value = mine[0, source, :].astype(jnp.float32)
+                for part in parts:
+                    value = value + landed[part, source, :].astype(jnp.float32)
+                target[span, :] = value
+            return carry
+
+        lax.fori_loop(0, rows // 16, body, 0)
+        value = mine[0, rows:out_at, :].astype(jnp.float32)
+        for part in parts:
+            value = value + landed[part, rows:out_at, :].astype(jnp.float32)
+        grad_ref[rows:, :] = value
 
     @pl.when(z == 0)
     def _():
-        add_blocks(grad_ref, [last, from_above.at[0]], tall)
+        total([1])
 
     @pl.when(z == 3)
     def _():
-        add_blocks(grad_ref, [last, from_below.at[3]], tall)
+        total([0])
 
     @pl.when((z > 0) & (z < 3))
     def _():
-        add_blocks(grad_ref, [last, from_below.at[z], from_above.at[z]], tall)
+        total([0, 1])
 
     for i in range(1, sources):
         kept_to(i).wait_send()
-    staged_free(3, 0)
-    staged_free(3, 1)
+    staged_free(0, 1)
+    for k in (0, 2, 3):
+        rs_over_a(k).wait_send()
+        for da in range(2):
+            rs_over_b(k, da).wait_send()
 
     def finish(i, carry):
         over_a(i, x_ref).wait_send()
         over_b(i, 0, x_ref).wait_send()
         over_b(i, 1, x_ref).wait_send()
-        remote(mine.at[0], from_a.at[0], ra_send.at[i], ra_recv.at[i], peer_a).wait_send()
-        for da in range(2):
-            n = i * 2 + da
-            remote(mine.at[0], from_b.at[0], rb_send.at[n], rb_recv.at[n], peer_b).wait_send()
         for n in range(4):
             block = spot(0, 0, 0)
             remote(block, block, s_sem.at[i * 4 + n], sib_sem.at[i * 4 + n], sibling).wait_send()
@@ -1591,13 +1695,15 @@
         def _():
             down(i, x_ref).wait_send()
 
-        @pl.when(i > z)
-        def _():
-            rs_up(i).wait_send()
-
-        @pl.when(i < z)
-        def _():
-            rs_down(i).wait_send()
+        for half in range(2):
+
+            @pl.when(i > z)
+            def _(half=half):
+                rs_up(0, i, half).wait_send()
+
+            @pl.when(i < z)
+            def _(half=half):
+                rs_down(0, i, half).wait_send()
 
         return carry
 
@@ -1607,56 +1713,596 @@
 def experts(x_cols, grads_all, kept_rows, weights, expert_total, cid):
     rows, cols = x_cols.shape
     total, model_dim = grads_all.shape
+    sources = total // rows
     expert_width, shared_width = weights[0].shape[0], weights[1].shape[0]
-    width = -(-(expert_width + shared_width + expert_total + 1) // 128) * 128
+    filled = expert_width + shared_width
+    width = -(-(filled + expert_total + 1) // 128) * 128
+    tall = 2 * rows + 16
+    tile = model_dim // sources
     low, dma = jnp.bfloat16, pltpu.SemaphoreType.DMA
     vmem, hbm = pl.BlockSpec(memory_space=pltpu.VMEM), pl.BlockSpec(memory_space=pl.ANY)
 
-    def held(count):
-        return pltpu.VMEM((count, rows + 16, cols), low)
+    def landing(count):
+        return jax.ShapeDtypeStruct((count, tall, cols), low)
 
     return pl.pallas_call(
         functools.partial(experts_kernel, expert_width, shared_width, expert_total),
         out_shape=[
+            jax.ShapeDtypeStruct((rows + 16, cols), jnp.float32),
+            jax.ShapeDtypeStruct((rows, cols), jnp.float32),
+            jax.ShapeDtypeStruct((rows, 128), jnp.float32),
+            jax.ShapeDtypeStruct((3, expert_width, model_dim), jnp.float32),
+            jax.ShapeDtypeStruct((sources, 3, shared_width, tile), low),
             jax.ShapeDtypeStruct((total, model_dim), low),
-            jax.ShapeDtypeStruct((total, width), low),
-            jax.ShapeDtypeStruct((total, 2 * width), low),
-            jax.ShapeDtypeStruct((total, model_dim), low),
-            jax.ShapeDtypeStruct((rows + 16, cols), jnp.float32),
-            jax.ShapeDtypeStruct((rows, 128), jnp.float32),
+            landing(16),
+            landing(8),
+            landing(4),
+            landing(4),
+            landing(4),
         ],
         in_specs=[hbm] * 10,
-        out_specs=[hbm, hbm, hbm, hbm, vmem, vmem],
+        out_specs=[vmem, vmem, vmem] + [hbm] * 8,
         scratch_shapes=[
             pltpu.VMEM((2 * width, model_dim), low),
             pltpu.VMEM((width, model_dim), low),
             pltpu.VMEM((rows, 128), jnp.float32),
-            pltpu.VMEM((total // rows, 16, rows), low),
-            pltpu.VMEM((2, rows, model_dim), low),
-            pltpu.VMEM((2, rows, model_dim), low),
+            pltpu.VMEM((sources, 16, rows), low),
+            pltpu.VMEM((rows, model_dim), low),
+            pltpu.VMEM((rows, model_dim), low),
             pltpu.VMEM((rows, 2 * width), jnp.float32),
             pltpu.VMEM((rows, width), jnp.float32),
-            pltpu.VMEM((2, rows, width), low),
-            pltpu.VMEM((2, rows, 2 * width), low),
-            pltpu.VMEM((2, rows, model_dim), low),
+            pltpu.VMEM((total, width), low),
+            pltpu.VMEM((total, 2 * width), low),
             pltpu.VMEM((rows, 128), jnp.float32),
-            held(4),
-            held(16),
-            held(16),
-            held(8),
-            held(4),
-            held(4),
-            held(4),
+            pltpu.VMEM((2, tall, cols), low),
+            pltpu.VMEM((13, tall, cols), low),
+            pltpu.VMEM((2, tall, cols), low),
+            pltpu.VMEM((total, tile), low),
+            pltpu.VMEM((total, tile), low),
+            pltpu.VMEM((3, filled, tile), jnp.float32),
+            pltpu.VMEM((3, shared_width, tile), low),
         ]
         + [dma((4,)), dma((4,)), dma((4,)), dma((8,)), dma((16,)), dma((16,)), dma((16,)), dma]
-        + [dma((4,)), dma((6,)), dma((8,)), dma((7,)), dma((7,))]
-        + [dma((16,)), dma((16,)), dma((8,)), dma((8,))]
-        + [dma((4,))] * 6,
+        + [dma((4,)), dma((2,)), dma((6,)), dma((8,)), dma((7,)), dma((7,))]
+        + [dma((16,)), dma((16,)), dma((8,)), dma((8,)), dma((4,)), dma((4,))]
+        + [dma((8,))] * 4,
         compiler_params=pltpu.CompilerParams(
             collective_id=cid, has_side_effects=True, vmem_limit_bytes=63 * 2**20
         ),
         name="experts",
     )(x_cols, grads_all, kept_rows, *weights)
+
+
+def row_of(columns):
+    part = columns[:, :128]
+    for i in range(1, columns.shape[1] // 128):
+        part = part + columns[:, i * 128 : (i + 1) * 128]
+    total = jnp.sum(part.T, axis=0, keepdims=True)
+    return jnp.broadcast_to(total, (8, total.shape[1]))
+
+
+def unwind_kernel(
+    dn2_ref,
+    unit_ref,
+    inv_ref,
+    second_ref,
+    grad_ref,
+    tokens_ref,
+    inv_one_ref,
+    first_ref,
+    small_ref,
+    q_ref,
+    k_ref,
+    v_ref,
+    ke_ref,
+    ve_ref,
+    context_ref,
+    log_ref,
+    cos_ref,
+    sin_ref,
+    n1_hbm,
+    wq_hbm,
+    wk_hbm,
+    wv_hbm,
+    wo_hbm,
+    tokens_grad_ref,
+    weight_grads_ref,
+    sums_ref,
+    n1,
+    wq,
+    wk,
+    wv,
+    wo,
+    grad_all,
+    grad_own,
+    hidden_grad,
+    dc,
+    dq,
+    dk,
+    dv,
+    lin_grads,
+    dke,
+    dve,
+    later_k,
+    later_v,
+    staged,
+    mine,
+    from_y,
+    from_below,
+    from_above,
+    tp_staged,
+    tp_mine,
+    tp_sib,
+    tp_x,
+    dn1,
+    row_mine,
+    row_sib,
+    row_x,
+    smalls,
+    load_sem,
+    g_send,
+    g_recv,
+    row_send,
+    row_recv,
+    kv_send,
+    kv_recv,
+    y_send,
+    y_recv,
+    up_send,
+    up_recv,
+    down_send,
+    down_recv,
+    tp_send,
+    tp_recv,
+    small_send,
+    small_recv,
+):
+    ep, tp, z, y, x, core = place()
+    rows, cols = unit_ref.shape
+    model_dim = n1.shape[1]
+    heads = cols // HD
+    block = mine.shape[1]
+    low, full = jnp.bfloat16, jnp.float32
+    score_scale = HD ** (-0.5)
+    sibling, across = (ep, tp + 1 - 2 * core), (ep, tp + 2 - 4 * x)
+    beside = (ep + 1 - 2 * y, tp)
+    above, below = (ep + 2, tp), (ep - 2, tp)
+    sources = smalls.shape[0]
+    others = [(lax.rem(ep + i, sources), tp) for i in range(1, sources)]
+    loads = [
+        pltpu.make_async_copy(source, target, load_sem.at[i])
+        for i, (source, target) in enumerate(
+            ((wo_hbm, wo), (n1_hbm, n1), (wq_hbm, wq), (wk_hbm, wk), (wv_hbm, wv))
+        )
+    ]
+    for copy in loads:
+        copy.start()
+    greet([across, sibling] + others)
+
+    step = 64
+
+    def by_rows(body):
+        def one(i, carry):
+            body(pl.ds(pl.multiple_of(i * step, step), step))
+            return carry
+
+        lax.fori_loop(0, rows // step, one, 0)
+
+    def row_exchange(i, values):
+        row_mine[2 * i] = values
+        first = remote(
+            row_mine.at[2 * i], row_sib.at[i], row_send.at[2 * i], row_recv.at[2 * i], sibling
+        )
+        first.start()
+        first.wait_recv()
+        row_mine[2 * i + 1] = row_mine[2 * i] + row_sib[i]
+        second = remote(
+            row_mine.at[2 * i + 1],
+            row_x.at[i],
+            row_send.at[2 * i + 1],
+            row_recv.at[2 * i + 1],
+            across,
+        )
+        second.start()
+        second.wait_recv()
+        first.wait_send()
+        second.wait_send()
+        return (row_mine[2 * i + 1] + row_x[i]).T[:, :1]
+
+    dn1[...] = dn2_ref[...] * second_ref[:1, :] * unit_ref[...]
+    mean = row_exchange(0, row_of(dn1[...])) * (1.0 / model_dim)
+    dn1[:, :128] = jnp.broadcast_to(mean, (rows, 128))
+
+    def norm_two(span):
+        scaled = dn2_ref[span, :] * second_ref[:1, :]
+        value = grad_ref[span, :].astype(full) + inv_ref[span, :1] * (
+            scaled - unit_ref[span, :] * dn1[span, :1]
+        )
+        hidden_grad[span, :] = value
+        grad_own[span, :] = value.astype(low)
+
+    by_rows(norm_two)
+
+    def quarter(at):
+        return grad_all.at[:, pl.ds(pl.multiple_of(at * cols, cols), cols)]
+
+    g_x = remote(grad_own, quarter(tp), g_send.at[0], g_recv.at[0], across)
+    g_s = remote(grad_own, quarter(tp), g_send.at[1], g_recv.at[1], sibling)
+    g_x.start()
+    g_s.start()
+    own_cut = pl.ds(pl.multiple_of(tp * cols, cols), cols)
+    grad_all[:, own_cut] = grad_own[...]
+    g_x.wait_recv()
+    theirs = quarter(tp + 2 - 4 * x)
+    g_f = remote(theirs, theirs, g_send.at[2], g_recv.at[2], sibling)
+    g_f.start()
+    g_s.wait_recv()
+    g_f.wait_recv()
+    loads[0].wait()
+    dc[...] = times_transpose(grad_all[...], wo[...]).astype(low)
+
+    def over_y(kind, z_at):
+        n = kind * 4 + z_at
+        return remote(staged.at[n], from_y.at[n], y_send.at[n], y_recv.at[n], beside)
+
+    def weight_blocks(kind, left, right):
+        def other(i, carry):
+            z_at = lax.rem(i * 3, 4)
+            cut = pl.ds(pl.multiple_of((z_at * 2 + 1 - y) * block, block), block)
+            staged[kind * 4 + z_at] = inner_rows(left[:, cut], right[...]).astype(low)
+            over_y(kind, z_at).start()
+            return carry
+
+        def ours(i, carry):
+            z_at = lax.rem(i * 3, 4)
+            cut = pl.ds(pl.multiple_of((z_at * 2 + y) * block, block), block)
+            mine[kind * 4 + z_at] = inner_rows(left[:, cut], right[...]).astype(low)
+            return carry
+
+        lax.fori_loop(0, 4, other, 0)
+        lax.fori_loop(0, 4, ours, 0)
+
+    def up(kind, z_at):
+        n = kind * 4 + z_at
+        return remote(mine.at[n], from_below.at[n], up_send.at[n], up_recv.at[n], above)
+
+    def down(kind, z_at):
+        n = kind * 4 + z_at
+        return remote(mine.at[n], from_above.at[n], down_send.at[n], down_recv.at[n], below)
+
+    def y_stage(kind):
+        def one(i, carry):
+            z_at = lax.rem(i * 3, 4)
+            n = kind * 4 + z_at
+            over_y(kind, z_at).wait_recv()
+            add_blocks(mine.at[n], [from_y.at[n]], block)
+
+            @pl.when((z == 0) & (z_at > 0))
+            def _():
+                up(kind, z_at).start()
+
+            @pl.when((z == 3) & (z_at < 3))
+            def _():
+                down(kind, z_at).start()
+
+            return carry
+
+        lax.fori_loop(0, 4, one, 0)
+
+    def chain(kind):
+        def rise(z_at):
+            n = kind * 4 + z_at
+            up(kind, z_at).wait_recv()
+            add_blocks(mine.at[n], [from_below.at[n]], block)
+            up(kind, z_at).start()
+
+        def fall(z_at):
+            n = kind * 4 + z_at
+            down(kind, z_at).wait_recv()
+            add_blocks(mine.at[n], [from_above.at[n]], block)
+            down(kind, z_at).start()
+
+        @pl.when(z == 1)
+        def _():
+            rise(3)
+            rise(2)
+            fall(0)
+
+        @pl.when(z == 2)
+        def _():
+            fall(0)
+            fall(1)
+            rise(3)
+
+    def final(kind):
+        n = kind * 4 + z
+
+        @pl.when(z > 0)
+        def _():
+            up(kind, z).wait_recv()
+
+        @pl.when(z < 3)
+        def _():
+            down(kind, z).wait_recv()
+
+        def one(i, carry):
+            span = pl.ds(pl.multiple_of(i * 32, 32), 32)
+            value = mine[n, span, :].astype(full)
+            low_part = from_below[n, span, :].astype(full)
+            high_part = from_above[n, span, :].astype(full)
+            value = value + jnp.where(z > 0, low_part, 0.0) + jnp.where(z < 3, high_part, 0.0)
+            weight_grads_ref[kind, span, :] = value
+            return carry
+
+        lax.fori_loop(0, block // 32, one, 0)
+
+    weight_blocks(0, grad_all, context_ref)
+
+    half = rows // 2
+
+    def terms(h, qb, key_count, keys, values):
+        cut = pl.ds(pl.multiple_of(h * HD, HD), HD)
+        span = pl.ds(qb * half, half)
+        lane = lax.broadcasted_iota(jnp.int32, (1, 128), 1)
+        log_total = jnp.sum(jnp.where(lane == h, log_ref[span, :], 0.0), axis=1, keepdims=True)
+        queries, grads = q_ref[span, cut], dc[span, cut]
+        delta = jnp.sum(
+            grads.astype(full) * context_ref[span, cut].astype(full), axis=1, keepdims=True
+        )
+        key_part, value_part = keys[:key_count, cut], values[:key_count, cut]
+        probs = jnp.exp(times_transpose(queries, key_part) * score_scale - log_total)
+        scores_grad = (probs * (times_transpose(grads, value_part) - delta)).astype(low)
+        return (
+            jnp.dot(scores_grad, key_part, preferred_element_type=full),
+            inner_rows(scores_grad, queries),
+            inner_rows(probs.astype(low), grads),
+        )
+
+    def spans(h, qb):
+        return pl.ds(qb * half, half), pl.ds(pl.multiple_of(h * HD, HD), HD)
+
+    later = (
+        remote(dke, later_k, kv_send.at[0], kv_recv.at[0], beside),
+        remote(dve, later_v, kv_send.at[1], kv_recv.at[1], beside),
+    )
+
+    @pl.when(y == 1)
+    def _():
+        def head(h, carry):
+            cut = pl.ds(pl.multiple_of(h * HD, HD), HD)
+            first = terms(h, 0, rows, ke_ref, ve_ref)
+            dq[spans(h, 0)[0], cut] = first[0]
+            dk[:, cut] = first[1]
+            dv[:, cut] = first[2]
+            second = terms(h, 1, rows, ke_ref, ve_ref)
+            dq[spans(h, 1)[0], cut] = second[0]
+            dke[:, cut] = ((dk[:, cut] + second[1]) * score_scale).astype(low)
+            dve[:, cut] = (dv[:, cut] + second[2]).astype(low)
+            return carry
+
+        lax.fori_loop(0, heads, head, 0)
+        for copy in later:
+            copy.start()
+
+    @pl.when(y == 0)
+    def _():
+        dq[...] = jnp.zeros_like(dq)
+
+    y_stage(0)
+
+    def head(h, carry):
+        cut = pl.ds(pl.multiple_of(h * HD, HD), HD)
+        second = terms(h, 1, rows, k_ref, v_ref)
+        dq[half:, cut] = dq[half:, cut] + second[0]
+        dk[:, cut] = second[1] * score_scale
+        dv[:, cut] = second[2]
+        first = terms(h, 0, half, k_ref, v_ref)
+        dq[:half, cut] = dq[:half, cut] + first[0]
+        dk[:half, cut] = dk[:half, cut] + first[1] * score_scale
+        dv[:half, cut] = dv[:half, cut] + first[2]
+        return carry
+
+    lax.fori_loop(0, heads, head, 0)
+
+    def rotate_back(source, target, scale):
+        def one(h, carry):
+            cut = pl.ds(pl.multiple_of(h * HD, HD), HD)
+            value = source[:, cut] * scale
+            turned = value * cos_ref[...] - pltpu.roll(value, HD // 2, 1) * sin_ref[...]
+            lin_grads[target, :, cut] = turned.astype(low)
+            return carry
+
+        lax.fori_loop(0, heads, one, 0)
+
+    rotate_back(dq, 0, score_scale)
+    loads[1].wait()
+    weight_blocks(1, n1, lin_grads.at[0])
+    chain(0)
+
+    @pl.when(y == 0)
+    def _():
+        for copy in later:
+            copy.wait_recv()
+
+        def add(span):
+            dk[span, :] = dk[span, :] + later_k[span, :].astype(full)
+            dv[span, :] = dv[span, :] + later_v[span, :].astype(full)
+
+        by_rows(add)
+
+    rotate_back(dk, 1, 1.0)
+    lin_grads[2] = dv[...].astype(low)
+    weight_blocks(2, n1, lin_grads.at[1])
+    weight_blocks(3, n1, lin_grads.at[2])
+    y_stage(1)
+    for copy in loads[2:]:
+        copy.wait()
+
+    def dn1_part(at, target):
+        cut = pl.ds(pl.multiple_of(at * cols, cols), cols)
+        total = times_transpose(lin_grads[0], wq[cut, :])
+        total = total + times_transpose(lin_grads[1], wk[cut, :])
+        total = total + times_transpose(lin_grads[2], wv[cut, :])
+        target[...] = total.astype(low)
+
+    def to_sibling(i):
+        return remote(tp_staged.at[i], tp_sib.at[i], tp_send.at[i], tp_recv.at[i], sibling)
+
+    def part_of(i):
+        x_at = 1 - x + (2 * x - 1) * i
+        dn1_part(x_at * 2 + 1 - core, tp_staged.at[i])
+        to_sibling(i).start()
+        dn1_part(x_at * 2 + core, tp_mine.at[i])
+
+    out_x = remote(tp_mine.at[0], tp_x, tp_send.at[2], tp_recv.at[2], across)
+    part_of(0)
+    to_sibling(0).wait_recv()
+    add_blocks(tp_mine.at[0], [tp_sib.at[0]], rows)
+    out_x.start()
+    part_of(1)
+    chain(1)
+    to_sibling(1).wait_recv()
+    out_x.wait_recv()
+
+    def sum_parts(span):
+        dn1[span, :] = (
+            tp_mine[1, span, :].astype(full)
+            + tp_sib[1, span, :].astype(full)
+            + tp_x[span, :].astype(full)
+        )
+
+    by_rows(sum_parts)
+
+    def unit_one(span):
+        return tokens_ref[span, :].astype(full) * inv_one_ref[span, :1]
+
+    def products(span):
+        dq[span, :] = dn1[span, :] * unit_one(span)
+
+    by_rows(products)
+    gain_grad = jnp.sum(dq[...], axis=0, keepdims=True)
+    dq[...] = dq[...] * first_ref[:1, :]
+    total = row_exchange(1, row_of(dq[...]))
+    dk[:, :128] = jnp.broadcast_to(total * (1.0 / model_dim), (rows, 128))
+
+    def norm_one(span):
+        scaled = dn1[span, :] * first_ref[:1, :]
+        value = hidden_grad[span, :] + inv_one_ref[span, :1] * (
+            scaled - unit_one(span) * dk[span, :1]
+        )
+        tokens_grad_ref[span, :] = value.astype(low)
+
+    by_rows(norm_one)
+
+    own = smalls.at[ep]
+    own[...] = small_ref[...]
+    own[0:1, :] = gain_grad
+    for i in range(3):
+        own[i + 1 : i + 2, :] = jnp.sum(lin_grads[i].astype(full), axis=0, keepdims=True)
+
+    def small_to(i):
+        return remote(own, own, small_send.at[i - 1], small_recv.at[i - 1], others[i - 1])
+
+    for i in range(1, sources):
+        small_to(i).start()
+    y_stage(2)
+    final(0)
+    chain(2)
+    y_stage(3)
+    final(1)
+    chain(3)
+    for i in range(1, sources):
+        small_to(i).wait_recv()
+    total = smalls[0]
+    for i in range(1, sources):
+        total = total + smalls[i]
+    sums_ref[...] = total
+    final(2)
+    final(3)
+
+    for copy in (g_x, g_s, g_f, out_x, to_sibling(0), to_sibling(1)):
+        copy.wait_send()
+
+    @pl.when(y == 1)
+    def _():
+        for copy in later:
+            copy.wait_send()
+
+    for i in range(1, sources):
+        small_to(i).wait_send()
+
+    def finish(n, carry):
+        remote(staged.at[0], from_y.at[0], y_send.at[n], y_recv.at[n], beside).wait_send()
+        z_at = lax.rem(n, 4)
+
+        @pl.when(z_at > z)
+        def _():
+            remote(mine.at[0], from_below.at[0], up_send.at[n], up_recv.at[n], above).wait_send()
+
+        @pl.when(z_at < z)
+        def _():
+            remote(mine.at[0], from_above.at[0], down_send.at[n], down_recv.at[n], below).wait_send()
+
+        return carry
+
+    lax.fori_loop(0, 16, finish, 0)
+
+
+def unwind(vmem_args, hbm_args, cid):
+    rows, cols = vmem_args[0].shape
+    model_dim = hbm_args[0].shape[1]
+    sources = 8
+    block = model_dim // sources
+    low, full, dma = jnp.bfloat16, jnp.float32, pltpu.SemaphoreType.DMA
+    vmem, hbm = pl.BlockSpec(memory_space=pltpu.VMEM), pl.BlockSpec(memory_space=pl.ANY)
+
+    def buffers(*shape, dtype=low):
+        return pltpu.VMEM(shape, dtype)
+
+    return pl.pallas_call(
+        unwind_kernel,
+        out_shape=[
+            jax.ShapeDtypeStruct((rows, cols), low),
+            jax.ShapeDtypeStruct((4, block, cols), full),
+            jax.ShapeDtypeStruct((16, cols), full),
+        ],
+        in_specs=[vmem] * len(vmem_args) + [hbm] * len(hbm_args),
+        out_specs=[vmem] * 3,
+        scratch_shapes=[buffers(*arg.shape) for arg in hbm_args]
+        + [
+            buffers(rows, model_dim),
+            buffers(rows, cols),
+            buffers(rows, cols, dtype=full),
+            buffers(rows, cols),
+            buffers(rows, cols, dtype=full),
+            buffers(rows, cols, dtype=full),
+            buffers(rows, cols, dtype=full),
+            buffers(3, rows, cols),
+            buffers(rows, cols),
+            buffers(rows, cols),
+            buffers(rows, cols),
+            buffers(rows, cols),
+        ]
+        + [buffers(16, block, cols)] * 5
+        + [
+            buffers(2, rows, cols),
+            buffers(2, rows, cols),
+            buffers(2, rows, cols),
+            buffers(rows, cols),
+            buffers(rows, cols, dtype=full),
+            buffers(4, 8, rows, dtype=full),
+            buffers(2, 8, rows, dtype=full),
+            buffers(2, 8, rows, dtype=full),
+            buffers(sources, 16, cols, dtype=full),
+        ]
+        + [dma((5,)), dma((3,)), dma((3,)), dma((4,)), dma((4,)), dma((2,)), dma((2,))]
+        + [dma((16,))] * 6
+        + [dma((3,)), dma((3,)), dma((7,)), dma((7,))],
+        compiler_params=pltpu.CompilerParams(
+            collective_id=cid, has_side_effects=True, vmem_limit_bytes=60 * 2**20
+        ),
+        name="unwind",
+    )(*vmem_args, *hbm_args)
 
 
 def tp_total(value):
@@ -1774,7 +2420,7 @@
     extra_rows = jnp.concatenate([router_weight.T, switch_vector[None, :]], axis=0)
     extra_rows = jnp.pad(extra_rows, ((0, 16 - extra_rows.shape[0]), (0, 0)))
     kept_rows = jnp.pad(kept_own.T, ((0, 16 - expert_total), (0, 0))).astype(jnp.bfloat16)
-    normed_all, hidden_all, both_all, out_part, reduced, logit_tile = experts(
+    reduced, ffn_cols, logit_tile, expert_grads, shared_parts, *_ = experts(
         normed_cols,
         grads_all,
         kept_rows,
@@ -1790,39 +2436,18 @@
         expert_total,
         4,
     )
-    padded = hidden_all.shape[1]
-    ffn_cols = lax.psum_scatter(
-        lax.psum_scatter(out_part, "tp", scatter_dimension=1, tiled=True),
-        "ep",
-        scatter_dimension=0,
-        tiled=True,
-    )
-    layer_out = (hidden_cols + ffn_cols.astype(jnp.float32)).astype(jnp.bfloat16)
-    down_grad = inner_rows(hidden_all[:, :width], grads_all)
-    gate_rows_grad = inner_rows(both_all[:, :width], normed_all)
-    up_rows_grad = inner_rows(both_all[:, padded : padded + width], normed_all)
-    expert_down_grad = down_grad[None, :expert_width]
-    expert_gate_grad = gate_rows_grad[:expert_width].T[None]
-    expert_up_grad = up_rows_grad[:expert_width].T[None]
-    shared_parts = jnp.stack(
-        [
-            gate_rows_grad[expert_width:],
-            up_rows_grad[expert_width:],
-            down_grad[expert_width:],
-        ]
-    ).astype(jnp.bfloat16)
-    shared_parts = shared_parts.reshape(3, shared_width, sources, -1).transpose(2, 0, 1, 3)
+    layer_out = (hidden_cols + ffn_cols).astype(jnp.bfloat16)
     shared_parts = lax.all_to_all(shared_parts, "ep", split_axis=0, concat_axis=0, tiled=True)
     shared_parts = shared_parts.transpose(1, 0, 2, 3).reshape(3, sources * shared_width, -1)
     shared_parts = shared_parts.astype(jnp.float32)
-    shared_gate_grad = shared_parts[0].T
-    shared_up_grad = shared_parts[1].T
-    shared_down_grad = shared_parts[2]
+    shared_gate_grad = shared_parts[1].T
+    shared_up_grad = shared_parts[2].T
+    shared_down_grad = shared_parts[0]
 
     normed_grad = reduced[:tok_count]
     probs_grad = reduced[tok_count : tok_count + expert_total].T * kept_own
     switch_grad = reduced[tok_count + expert_total]
-    logit_at = width - (padded - 128)
+    logit_at = width % 128
     probs_own = softmax_rows(logit_tile[:, logit_at : logit_at + expert_total])
     switch = jax.nn.sigmoid(logit_tile[:, logit_at + expert_total])
     logit_grad = (
@@ -1838,119 +2463,76 @@
         + switch_lin_grad[:, None] * own_cols(switch_vector).astype(jnp.float32)[None, :]
     )
     second_gain_grad = jnp.sum(normed_grad * unit_two, axis=0)
-    scaled_two = normed_grad * second_cols
-    mean_two = tp_total(jnp.sum(scaled_two * unit_two, axis=-1, keepdims=True)) / model_dim
-    hidden_grad_cols = out_grad.astype(jnp.float32) + inv_two * (scaled_two - unit_two * mean_two)
-
-    attended_grad = gather_tp(hidden_grad_cols.astype(jnp.bfloat16), 0)
-    output_grad = inner_rows(attended_grad, context)
-    output_grad = lax.psum_scatter(
-        output_grad.astype(jnp.bfloat16), "ep", scatter_dimension=0, tiled=True
-    )
-    output_grad = output_grad.astype(jnp.float32).T
-    context_grad = (
-        times_transpose(attended_grad, output_weight)
-        .astype(jnp.bfloat16)
-        .reshape(tok_count, head_count, HD)
-    )
-    scores = attention_scores()
-    attn_probs = jnp.exp(scores - log_total)
-    probs_again = attn_probs.astype(jnp.bfloat16)
-    probs_grad_att = jnp.einsum(
-        "qhd,khd->hqk", context_grad, values_both, preferred_element_type=jnp.float32
-    )
-    values_both_grad = jnp.einsum(
-        "hqk,qhd->khd", probs_again, context_grad, preferred_element_type=jnp.float32
-    )
-    scores_grad = (
-        attn_probs * (probs_grad_att - jnp.sum(attn_probs * probs_grad_att, axis=-1, keepdims=True))
-    ).astype(jnp.bfloat16)
-    queries_grad = (
-        jnp.einsum("hqk,khd->qhd", scores_grad, keys_both, preferred_element_type=jnp.float32)
-        * score_scale
-    )
-    keys_both_grad = (
-        jnp.einsum("hqk,qhd->khd", scores_grad, queries, preferred_element_type=jnp.float32)
-        * score_scale
-    )
-    later_keys_grad, later_values_grad = passed_along(
-        (
-            keys_both_grad[:tok_count].astype(jnp.bfloat16),
-            values_both_grad[:tok_count].astype(jnp.bfloat16),
-        ),
-        "ep",
-        -1,
-    )
-    keep_later = jnp.where(has_earlier, 0.0, 1.0).astype(jnp.float32)
-    keys_grad = keys_both_grad[tok_count:] + keep_later * later_keys_grad
-    values_grad = values_both_grad[tok_count:] + keep_later * later_values_grad
-    value_lin_grad = values_grad.reshape(tok_count, head_count * HD).astype(jnp.bfloat16)
-    query_lin_grad = (
-        rotate(queries_grad, cosine, -sine_part)
-        .reshape(tok_count, head_count * HD)
-        .astype(jnp.bfloat16)
-    )
-    key_lin_grad = (
-        rotate(keys_grad, cosine, -sine_part)
-        .reshape(tok_count, head_count * HD)
-        .astype(jnp.bfloat16)
-    )
-    lin_grads = jnp.concatenate([query_lin_grad, key_lin_grad, value_lin_grad], axis=1)
-    lin_width = head_count * HD
-    normed_one_grad = times_transpose(query_lin_grad, query_weight) + times_transpose(
-        key_lin_grad, key_weight
-    )
-    normed_one_grad = normed_one_grad + times_transpose(value_lin_grad, value_weight)
-    normed_one_cols = scatter_tp(normed_one_grad.astype(jnp.bfloat16), 1)
-    unit_cols = tokens.astype(jnp.float32) * inv_one
-    first_cols = own_cols(first_gain)
-    first_gain_grad = jnp.sum(normed_one_cols * unit_cols, axis=0)
-    scaled_one = normed_one_cols * first_cols
-    mean_one = tp_total(jnp.sum(scaled_one * unit_cols, axis=-1, keepdims=True)) / model_dim
-    tokens_grad = (hidden_grad_cols + inv_one * (scaled_one - unit_cols * mean_one)).astype(
-        jnp.bfloat16
-    )
+
+    def wide(column):
+        return jnp.broadcast_to(column, (tok_count, 128))
+
+    def tall(vector):
+        return jnp.broadcast_to(vector[None, :], (8, vector.shape[0]))
+
+    def flat(heads_apart):
+        return heads_apart.reshape(tok_count, head_count * HD)
 
     small = jnp.concatenate(
-        [first_gain_grad[None], second_gain_grad[None], switch_vector_grad[None], router_grad.T],
-        axis=0,
+        [second_gain_grad[None], switch_vector_grad[None], router_grad.T], axis=0
     )
     small_rows = small.shape[0]
-    small = jnp.concatenate([jnp.sum(lin_grads.astype(jnp.float32), axis=0), small.reshape(-1)])
-    small = jnp.pad(small, (0, 16 * 3 * lin_width - small.shape[0])).reshape(16, 3 * lin_width)
-    weight_grads = scatter_ep(
-        inner_rows(normed_one, lin_grads).astype(jnp.bfloat16), small.astype(jnp.bfloat16), 5
+    small = jnp.pad(small, ((4, 12 - small_rows), (0, 0)))
+    log_rows = jnp.pad(log_total[:, :, 0].T, ((0, 0), (0, 128 - head_count)))
+    cos_wide = jnp.concatenate([cosine[:, 0], cosine[:, 0]], axis=1)
+    sin_wide = jnp.concatenate([-sine_part[:, 0], sine_part[:, 0]], axis=1)
+    tokens_grad, weight_grads, sums = unwind(
+        [
+            normed_grad,
+            unit_two,
+            wide(inv_two),
+            tall(second_cols),
+            out_grad,
+            tokens,
+            wide(inv_one),
+            tall(own_cols(first_gain)),
+            small,
+            flat(queries),
+            flat(keys_rot),
+            flat(values_all),
+            flat(earlier_keys),
+            flat(earlier_values),
+            context,
+            log_rows,
+            cos_wide,
+            sin_wide,
+        ],
+        [normed_one, query_weight, key_weight, value_weight, output_weight],
+        5,
     )
     share = model_dim // sources
-    small = weight_grads[share:].reshape(-1)
-    weight_grads = weight_grads[:share]
     bias_width = HD // sources
     bias_sums = lax.dynamic_slice_in_dim(
-        small[: 3 * lin_width].reshape(3, head_count, HD), ep * bias_width, bias_width, 2
-    )
-    small = small[3 * lin_width : 3 * lin_width + small_rows * col_width]
-    spread = lax.all_gather(small.reshape(small_rows, col_width), "tp", axis=1, tiled=True)
+        sums[1:4].reshape(3, head_count, HD), ep * bias_width, bias_width, 2
+    )
+    spread = jnp.concatenate([sums[:1], sums[4 : 4 + small_rows]], axis=0)
+    spread = lax.all_gather(spread, "tp", axis=1, tiled=True)
     spread = lax.dynamic_slice_in_dim(spread, ep * share, share, 1)
     return (
         layer_out,
         tokens_grad,
         spread[0],
-        weight_grads[:, :lin_width],
-        weight_grads[:, lin_width : 2 * lin_width],
-        weight_grads[:, 2 * lin_width :],
+        weight_grads[1],
+        weight_grads[2],
+        weight_grads[3],
         bias_sums[0],
         bias_sums[1],
         bias_sums[2],
-        output_grad,
+        weight_grads[0].T,
         spread[1],
         spread[3:].T,
         shared_gate_grad,
         shared_up_grad,
         shared_down_grad,
         spread[2],
-        expert_gate_grad,
-        expert_up_grad,
-        expert_down_grad,
+        expert_grads[1].T[None],
+        expert_grads[2].T[None],
+        expert_grads[0][None],
     )
 
 

time: 842 us -> 731 us (0.87)
  matrix products: 103 us -> 20.7 us
  Pallas kernels: 541 us -> 588 us
  waiting for transfers between devices: 21.2 us -> 0.01 us
  other arithmetic: 47.3 us -> 33.6 us
  between operations: 15.3 us -> 1.66 us
  blocking collectives: 24.5 us -> 12.2 us
    pallas_call x1, Pallas kernels: 224 us -> 308 us  [experts(): pl.pallas_call(functools.partial(experts_kernel, expert_width, shared_wid...]
    dot_general x6 -> x1, matrix products: 53.9 us -> 0.9 us  [inner_rows(): lax.dot_general(left_side, right_side, (((0,), (0,)), ((), ())), preferre...]
    pallas_call x2 -> x1, Pallas kernels: 46.2 us -> 18.3 us  [gather_tp(): pl.pallas_call(gather_tp_kernel, out_shape=jax.ShapeDtypeStruct((rows, 4...]
    pallas_call x2 -> x1, Pallas kernels: 36 us -> 16.5 us  [scatter_tp(): pl.pallas_call(scatter_tp_kernel, out_shape=jax.ShapeDtypeStruct((rows, c...]
    dot_general x4 -> x0, matrix products: 18 us -> none  [the longest x1 5.16 us: dense_plan(): jnp.einsum('qhd,khd->hqk', context_grad, values_both, preferred_element_t...]
    unnamed x134 -> x66, local copies, waits for them, and re-layouts: 27.2 us -> 11.5 us
    ppermute x4 -> x2, starting transfers between devices: 20.7 us -> 6.79 us  [passed_along(): lax.ppermute(value, axis, [(source, source + steps) for source in range(l...]
    ppermute x4 -> x2, waiting for transfers between devices: 13.6 us -> 0.01 us  [passed_along(): lax.ppermute(value, axis, [(source, source + steps) for source in range(l...]
  transfers between devices with their start and end apart: 8 -> 3, of which waited for: 2 -> 0; matrix products, arithmetic and copies ran while one was open for 22% -> 10% of each run, Pallas kernels for 34% -> 34%
where the time goes in v3:
time: 731 us; the launch traced here: 723 us
  Pallas kernels  588 us (80%)
  local copies, waits for them, and re-layouts  47.7 us (7%)
  other arithmetic  33.6 us (5%)
  matrix products  20.7 us (3%)
  starting transfers between devices  19.7 us (3%)
  blocking collectives  12.2 us (2%)
    pallas_call x1, Pallas kernels, experts(): pl.pallas_call(functools.partial(experts_kernel, expert_width, shared_wid...  308 us
    pallas_call x1, Pallas kernels, unwind(): pl.pallas_call(unwind_kernel, out_shape=[jax.ShapeDtypeStruct((rows, cols...  171 us
    pallas_call x1, Pallas kernels, gather_all(): pl.pallas_call(gather_all_kernel, out_shape=jax.ShapeDtypeStruct((8 * row...  74.5 us
    pallas_call x1, Pallas kernels, gather_tp(): pl.pallas_call(gather_tp_kernel, out_shape=jax.ShapeDtypeStruct((rows, 4...  18.3 us
    pallas_call x1, Pallas kernels, scatter_tp(): pl.pallas_call(scatter_tp_kernel, out_shape=jax.ShapeDtypeStruct((rows, c...  16.5 us
  transfers between devices with their start and end apart: 3, of which 0 were waited for; matrix products, arithmetic and copies ran while one was open for 10% of the time, Pallas kernels for 34%

profile of v3, /device:TPU:9, one launch (start us, length us, event | category | flops | bytes accessed | tf_op | source)
XLA Modules:
  0.0 723.5 jit_solution(15783591004685042637)
XLA Ops:
  0.7 18.3 %gather_tp.1 = bf16[512,2048]{1,0:T(8,128)(2,1)} custom-call(bf16[512,512]{1,0:T(8,128)(2,1)} %tokens_ref.1), custom_call_target="tpu_custom_call" | custom-call | tf_op jit(solution)/shard_map/gather_tp/pallas_call | solution.py:531
  19.0 2.2 fusion.2
  24.1 3.1 collective-permute-start
  27.3 2.9 convolution_add_fusion.1
  32.7 2.4 copy.165
  35.1 2.9 convolution_add_fusion.2
  40.7 1.8 fusion.18
  42.5 3.2 multiply_subtract_fusion
  46.7 3.7 collective-permute-start.1
  50.4 1.8 select_reduce_fusion
  53.6 9.4 %convert_reduce_fusion = s32[512,8]{1,0:T(8,128)S(1)} fusion(s32[512,8]{1,0:T(8,128)S(1)} %copy.142, s32[512,8]{0,1:T(8,128)S(1)} %broadcast_select_fusion), kind=kLoop, calls=%fused_computation.2 | loop fusion | flops 6287360 | bytes 49152 | tf_op jit(solution)/shard_map/reduce_sum | solution.py:2323
  63.8 2.9 constant_dynamic-slice_fusion.1
  70.1 74.5 %gather_all.1.g_ref = bf16[4096,2048]{1,0:T(8,128)(2,1)} custom-call(bf16[512,512]{1,0:T(8,128)(2,1)} %grad_ref.1), custom_call_target="tpu_custom_call" | custom-call | tf_op jit(solution)/shard_map/gather_all/pallas_call | solution.py:778
  146.6 1.5 copy_bitcast_fusion.1
  148.8 2.0 copy.161.ve_ref
  150.8 3.3 fusion
  154.2 2.4 fusion.1
  157.6 5.4 fusion.7
  165.2 16.5 %scatter_tp.1 = f32[512,512]{1,0:T(8,128)S(1)} custom-call(bf16[512,2048]{1,0:T(8,128)(2,1)S(1)} %convolution_convert_fusion.p_ref), custom_call_target="tpu_custom_call" | custom-call | tf_op jit(solution)/shard_map/scatter_tp/pallas_call | solution.py:581
  182.0 6.0 psum.7
  189.3 307.8 %experts.1 = (f32[528,512]{1,0:T(8,128)}, f32[512,512]{1,0:T(8,128)}, f32[512,128]{1,0:T(8,128)}, f32[3,352,2048]{2,1,0:T(8,128)}, bf16[8,3,176,256]{3,2,1,0:T(8...) custom-call(bf16[512,512]{1,0:T(8,128)(2,1)} %get-tuple-element.132., ...), custom_call_target="tpu_custom_call" | custom-call | tf_op jit(solution)/shard_map/experts/pallas_call | solution.py:1728
  497.2 12.9 %all-to-all-start = ((bf16[8,3,176,256]{3,2,1,0:T(8,128)(2,1)}), bf16[8,3,176,256]{3,2,1,0:T(8,128)(2,1)}, u32[]{:S(2)}, u32[]{:S(2)}) async-start(bf16[8,3,176,256]{3,2,1,0:T(8,128)(2,1)} %get-tuple-element.33), calls=%async_computation | async-start | bytes 4325376 | tf_op jit(solution)/shard_map/all_to_all | solution.py:2440
  514.1 2.6 multiply_reduce_fusion
  517.3 1.9 copy_bitcast_fusion.ke_ref
  522.1 170.7 %unwind.1 = (bf16[512,512]{1,0:T(8,128)(2,1)}, f32[4,256,512]{2,1,0:T(8,128)}, f32[16,512]{1,0:T(8,128)}) custom-call(f32[512,512]{1,0:T(8,128)} %get-tuple-element.168.dn2_ref, f32[512,512]{1,0:T(8,128)} %get-tuple-element.133.unit_ref, f32[512,128]{1,0:T(8,128)} %broadcast_in_dim.72.inv_ref, f32[8,512]{1,0:T(8,128)} %broadcast_in_dim.120.second_ref, ...), custom_call_target="tpu_custom_call" | custom-call | tf_op jit(solution)/shard_map/unwind/pallas_call | solution.py:2262
  695.2 2.7 slice_bitcast_fusion.2
  698.9 6.3 all_gather.3
  708.2 7.3 %fusion.34 = (f32[1,352,2048]{2,1,0:T(8,128)}, f32[1,2048,352]{1,2,0:T(8,128)}, f32[1,2048,352]{1,2,0:T(8,128)}) fusion(f32[3,352,2048]{2,1,0:T(8,128)} %get-tuple-element.34), kind=kLoop, calls=%fused_computation.111 | loop fusion | bytes 17301504 | tf_op jit(solution)/shard_map/slice | solution.py:2535
  715.6 2.1 convert_bitcast_fusion
  717.7 1.5 fusion.35
  719.2 1.5 copy.157
  720.7 1.5 copy.156
  (127 shorter events, 36.9 us)
Async XLA Ops:
  0.7 20.6 %copy-start.23 = (f32[2048]{0:T(1024)S(1)}, f32[2048]{0:T(1024)}, u32[]{:S(2)}) copy-start(f32[2048]{0:T(1024)} %param.23) | copy-start | bytes 24580
  19.0 2.3 copy-start.2
  19.0 2.8 copy-start.12
  19.0 2.8 copy-start.26
  21.8 13.3 %copy-start.7 = (bf16[512,2048]{1,0:T(8,128)(2,1)}, bf16[512,2048]{1,0:T(8,128)(2,1)S(1)}, u32[]{:S(2)}) copy-start(bf16[512,2048]{1,0:T(8,128)(2,1)S(1)} %fusion.4.n1_hbm) | copy-start | bytes 6291460
  21.8 5.5 copy-start.27
  23.1 7.1 copy-start.14
  24.1 124.7 %collective-permute-start = (bf16[512,4,128]{0,2,1:T(8,128)(2,1)}, bf16[512,4,128]{0,2,1:T(8,128)(2,1)}, u32[]{:S(2)}, u32[]{:S(2)}) collective-permute-start(bf16[512,4,128]{0,2,1:T(8,128)(2,1)} %bitcast.49), channel_id=1, source_target_pairs={{0,4},{4,8},{8,12},{12,16},{16,20},{20,24},{24,28},{1,5},{5,9},{9,... | collective-permute-start | bytes 1572872 | tf_op jit(solution)/shard_map/ppermute | solution.py:24
  30.2 4.8 copy-start.28
  38.0 4.5 copy-start.9
  42.4 3.2 copy-start.10
  42.5 7.9 %copy-start.22 = (s32[512,4]{0,1:T(4,128)S(1)}, s32[512,4]{0,1:T(4,128)}, u32[]{:S(2)}) copy-start(s32[512,4]{0,1:T(4,128)} %param.40) | copy-start | bytes 24580
  42.5 8.0 %copy-start.25 = (s32[1,2048]{1,0:T(1,128)S(1)}, s32[1,2048]{1,0:T(1,128)}, u32[]{:S(2)}) copy-start(s32[1,2048]{1,0:T(1,128)} %param.41) | copy-start | bytes 24580
  46.7 104.1 %collective-permute-start.1 = (bf16[512,4,128]{2,0,1:T(8,128)(2,1)}, bf16[512,4,128]{2,0,1:T(8,128)(2,1)}, u32[]{:S(2)}, u32[]{:S(2)}) collective-permute-start(bf16[512,4,128]{2,0,1:T(8,128)(2,1)} %maximum_convert_fusion.1), channel_id=1, source_target_pairs={{0,4},{4,8},{8,12},{12,16},{16,20},{20,24},{24,28},{1,5},{5,9},{9,... | collective-permute-start | bytes 1572872 | tf_op jit(solution)/shard_map/ppermute | solution.py:24
  52.6 14.1 %copy-start.24 = (bf16[2048]{0:T(1024)(128)(2,1)S(1)}, bf16[2048]{0:T(1024)(128)(2,1)}, u32[]{:S(2)}) copy-start(bf16[2048]{0:T(1024)(128)(2,1)} %param.36) | copy-start | bytes 12292
  70.1 75.5 %copy-start.11 = (f32[512,64]{1,0:T(8,128)S(1)}, f32[512,64]{1,0:T(8,128)}, u32[]{:S(2)}) copy-start(f32[512,64]{1,0:T(8,128)} %copy-done.10) | copy-start | bytes 393220
  70.1 75.6 %copy-start.18 = (f32[512,64]{1,0:T(8,128)S(1)}, f32[512,64]{1,0:T(8,128)}, u32[]{:S(2)}) copy-start(f32[512,64]{1,0:T(8,128)} %get-tuple-element.162) | copy-start | bytes 393220
  70.1 76.6 %copy-start.15 = (bf16[512,4,64]{2,0,1:T(8,128)(2,1)S(1)}, bf16[512,4,64]{2,0,1:T(8,128)(2,1)}, u32[]{:S(2)}) copy-start(bf16[512,4,64]{2,0,1:T(8,128)(2,1)} %get-tuple-element.154) | copy-start | bytes 786436
  70.1 76.6 %copy-start.16 = (bf16[512,4,64]{2,0,1:T(8,128)(2,1)S(1)}, bf16[512,4,64]{2,0,1:T(8,128)(2,1)}, u32[]{:S(2)}) copy-start(bf16[512,4,64]{2,0,1:T(8,128)(2,1)} %get-tuple-element.155) | copy-start | bytes 786436
  144.5 3.6 copy-start.21
  154.1 3.2 copy-start.8
  157.6 6.4 copy-start.13
  165.2 16.5 %copy-start.3 = (bf16[512,512]{1,0:T(8,128)(2,1)S(1)}, bf16[512,512]{1,0:T(8,128)(2,1)}, u32[]{:S(2)}) copy-start(bf16[512,512]{1,0:T(8,128)(2,1)} %tokens_ref.1) | copy-start | bytes 1572868
  181.8 6.2 copy-start
  497.2 13.0 %copy-start.19 = (f32[512,128]{1,0:T(8,128)S(1)}, f32[512,128]{1,0:T(8,128)}, u32[]{:S(2)}) copy-start(f32[512,128]{1,0:T(8,128)} %get-tuple-element.29) | copy-start | bytes 786436
  497.2 15.8 %copy-start.6 = (bf16[512,512]{1,0:T(8,128)(2,1)S(1)}, bf16[512,512]{1,0:T(8,128)(2,1)}, u32[]{:S(2)}) copy-start(bf16[512,512]{1,0:T(8,128)(2,1)} %get-tuple-element.132.x_ref) | copy-start | bytes 1572868
  497.2 16.9 %copy-start.5 = (f32[512,512]{1,0:T(8,128)S(1)}, f32[512,512]{1,0:T(8,128)}, u32[]{:S(2)}) copy-start(f32[512,512]{1,0:T(8,128)} %get-tuple-element.133.unit_ref) | copy-start | bytes 3145732
  497.2 218.4 %all-to-all-start = ((bf16[8,3,176,256]{3,2,1,0:T(8,128)(2,1)}), bf16[8,3,176,256]{3,2,1,0:T(8,128)(2,1)}, u32[]{:S(2)}, u32[]{:S(2)}) async-start(bf16[8,3,176,256]{3,2,1,0:T(8,128)(2,1)} %get-tuple-element.33), calls=%async_computation | async-start | bytes 4325376 | tf_op jit(solution)/shard_map/all_to_all | solution.py:2440
  692.8 14.3 %copy-start.1 = (f32[512,512]{1,0:T(8,128)S(1)}, f32[512,512]{1,0:T(8,128)}, u32[]{:S(2)}) copy-start(f32[512,512]{1,0:T(8,128)} %copy-done) | copy-start | bytes 3145732
  692.8 14.3 %copy-start.4 = (bf16[512,512]{1,0:T(8,128)(2,1)S(1)}, bf16[512,512]{1,0:T(8,128)(2,1)}, u32[]{:S(2)}) copy-start(bf16[512,512]{1,0:T(8,128)(2,1)} %tokens_ref.1) | copy-start | bytes 1572868
  692.8 14.3 %copy-start.17 = (f32[512,512]{1,0:T(8,128)S(1)}, f32[512,512]{1,0:T(8,128)}, u32[]{:S(2)}) copy-start(f32[512,512]{1,0:T(8,128)} %get-tuple-element.27) | copy-start | bytes 3145732
  719.2 3.1 copy-start.20

commit v4 on v3

--- a/solution.py
+++ b/solution.py
@@ -2305,8 +2305,473 @@
     )(*vmem_args, *hbm_args)
 
 
-def tp_total(value):
-    return lax.psum(value, "tp")
+def attend_kernel(
+    first_ref,
+    bias_ref,
+    second_ref,
+    cos_ref,
+    sin_ref,
+    tokens_hbm,
+    grad_hbm,
+    wq_hbm,
+    wk_hbm,
+    wv_hbm,
+    wo_hbm,
+    hidden_ref,
+    unit_ref,
+    inv_ref,
+    normed_ref,
+    n1_ref,
+    inv_one_ref,
+    q_ref,
+    k_ref,
+    v_ref,
+    ke_ref,
+    ve_ref,
+    context_ref,
+    log_ref,
+    all_ref,
+    wq,
+    wk,
+    wv,
+    wo,
+    tokens,
+    lin,
+    total,
+    most,
+    weight,
+    earlier_k,
+    earlier_v,
+    tp_staged,
+    tp_mine,
+    tp_sib,
+    tp_x,
+    row_mine,
+    row_sib,
+    row_x,
+    load_sem,
+    t_send,
+    t_recv,
+    kv_send,
+    kv_recv,
+    tp_send,
+    tp_recv,
+    row_send,
+    row_recv,
+    up_sem,
+    down_sem,
+    a_sem,
+    b_sem,
+    s_sem,
+    recv_sem,
+    sib_sem,
+):
+    ep, tp, z, y, x, core = place()
+    rows, cols = hidden_ref.shape
+    model_dim = n1_ref.shape[1]
+    heads = cols // HD
+    low, full = jnp.bfloat16, jnp.float32
+    score_scale = HD ** (-0.5)
+    sibling, across = (ep, tp + 1 - 2 * core), (ep, tp + 2 - 4 * x)
+    beside = (ep + 1 - 2 * y, tp)
+    peer_a, peer_b, _, above, below = lane_peers()
+
+    def quarter(at):
+        return tokens.at[:, pl.ds(pl.multiple_of(at * cols, cols), cols)]
+
+    loads = [
+        pltpu.make_async_copy(source, target, load_sem.at[i])
+        for i, (source, target) in enumerate(
+            (
+                (tokens_hbm, quarter(tp)),
+                (wk_hbm, wk),
+                (wv_hbm, wv),
+                (wq_hbm, wq),
+                (wo_hbm, wo),
+            )
+        )
+    ]
+    for copy in loads:
+        copy.start()
+    greet([across, beside, sibling], True)
+
+    t_x = remote(tokens_hbm, quarter(tp), t_send.at[0], t_recv.at[0], across)
+    t_s = remote(tokens_hbm, quarter(tp), t_send.at[1], t_recv.at[1], sibling)
+    t_x.start()
+    t_s.start()
+
+    def choose(*values):
+        return jnp.where(
+            z == 0, values[0], jnp.where(z == 1, values[1], jnp.where(z == 2, values[2], values[3]))
+        )
+
+    coming = (z, choose(1, 0, 3, 2), choose(2, 2, 1, 1), choose(3, 3, 0, 0))
+
+    def spot(z_at, da, db):
+        group, at_quarter = lane_spot(z_at, da, db, core)
+        return all_ref.at[
+            pl.ds(pl.multiple_of(group * rows, rows), rows),
+            pl.ds(pl.multiple_of(at_quarter * cols, cols), cols),
+        ]
+
+    def at(z_at, da, db):
+        return z_at * 4 + da * 2 + db
+
+    def arrived(z_at, da, db):
+        block, n = spot(z_at, da, db), at(z_at, da, db)
+        remote(block, block, s_sem.at[n], recv_sem.at[n], sibling).wait_recv()
+        return block
+
+    def up(z_at, source):
+        return remote(source, spot(z_at, 0, 0), up_sem.at[z_at], recv_sem.at[at(z_at, 0, 0)], above)
+
+    def down(z_at, source):
+        return remote(source, spot(z_at, 0, 0), down_sem.at[z_at], recv_sem.at[at(z_at, 0, 0)], below)
+
+    def over_a(z_at, source):
+        return remote(source, spot(z_at, 0, 0), a_sem.at[z_at], recv_sem.at[at(z_at, 1, 0)], peer_a)
+
+    def over_b(z_at, da, source):
+        return remote(
+            source, spot(z_at, da, 0), b_sem.at[z_at * 2 + da], recv_sem.at[at(z_at, da, 1)], peer_b
+        )
+
+    def to_sibling(z_at, da, db, source):
+        n = at(z_at, da, db)
+        return remote(source, spot(z_at, da, db), s_sem.at[n], sib_sem.at[n], sibling)
+
+    def pass_z(k):
+        z_at = coming[k]
+        block = arrived(z_at, 0, 0)
+
+        @pl.when((z_at > z) & (z > 0))
+        def _():
+            down(z_at, block).start()
+
+        @pl.when((z_at < z) & (z < 3))
+        def _():
+            up(z_at, block).start()
+
+        over_a(z_at, block).start()
+        over_b(z_at, 0, block).start()
+        to_sibling(z_at, 0, 0, block).start()
+
+    def pass_a(k):
+        block = arrived(coming[k], 1, 0)
+        over_b(coming[k], 1, block).start()
+        to_sibling(coming[k], 1, 0, block).start()
+
+    def pass_b(k, da):
+        block = arrived(coming[k], da, 1)
+        to_sibling(coming[k], da, 1, block).start()
+
+    own = pltpu.make_async_copy(grad_hbm, spot(z, 0, 0), load_sem.at[5])
+    over_b(z, 0, grad_hbm).start()
+    over_a(z, grad_hbm).start()
+
+    @pl.when(z < 3)
+    def _():
+        up(z, grad_hbm).start()
+
+    @pl.when(z > 0)
+    def _():
+        down(z, grad_hbm).start()
+
+    to_sibling(z, 0, 0, grad_hbm).start()
+    own.start()
+
+    t_x.wait_recv()
+    theirs = quarter(tp + 2 - 4 * x)
+    t_f = remote(theirs, theirs, t_send.at[2], t_recv.at[2], sibling)
+    t_f.start()
+    loads[0].wait()
+    t_s.wait_recv()
+    t_f.wait_recv()
+
+    def by_rows(step, body):
+        def one(i, carry):
+            body(pl.ds(pl.multiple_of(i * step, step), step))
+            return carry
+
+        lax.fori_loop(0, rows // step, one, 0)
+
+    def norm_one(span):
+        values = tokens[span, :].astype(full)
+        inv = lax.rsqrt(jnp.mean(values * values, axis=1, keepdims=True) + norm_eps)
+        n1_ref[span, :] = (values * inv * first_ref[:1, :]).astype(low)
+        inv_one_ref[span, :] = jnp.broadcast_to(inv, (inv.shape[0], 128))
+
+    by_rows(32, norm_one)
+    pass_z(1)
+    pass_a(0)
+
+    def project(weights, bias_at):
+        def one(i, carry):
+            cut = pl.ds(pl.multiple_of(i * 256, 256), 256)
+            lin[:, cut] = (
+                jnp.dot(n1_ref[...], weights[:, cut], preferred_element_type=full)
+                + bias_ref[bias_at : bias_at + 1, cut]
+            )
+            return carry
+
+        lax.fori_loop(0, cols // 256, one, 0)
+
+    def rotate_into(target):
+        def one(h, carry):
+            cut = pl.ds(pl.multiple_of(h * HD, HD), HD)
+            value = lin[:, cut]
+            turned = value * cos_ref[...] + pltpu.roll(value, HD // 2, 1) * sin_ref[...]
+            target[:, cut] = turned.astype(low)
+            return carry
+
+        lax.fori_loop(0, heads, one, 0)
+
+    loads[1].wait()
+    project(wk, 1)
+    rotate_into(k_ref)
+    loads[2].wait()
+    project(wv, 2)
+    v_ref[...] = lin[...].astype(low)
+    earlier = (
+        remote(k_ref, earlier_k, kv_send.at[0], kv_recv.at[0], beside),
+        remote(v_ref, earlier_v, kv_send.at[1], kv_recv.at[1], beside),
+    )
+
+    @pl.when(y == 0)
+    def _():
+        for copy in earlier:
+            copy.start()
+
+    pass_b(0, 0)
+    pass_z(2)
+    pass_a(1)
+    loads[3].wait()
+    project(wq, 0)
+    rotate_into(q_ref)
+
+    half = rows // 2
+    lane = lax.broadcasted_iota(jnp.int32, (1, 128), 1)
+
+    def pick(held, span, h):
+        return jnp.sum(jnp.where(lane == h, held[span, :], 0.0), axis=1, keepdims=True)
+
+    def put(held, span, h, value):
+        held[span, :] = jnp.where(lane == h, value, held[span, :])
+
+    most[...] = jnp.zeros_like(most)
+    weight[...] = jnp.ones_like(weight)
+
+    def local_head(h, carry):
+        cut = pl.ds(pl.multiple_of(h * HD, HD), HD)
+        for qb in range(2):
+            span, count = pl.ds(qb * half, half), (qb + 1) * half
+            scores = times_transpose(q_ref[span, cut], k_ref[:count, cut]) * score_scale
+            top = jnp.max(scores, axis=1, keepdims=True)
+            powers = jnp.exp(scores - top)
+            put(most, span, h, top)
+            put(weight, span, h, jnp.sum(powers, axis=1, keepdims=True))
+            total[span, cut] = jnp.dot(
+                powers.astype(low), v_ref[:count, cut], preferred_element_type=full
+            )
+        return carry
+
+    lax.fori_loop(0, heads, local_head, 0)
+    pass_z(3)
+    pass_a(2)
+    pass_b(0, 1)
+    pass_b(1, 0)
+
+    @pl.when(y == 0)
+    def _():
+        ke_ref[...] = jnp.zeros_like(ke_ref)
+        ve_ref[...] = jnp.zeros_like(ve_ref)
+
+    @pl.when(y == 1)
+    def _():
+        for copy in earlier:
+            copy.wait_recv()
+        ke_ref[...] = earlier_k[...]
+        ve_ref[...] = earlier_v[...]
+
+        def remote_head(h, carry):
+            cut = pl.ds(pl.multiple_of(h * HD, HD), HD)
+            for qb in range(2):
+                span = pl.ds(qb * half, half)
+                scores = times_transpose(q_ref[span, cut], ke_ref[:, cut]) * score_scale
+                before = pick(most, span, h)
+                top = jnp.maximum(before, jnp.max(scores, axis=1, keepdims=True))
+                powers = jnp.exp(scores - top)
+                shrink = jnp.exp(before - top)
+                put(most, span, h, top)
+                put(
+                    weight,
+                    span,
+                    h,
+                    pick(weight, span, h) * shrink + jnp.sum(powers, axis=1, keepdims=True),
+                )
+                total[span, cut] = total[span, cut] * shrink + jnp.dot(
+                    powers.astype(low), ve_ref[:, cut], preferred_element_type=full
+                )
+            return carry
+
+        lax.fori_loop(0, heads, remote_head, 0)
+
+    def finish_head(h, carry):
+        cut = pl.ds(pl.multiple_of(h * HD, HD), HD)
+        context_ref[:, cut] = (total[:, cut] / pick(weight, slice(None), h)).astype(low)
+        return carry
+
+    lax.fori_loop(0, heads, finish_head, 0)
+    log_ref[...] = most[...] + jnp.log(weight[...])
+
+    loads[4].wait()
+
+    def out_part(at_quarter, target):
+        cut = pl.ds(pl.multiple_of(at_quarter * cols, cols), cols)
+        target[...] = jnp.dot(context_ref[...], wo[:, cut], preferred_element_type=full).astype(low)
+
+    def part_to_sibling(i):
+        return remote(tp_staged.at[i], tp_sib.at[i], tp_send.at[i], tp_recv.at[i], sibling)
+
+    def part_of(i):
+        x_at = 1 - x + (2 * x - 1) * i
+        out_part(x_at * 2 + 1 - core, tp_staged.at[i])
+        part_to_sibling(i).start()
+        out_part(x_at * 2 + core, tp_mine.at[i])
+
+    out_x = remote(tp_mine.at[0], tp_x, tp_send.at[2], tp_recv.at[2], across)
+    part_of(0)
+    part_to_sibling(0).wait_recv()
+    add_blocks(tp_mine.at[0], [tp_sib.at[0]], rows)
+    out_x.start()
+    part_of(1)
+    pass_a(3)
+    pass_b(1, 1)
+    pass_b(2, 0)
+    part_to_sibling(1).wait_recv()
+    out_x.wait_recv()
+    own_cut = pl.ds(pl.multiple_of(tp * cols, cols), cols)
+
+    def sum_parts(span):
+        value = tokens[span, own_cut].astype(full) + (
+            tp_mine[1, span, :].astype(full)
+            + tp_sib[1, span, :].astype(full)
+            + tp_x[span, :].astype(full)
+        )
+        hidden_ref[span, :] = value
+        lin[span, :] = value * value
+
+    by_rows(64, sum_parts)
+
+    row_mine[0] = row_of(lin[...])
+    first = remote(row_mine.at[0], row_sib, row_send.at[0], row_recv.at[0], sibling)
+    first.start()
+    first.wait_recv()
+    row_mine[1] = row_mine[0] + row_sib[...]
+    second = remote(row_mine.at[1], row_x, row_send.at[1], row_recv.at[1], across)
+    second.start()
+    second.wait_recv()
+    squares = (row_mine[1] + row_x[...]).T[:, :1]
+    inv_two = lax.rsqrt(squares * (1.0 / model_dim) + norm_eps)
+    inv_ref[...] = jnp.broadcast_to(inv_two, (rows, 128))
+
+    def norm_two(span):
+        unit = hidden_ref[span, :] * inv_ref[span, :1]
+        unit_ref[span, :] = unit
+        normed_ref[span, :] = (unit * second_ref[:1, :]).astype(low)
+
+    by_rows(64, norm_two)
+
+    pass_b(2, 1)
+    pass_b(3, 0)
+    pass_b(3, 1)
+
+    def finish_sibling(i, carry):
+        block = spot(0, 0, 0)
+        copy = remote(block, block, s_sem.at[i], sib_sem.at[i], sibling)
+        copy.wait_recv()
+        copy.wait_send()
+        return carry
+
+    lax.fori_loop(0, 16, finish_sibling, 0)
+
+    def finish_links(i, carry):
+        over_a(i, grad_hbm).wait_send()
+        over_b(i, 0, grad_hbm).wait_send()
+        over_b(i, 1, grad_hbm).wait_send()
+
+        @pl.when((z < 3) & (i <= z))
+        def _():
+            up(i, grad_hbm).wait_send()
+
+        @pl.when((z > 0) & (i >= z))
+        def _():
+            down(i, grad_hbm).wait_send()
+
+        return carry
+
+    lax.fori_loop(0, 4, finish_links, 0)
+    own.wait()
+    for copy in (t_x, t_s, t_f, out_x, part_to_sibling(0), part_to_sibling(1), first, second):
+        copy.wait_send()
+
+    @pl.when(y == 0)
+    def _():
+        for copy in earlier:
+            copy.wait_send()
+
+
+def attend(vmem_args, hbm_args, cid):
+    rows, cols = hbm_args[0].shape
+    model_dim = vmem_args[0].shape[1]
+    low, full, dma = jnp.bfloat16, jnp.float32, pltpu.SemaphoreType.DMA
+    vmem, hbm = pl.BlockSpec(memory_space=pltpu.VMEM), pl.BlockSpec(memory_space=pl.ANY)
+
+    def buffers(*shape, dtype=low):
+        return pltpu.VMEM(shape, dtype)
+
+    def result(*shape, dtype=low):
+        return jax.ShapeDtypeStruct(shape, dtype)
+
+    return pl.pallas_call(
+        attend_kernel,
+        out_shape=[
+            result(rows, cols, dtype=full),
+            result(rows, cols, dtype=full),
+            result(rows, 128, dtype=full),
+            result(rows, cols),
+            result(rows, model_dim),
+            result(rows, 128, dtype=full),
+        ]
+        + [result(rows, cols)] * 6
+        + [result(rows, 128, dtype=full), result(8 * rows, model_dim)],
+        in_specs=[vmem] * len(vmem_args) + [hbm] * len(hbm_args),
+        out_specs=[vmem] * 13 + [hbm],
+        scratch_shapes=[buffers(*arg.shape) for arg in hbm_args[2:]]
+        + [
+            buffers(rows, model_dim),
+            buffers(rows, cols, dtype=full),
+            buffers(rows, cols, dtype=full),
+            buffers(rows, 128, dtype=full),
+            buffers(rows, 128, dtype=full),
+            buffers(rows, cols),
+            buffers(rows, cols),
+            buffers(2, rows, cols),
+            buffers(2, rows, cols),
+            buffers(2, rows, cols),
+            buffers(rows, cols),
+            buffers(2, 8, rows, dtype=full),
+            buffers(8, rows, dtype=full),
+            buffers(8, rows, dtype=full),
+        ]
+        + [dma((6,)), dma((3,)), dma((3,)), dma((2,)), dma((2,)), dma((3,)), dma((3,))]
+        + [dma((2,)), dma((2,))]
+        + [dma((4,)), dma((4,)), dma((4,)), dma((8,)), dma((16,)), dma((16,)), dma((16,))],
+        compiler_params=pltpu.CompilerParams(
+            collective_id=cid, has_side_effects=True, vmem_limit_bytes=60 * 2**20
+        ),
+        name="attend",
+    )(*vmem_args, *hbm_args)
 
 
 def kept_choice(expert_ids, pair_order, expert_total, capacity):
@@ -2317,10 +2782,12 @@
     turn = jnp.sum(jnp.where(order[None, :] == pairs[:, None], pairs[None, :], 0), axis=1)
     turn = turn.reshape(tok_count, top_count)
     picked = expert_ids[:, :, None] == jnp.arange(expert_total, dtype=jnp.int32)[None, None, :]
-    turn_of = jnp.sum(jnp.where(picked, turn[:, :, None], 0), axis=1)
+    experts_apart = jnp.arange(expert_total, dtype=jnp.int32)[:, None, None]
+    picked = expert_ids.T[None] == experts_apart
     named = jnp.any(picked, axis=1)
+    turn_of = jnp.sum(jnp.where(picked, turn.T[None], 0), axis=1)
     turn_of = jnp.where(named, turn_of, pair_count)
-    slot = jnp.sum((turn_of[None, :, :] < turn_of[:, None, :]).astype(jnp.int32), axis=1)
+    slot = jnp.sum((turn_of[:, None, :] < turn_of[:, :, None]).astype(jnp.int32), axis=2)
     return (named & (slot < capacity)).astype(jnp.float32)
 
 
@@ -2352,11 +2819,9 @@
     model_dim = query_weight.shape[0]
     sources = lax.axis_size("ep")
     place_in_seq = ep % SPAN
-    has_earlier = place_in_seq > 0
     expert_total = router_weight.shape[1]
     capacity = 9 * tok_count * expert_ids.shape[1] // (8 * expert_total)
     head_count = query_weight.shape[1] // HD
-    score_scale = HD ** (-0.5)
     expert_width = expert_gate_weight.shape[2]
     shared_width = shared_gate_weight.shape[1] // sources
     width = expert_width + shared_width
@@ -2365,61 +2830,42 @@
         return lax.dynamic_slice_in_dim(vector, tp * col_width, col_width, vector.ndim - 1)
 
     kept_own = kept_choice(expert_ids, pair_order, expert_total, capacity)
-    grads_all = gather_all(out_grad, 2)
-
-    inputs_full = gather_tp(tokens, 0).astype(jnp.float32)
-    unit_one, inv_one = row_stats(inputs_full)
-    normed_one = (unit_one * first_gain).astype(jnp.bfloat16)
-    query_lin = jnp.dot(normed_one, query_weight, preferred_element_type=jnp.float32) + query_bias
-    key_lin = jnp.dot(normed_one, key_weight, preferred_element_type=jnp.float32) + key_bias
-    value_lin = jnp.dot(normed_one, value_weight, preferred_element_type=jnp.float32) + value_bias
+
+    def tall(vector):
+        return jnp.broadcast_to(vector[None, :], (8, vector.shape[0]))
+
     cosine, sine_part = rope_tables(tok_count, HD, place_in_seq * tok_count)
-    queries = rotate(query_lin.reshape(tok_count, head_count, HD), cosine, sine_part).astype(
-        jnp.bfloat16
-    )
-    keys_rot = rotate(key_lin.reshape(tok_count, head_count, HD), cosine, sine_part).astype(
-        jnp.bfloat16
-    )
-    values_all = value_lin.reshape(tok_count, head_count, HD).astype(jnp.bfloat16)
-    earlier_keys, earlier_values = passed_along((keys_rot, values_all), "ep", 1)
-    keys_both = jnp.concatenate([earlier_keys, keys_rot], axis=0)
-    values_both = jnp.concatenate([earlier_values, values_all], axis=0)
-    blocks = jnp.arange(tok_count) // BLOCK
-    local_allowed = blocks[None, :] <= blocks[:, None]
-    remote_allowed = jnp.broadcast_to(has_earlier, (tok_count, tok_count))
-    allowed = jnp.concatenate([remote_allowed, local_allowed], axis=1)[None]
-
-    def attention_scores():
-        scored = (
-            jnp.einsum("qhd,khd->hqk", queries, keys_both, preferred_element_type=jnp.float32)
-            * score_scale
-        )
-        return jnp.where(allowed, scored, masked_score)
-
-    scores = attention_scores()
-    row_max = jnp.max(scores, axis=-1, keepdims=True)
-    powers = jnp.exp(scores - row_max)
-    totals = jnp.sum(powers, axis=-1, keepdims=True)
-    log_total = row_max + jnp.log(totals)
-    probs_low = (powers / totals).astype(jnp.bfloat16)
-    context = jnp.einsum("hqk,khd->qhd", probs_low, values_both, preferred_element_type=jnp.float32)
-    context = context.reshape(tok_count, head_count * HD).astype(jnp.bfloat16)
-    attn_part = jnp.dot(context, output_weight, preferred_element_type=jnp.float32)
-    attended = scatter_tp(attn_part.astype(jnp.bfloat16), 1)
-
-    hidden_cols = tokens.astype(jnp.float32) + attended
-    squares = tp_total(jnp.sum(hidden_cols * hidden_cols, axis=-1, keepdims=True))
-    inv_two = lax.rsqrt(squares / model_dim + norm_eps)
-    unit_two = hidden_cols * inv_two
+    cos_wide = jnp.concatenate([cosine[:, 0], cosine[:, 0]], axis=1)
+    sin_wide = jnp.concatenate([-sine_part[:, 0], sine_part[:, 0]], axis=1)
     second_cols = own_cols(second_gain)
-    normed_cols = (unit_two * second_cols).astype(jnp.bfloat16)
+    biases = jnp.pad(jnp.stack([query_bias, key_bias, value_bias]), ((0, 5), (0, 0)))
+    (
+        hidden_cols,
+        unit_two,
+        inv_two,
+        normed_cols,
+        normed_one,
+        inv_one,
+        queries,
+        keys_rot,
+        values_all,
+        earlier_keys,
+        earlier_values,
+        context,
+        log_rows,
+        grads_all,
+    ) = attend(
+        [tall(first_gain), biases, tall(second_cols), cos_wide, sin_wide],
+        [tokens, out_grad, query_weight, key_weight, value_weight, output_weight],
+        2,
+    )
 
     def shared_rows(weight):
         return lax.dynamic_slice_in_dim(weight, ep * shared_width, shared_width, 1).T
 
     extra_rows = jnp.concatenate([router_weight.T, switch_vector[None, :]], axis=0)
     extra_rows = jnp.pad(extra_rows, ((0, 16 - extra_rows.shape[0]), (0, 0)))
-    kept_rows = jnp.pad(kept_own.T, ((0, 16 - expert_total), (0, 0))).astype(jnp.bfloat16)
+    kept_rows = jnp.pad(kept_own, ((0, 16 - expert_total), (0, 0))).astype(jnp.bfloat16)
     reduced, ffn_cols, logit_tile, expert_grads, shared_parts, *_ = experts(
         normed_cols,
         grads_all,
@@ -2445,7 +2891,7 @@
     shared_down_grad = shared_parts[0]
 
     normed_grad = reduced[:tok_count]
-    probs_grad = reduced[tok_count : tok_count + expert_total].T * kept_own
+    probs_grad = (reduced[tok_count : tok_count + expert_total] * kept_own).T
     switch_grad = reduced[tok_count + expert_total]
     logit_at = width % 128
     probs_own = softmax_rows(logit_tile[:, logit_at : logit_at + expert_total])
@@ -2464,39 +2910,27 @@
     )
     second_gain_grad = jnp.sum(normed_grad * unit_two, axis=0)
 
-    def wide(column):
-        return jnp.broadcast_to(column, (tok_count, 128))
-
-    def tall(vector):
-        return jnp.broadcast_to(vector[None, :], (8, vector.shape[0]))
-
-    def flat(heads_apart):
-        return heads_apart.reshape(tok_count, head_count * HD)
-
     small = jnp.concatenate(
         [second_gain_grad[None], switch_vector_grad[None], router_grad.T], axis=0
     )
     small_rows = small.shape[0]
     small = jnp.pad(small, ((4, 12 - small_rows), (0, 0)))
-    log_rows = jnp.pad(log_total[:, :, 0].T, ((0, 0), (0, 128 - head_count)))
-    cos_wide = jnp.concatenate([cosine[:, 0], cosine[:, 0]], axis=1)
-    sin_wide = jnp.concatenate([-sine_part[:, 0], sine_part[:, 0]], axis=1)
     tokens_grad, weight_grads, sums = unwind(
         [
             normed_grad,
             unit_two,
-            wide(inv_two),
+            inv_two,
             tall(second_cols),
             out_grad,
             tokens,
-            wide(inv_one),
+            inv_one,
             tall(own_cols(first_gain)),
             small,
-            flat(queries),
-            flat(keys_rot),
-            flat(values_all),
-            flat(earlier_keys),
-            flat(earlier_values),
+            queries,
+            keys_rot,
+            values_all,
+            earlier_keys,
+            earlier_values,
             context,
             log_rows,
             cos_wide,

time: 731 us -> 658 us (0.900)
  other arithmetic: 33.6 us -> 11.8 us
  local copies, waits for them, and re-layouts: 47.7 us -> 30.1 us
  matrix products: 20.7 us -> 4 us
  Pallas kernels: 588 us -> 576 us
    dot_general x6 -> x0, matrix products: 17 us -> none  [the longest x1 5.37 us: dense_plan(): jnp.einsum('hqk,khd->qhd', probs_low, values_both, preferred_element_type...]
    reduce_sum x5 -> x2, other arithmetic: 14.2 us -> 1.37 us  [the longest x1 1.35 us: kept_choice(): jnp.sum((turn_of[:, None, :] < turn_of[:, :, None]).astype(jnp.int32), ax...]
    pallas_call x3 -> x1, Pallas kernels: 109 us -> 104 us  [attend(): pl.pallas_call(attend_kernel, out_shape=[result(rows, cols, dtype=full),...]
  transfers between devices with their start and end apart: 3 -> 1, of which waited for: 0 -> 0; matrix products, arithmetic and copies ran while one was open for 10% -> 4% of each run, Pallas kernels for 34% -> 26%
where the time goes in v4:
time: 658 us; the launch traced here: 649 us
  Pallas kernels  576 us (88%)
  local copies, waits for them, and re-layouts  30.1 us (5%)
  starting transfers between devices  19.8 us (3%)
  other arithmetic  11.8 us (2%)
    pallas_call x1, Pallas kernels, experts(): pl.pallas_call(functools.partial(experts_kernel, expert_width, shared_wid...  306 us
    pallas_call x1, Pallas kernels, unwind(): pl.pallas_call(unwind_kernel, out_shape=[jax.ShapeDtypeStruct((rows, cols...  166 us
    pallas_call x1, Pallas kernels, attend(): pl.pallas_call(attend_kernel, out_shape=[result(rows, cols, dtype=full),...  104 us
    all_to_all x1, starting transfers between devices, dense_plan(): lax.all_to_all(shared_parts, 'ep', split_axis=0, concat_axis=0, tiled=True)  19.8 us
  transfers between devices with their start and end apart: 1, of which 0 were waited for; matrix products, arithmetic and copies ran while one was open for 4% of the time, Pallas kernels for 26%

profile of v4, /device:TPU:9, one launch (start us, length us, event | category | flops | bytes accessed | tf_op | source)
XLA Modules:
  0.0 649.3 jit_solution(11713560568210086725)
XLA Ops:
  0.7 3.0 constant_dynamic-slice_fusion.1
  3.8 1.2 copy.74
  5.0 1.2 copy.73
  6.2 1.8 select_reduce_fusion
  8.4 1.4 convert_reduce_fusion
  10.4 1.0 fusion.3
  11.4 0.8 dynamic_slice.24
  12.2 0.6 fusion.4.extra_ref
  12.8 1.0 pad_maximum_fusion
  15.7 104.1 %attend.1 = (f32[512,512]{1,0:T(8,128)}, f32[512,512]{1,0:T(8,128)}, f32[512,128]{1,0:T(8,128)}, bf16[512,512]{1,0:T(8,128)(2,1)}, bf16[512,2048]{1,0:T(8,128)(2...) custom-call(f32[8,2048]{1,0:T(8,128)} %broadcast_in_dim.44.first_ref, ...), custom_call_target="tpu_custom_call" | custom-call | tf_op jit(solution)/shard_map/attend/pallas_call | solution.py:2736
  119.8 306.2 %experts.1 = (f32[528,512]{1,0:T(8,128)}, f32[512,512]{1,0:T(8,128)}, f32[512,128]{1,0:T(8,128)}, f32[3,352,2048]{2,1,0:T(8,128)}, bf16[8,3,176,256]{3,2,1,0:T(8...) custom-call(bf16[512,512]{1,0:T(8,128)(2,1)} %get-tuple-element.42.x, ...), custom_call_target="tpu_custom_call" | custom-call | tf_op jit(solution)/shard_map/experts/pallas_call | solution.py:1728
  426.0 19.8 %all-to-all-start = ((bf16[8,3,176,256]{3,2,1,0:T(8,128)(2,1)}), bf16[8,3,176,256]{3,2,1,0:T(8,128)(2,1)S(1)}, u32[]{:S(2)}, u32[]{:S(2)}) async-start(bf16[8,3,176,256]{3,2,1,0:T(8,128)(2,1)} %get-tuple-element.61), calls=%async_computation | async-start | bytes 4325376 | tf_op jit(solution)/shard_map/all_to_all | solution.py:2886
  445.8 0.7 fusion.17
  447.0 0.7 fusion.8
  448.2 0.9 fusion.19
  449.1 2.9 multiply_reduce_fusion
  453.3 165.7 %unwind.1 = (bf16[512,512]{1,0:T(8,128)(2,1)}, f32[4,256,512]{2,1,0:T(8,128)}, f32[16,512]{1,0:T(8,128)}) custom-call(f32[512,512]{1,0:T(8,128)} %get-tuple-element.163.dn2_ref, f32[512,512]{1,0:T(8,128)} %get-tuple-element.47.unit_ref, f32[512,128]{1,0:T(8,128)} %get-tuple-element.48.inv_ref, f32[8,512]{1,0:T(8,128)} %broadcast_in_dim.45.second_ref, ...), custom_call_target="tpu_custom_call" | custom-call | tf_op jit(solution)/shard_map/unwind/pallas_call | solution.py:2262
  619.1 0.8 slice.84
  619.8 0.7 slice.83
  620.5 0.7 slice.89
  621.3 2.7 slice_bitcast_fusion.2
  624.0 1.0 copy.72
  625.0 6.3 all_gather.3
  631.2 0.6 fusion.18
  631.9 0.7 dynamic-slice_bitcast_fusion.1
  632.5 0.7 dynamic-slice_bitcast_fusion
  633.2 2.5 add_convert_fusion
  635.7 7.3 %fusion.15 = (f32[1,352,2048]{2,1,0:T(8,128)}, f32[1,2048,352]{1,2,0:T(8,128)}, f32[1,2048,352]{1,2,0:T(8,128)}) fusion(f32[3,352,2048]{2,1,0:T(8,128)} %get-tuple-element.62), kind=kLoop, calls=%fused_computation.65 | loop fusion | bytes 17301504 | tf_op jit(solution)/shard_map/slice | solution.py:2969
  643.5 1.5 fusion.16
  645.0 1.5 copy.70
  646.6 1.5 copy.71
  648.1 0.8 copy.76
  (50 shorter events, 5.7 us)
Async XLA Ops:
  0.7 5.5 copy-start.4
  0.7 5.5 copy-start.10
  3.7 6.7 %copy-start.6 = (bf16[2048]{0:T(1024)(128)(2,1)S(1)}, bf16[2048]{0:T(1024)(128)(2,1)}, u32[]{:S(2)}) copy-start(bf16[2048]{0:T(1024)(128)(2,1)} %param.36) | copy-start | bytes 12292
  3.7 8.4 %copy-start.3 = (bf16[2048,8]{0,1:T(8,128)(2,1)S(1)}, bf16[2048,8]{0,1:T(8,128)(2,1)}, u32[]{:S(2)}) copy-start(bf16[2048,8]{0,1:T(8,128)(2,1)} %param.32) | copy-start | bytes 98308
  3.7 10.1 %copy-start.7 = (f32[512]{0:T(512)S(1)}, f32[512]{0:T(512)}, u32[]{:S(2)}) copy-start(f32[512]{0:T(512)} %param.29) | copy-start | bytes 6148
  3.7 10.1 %copy-start.8 = (f32[512]{0:T(512)S(1)}, f32[512]{0:T(512)}, u32[]{:S(2)}) copy-start(f32[512]{0:T(512)} %param.28) | copy-start | bytes 6148
  3.8 10.1 %copy-start.9 = (f32[512]{0:T(512)S(1)}, f32[512]{0:T(512)}, u32[]{:S(2)}) copy-start(f32[512]{0:T(512)} %param.27) | copy-start | bytes 6148
  3.8 11.3 %copy-start.5 = (f32[2048]{0:T(1024)S(1)}, f32[2048]{0:T(1024)}, u32[]{:S(2)}) copy-start(f32[2048]{0:T(1024)} %param.23) | copy-start | bytes 24580
  426.0 20.7 %copy-start.1 = (f32[512,128]{1,0:T(8,128)S(1)}, f32[512,128]{1,0:T(8,128)}, u32[]{:S(2)}) copy-start(f32[512,128]{1,0:T(8,128)} %get-tuple-element.46) | copy-start | bytes 786436
  426.0 22.1 %copy-start = (bf16[512,512]{1,0:T(8,128)(2,1)S(1)}, bf16[512,512]{1,0:T(8,128)(2,1)}, u32[]{:S(2)}) copy-start(bf16[512,512]{1,0:T(8,128)(2,1)} %get-tuple-element.42.x_ref) | copy-start | bytes 1572868
  426.0 217.1 %all-to-all-start = ((bf16[8,3,176,256]{3,2,1,0:T(8,128)(2,1)}), bf16[8,3,176,256]{3,2,1,0:T(8,128)(2,1)S(1)}, u32[]{:S(2)}, u32[]{:S(2)}) async-start(bf16[8,3,176,256]{3,2,1,0:T(8,128)(2,1)} %get-tuple-element.61), calls=%async_computation | async-start | bytes 4325376 | tf_op jit(solution)/shard_map/all_to_all | solution.py:2886
  645.0 3.1 copy-start.2

commit v5 on v4

--- a/solution.py
+++ b/solution.py
@@ -1172,7 +1172,7 @@
         )
 
     coming = (z, choose(1, 0, 3, 2), choose(2, 2, 1, 1), choose(3, 3, 0, 0))
-    turns = (z, choose(2, 0, 3, 1), choose(3, 3, 0, 0), choose(1, 2, 1, 2))
+    turns = (z, choose(1, 0, 3, 2), choose(3, 3, 0, 0), choose(2, 2, 1, 1))
 
     def arrived(z_at, da, db):
         block, n = spot(z_at, da, db), at(z_at, da, db)
@@ -1212,9 +1212,10 @@
         over_b(z_at, 0, block).start()
         to_sibling(z_at, 0, 0, block).start()
 
-    def pass_a(z_at):
+    def pass_a(z_at, onward=True):
         block = arrived(z_at, 1, 0)
-        over_b(z_at, 1, block).start()
+        if onward:
+            over_b(z_at, 1, block).start()
         to_sibling(z_at, 1, 0, block).start()
 
     def pass_b(z_at, da):
@@ -1342,14 +1343,24 @@
         for dx in range(2):
             rs_sibling(k, dx, dy).wait_send()
 
-    def rs_over_b(k, da):
-        n = turns[k] * 2 + da
-        return remote(mine.at[hold(k, da, 1)], from_b.at[n], rb_send.at[n], rb_recv.at[n], peer_b)
-
-    def rs_over_a(k):
-        z_at = turns[k]
+    def rs_over_b(k, da, part):
+        n, span = turns[k] * 2 + da, pl.ds(*cuts[part])
         return remote(
-            mine.at[hold(k, 1, 0)], from_a.at[z_at], ra_send.at[z_at], ra_recv.at[z_at], peer_a
+            mine.at[hold(k, da, 1), span],
+            from_b.at[n, span],
+            rb_send.at[n * 2 + part],
+            rb_recv.at[n * 2 + part],
+            peer_b,
+        )
+
+    def rs_over_a(k, part):
+        z_at, span = turns[k], pl.ds(*cuts[part])
+        return remote(
+            mine.at[hold(k, 1, 0), span],
+            from_a.at[z_at, span],
+            ra_send.at[z_at * 2 + part],
+            ra_recv.at[z_at * 2 + part],
+            peer_a,
         )
 
     def rs_up(k, z_at, half):
@@ -1375,77 +1386,86 @@
         span = pl.ds(*cuts[half])
         return pltpu.make_async_copy(source.at[span], landed.at[i, span], fetch_sem.at[i])
 
-    def reduce_sibling(k, dy):
-        spots = []
+    def fetch_sibling(k, dy):
         for dx in range(2):
             n = at(turns[k], *lane_offsets(dx, dy, core))
             remote(staged.at[0], from_sib.at[n], rs_send.at[n], rs_recv.at[n], sibling).wait_recv()
             fetch(from_sib.at[n], dx).start()
-            spots.append(n)
+
+    def reduce_sibling(k, dy):
         for dx in range(2):
-            fetch(from_sib.at[spots[dx]], dx).wait()
+            n = at(turns[k], *lane_offsets(dx, dy, core))
+            fetch(from_sib.at[n], dx).wait()
             add_blocks(mine.at[hold(k, *lane_offsets(dx, dy, core))], [landed.at[dx]], tall)
 
-        @pl.when(core == 0)
+        for part in range(2):
+
+            @pl.when(core == 0)
+            def _(part=part):
+                rs_over_b(k, dy, part).start()
+
+            if dy == 1:
+
+                @pl.when(core == 1)
+                def _(part=part):
+                    rs_over_b(k, 0, part).start()
+                    rs_over_b(k, 1, part).start()
+
+    def add_part(target, part, copies):
+        first, count = cuts[part]
+        span = pl.ds(first, count)
+        for copy in copies:
+            copy.wait()
+        add_blocks(
+            mine.at[target, span], [landed.at[i, span] for i in range(len(copies))], count
+        )
+
+    def reduce_b(k, part):
+        rs_over_b(k, 1, part).wait_recv()
+        copy = fetch_part(from_b.at[turns[k] * 2 + 1], part, 0)
+        copy.start()
+        add_part(hold(k, 1, 0), part, [copy])
+        rs_over_a(k, part).start()
+
+    def reduce_a(k, part):
+        z_at = turns[k]
+        rs_over_b(k, 0, part).wait_recv()
+        rs_over_a(k, part).wait_recv()
+        copies = [
+            fetch_part(from_b.at[z_at * 2], part, 0),
+            fetch_part(from_a.at[z_at], part, 1),
+        ]
+        for copy in copies:
+            copy.start()
+        add_part(k, part, copies)
+        if k > 0:
+
+            @pl.when(z == 0)
+            def _():
+                rs_up(k, z_at, part).start()
+
+            @pl.when(z == 3)
+            def _():
+                rs_down(k, z_at, part).start()
+
+    def chain(k, part):
+        z_at = turns[k]
+
+        @pl.when((z > 0) & (z < 3) & (z_at > z))
         def _():
-            rs_over_b(k, dy).start()
-
-        if dy == 1:
-
-            @pl.when(core == 1)
-            def _():
-                rs_over_b(k, 0).start()
-                rs_over_b(k, 1).start()
-
-    def reduce_b(k):
-        rs_over_b(k, 1).wait_recv()
-        source = from_b.at[turns[k] * 2 + 1]
-        fetch(source, 0).start()
-        fetch(source, 0).wait()
-        add_blocks(mine.at[hold(k, 1, 0)], [landed.at[0]], tall)
-        rs_over_a(k).start()
-
-    def reduce_a(k):
-        z_at = turns[k]
-        rs_over_b(k, 0).wait_recv()
-        fetch(from_b.at[z_at * 2], 0).start()
-        rs_over_a(k).wait_recv()
-        fetch(from_a.at[z_at], 1).start()
-        fetch(from_b.at[z_at * 2], 0).wait()
-        fetch(from_a.at[z_at], 1).wait()
-        add_blocks(mine.at[k], [landed.at[0], landed.at[1]], tall)
-        if k > 0:
-            for half in range(2):
-
-                @pl.when(z == 0)
-                def _(half=half):
-                    rs_up(k, z_at, half).start()
-
-                @pl.when(z == 3)
-                def _(half=half):
-                    rs_down(k, z_at, half).start()
-
-    def chain(k):
-        z_at = turns[k]
-        first, count = cuts[0]
-        for half, (first, count) in enumerate(cuts):
-            span = pl.ds(first, count)
-
-            @pl.when((z > 0) & (z < 3) & (z_at > z))
-            def _(half=half, span=span, count=count):
-                rs_up(k, z_at, half).wait_recv()
-                fetch_part(from_below.at[z_at], half, half).start()
-                fetch_part(from_below.at[z_at], half, half).wait()
-                add_blocks(mine.at[k, span], [landed.at[half, span]], count)
-                rs_up(k, z_at, half).start()
-
-            @pl.when((z > 0) & (z < 3) & (z_at < z))
-            def _(half=half, span=span, count=count):
-                rs_down(k, z_at, half).wait_recv()
-                fetch_part(from_above.at[z_at], half, half).start()
-                fetch_part(from_above.at[z_at], half, half).wait()
-                add_blocks(mine.at[k, span], [landed.at[half, span]], count)
-                rs_down(k, z_at, half).start()
+            rs_up(k, z_at, part).wait_recv()
+            copy = fetch_part(from_below.at[z_at], part, 0)
+            copy.start()
+            add_part(k, part, [copy])
+            rs_up(k, z_at, part).start()
+
+        @pl.when((z > 0) & (z < 3) & (z_at < z))
+        def _():
+            rs_down(k, z_at, part).wait_recv()
+            copy = fetch_part(from_above.at[z_at], part, 0)
+            copy.start()
+            add_part(k, part, [copy])
+            rs_down(k, z_at, part).start()
 
     tile = x_tile.shape[1]
 
@@ -1548,59 +1568,83 @@
         load_x(k, dy).start()
 
     order = [(0, 0)] + [(k, dy) for k in range(1, 4) for dy in range(2)] + [(0, 1)]
-    pass_a(z)
+    edge = (z == 0) | (z == 3)
+    pass_z(coming[1])
+    pass_a(z, False)
     pass_b(z, 0)
+
+    @pl.when(jnp.logical_not(edge))
+    def _():
+        pass_z(coming[2])
+
     ready(0, 0)
     for s, (k, dy) in enumerate(order):
         following = order[s + 1] if s < 7 else None
         load_x(k, dy).wait()
+        if s >= 1:
+            fetch_sibling(*order[s - 1])
         project()
-        if s == 0:
-            pass_z(coming[1])
         if s >= 1:
             load_g(k, dy).wait()
             project_grad()
         if following is not None:
             load_g(*following).start()
+        if s >= 1:
+            reduce_sibling(*order[s - 1])
+        if s == 1:
+            pass_z(coming[3])
+            over_b(z, 1, spot(z, 1, 0)).start()
+        if s in (4, 6):
+            reduce_b(s // 2 - 1, 0)
+        activate(k, dy)
         if s == 0:
-            pass_z(coming[2])
-            pass_b(z, 1)
+
+            @pl.when(edge)
+            def _():
+                pass_z(coming[2])
+
             pass_a(coming[1])
         if s == 1:
-            pass_z(coming[3])
-        if s >= 1:
-            reduce_sibling(*order[s - 1])
-        if s in (4, 6):
-            reduce_b(s // 2 - 1)
-        activate(k, dy)
-        if s == 0:
             pass_a(coming[2])
         if s == 2:
             pass_a(coming[3])
+        if s == 4:
+            pass_b(z, 1)
         if following is not None:
             ready(*following)
+        if s in (4, 6):
+            reduce_b(s // 2 - 1, 1)
         if s in (5, 7):
-            reduce_a((s - 3) // 2)
+            reduce_a((s - 3) // 2, 0)
         if s >= 1:
             staged_free(*order[s - 1])
         if s == 5:
-            for da in range(2):
-                rs_over_b(1, da).wait_send()
-            rs_over_a(1).wait_send()
+            for part in range(2):
+                for da in range(2):
+                    rs_over_b(1, da, part).wait_send()
+                rs_over_a(1, part).wait_send()
         block_rows(k, dy)
+        if s in (5, 7):
+            reduce_a((s - 3) // 2, 1)
 
     load_tile(g_ref, g_tile, 0, 2).start()
     load_tile(all_ref, x_tile, 0, 3).start()
     tiles = shared_grads_ref.shape[0]
     services = {
+        (0, 0): lambda: fetch_sibling(0, 1),
         (0, 1): lambda: reduce_sibling(0, 1),
-        (0, 2): lambda: chain(2),
-        (1, 1): lambda: reduce_b(3),
-        (1, 2): lambda: reduce_b(0),
-        (2, 0): lambda: chain(1),
-        (3, 0): lambda: reduce_a(3),
-        (4, 0): lambda: chain(3),
-        (5, 1): lambda: reduce_a(0),
+        (0, 2): lambda: chain(2, 0),
+        (1, 0): lambda: reduce_b(3, 0),
+        (1, 1): lambda: chain(2, 1),
+        (2, 0): lambda: chain(1, 0),
+        (2, 2): lambda: chain(1, 1),
+        (4, 0): lambda: reduce_b(3, 1),
+        (4, 2): lambda: reduce_a(3, 0),
+        (5, 1): lambda: reduce_b(0, 0),
+        (6, 0): lambda: chain(3, 0),
+        (6, 2): lambda: reduce_a(3, 1),
+        (7, 0): lambda: reduce_b(0, 1),
+        (7, 2): lambda: chain(3, 1),
     }
 
     def tile_step(t, carry):
@@ -1627,6 +1671,9 @@
     for kind in range(3):
         for copy in tile_stores(tiles - 1, kind):
             copy.wait()
+
+    reduce_a(0, 0)
+    reduce_a(0, 1)
 
     for half in range(2):
 
@@ -1675,9 +1722,10 @@
         kept_to(i).wait_send()
     staged_free(0, 1)
     for k in (0, 2, 3):
-        rs_over_a(k).wait_send()
-        for da in range(2):
-            rs_over_b(k, da).wait_send()
+        for part in range(2):
+            rs_over_a(k, part).wait_send()
+            for da in range(2):
+                rs_over_b(k, da, part).wait_send()
 
     def finish(i, carry):
         over_a(i, x_ref).wait_send()
@@ -1764,8 +1812,8 @@
         ]
         + [dma((4,)), dma((4,)), dma((4,)), dma((8,)), dma((16,)), dma((16,)), dma((16,)), dma]
         + [dma((4,)), dma((2,)), dma((6,)), dma((8,)), dma((7,)), dma((7,))]
-        + [dma((16,)), dma((16,)), dma((8,)), dma((8,)), dma((4,)), dma((4,))]
-        + [dma((8,))] * 4,
+        + [dma((16,))] * 4
+        + [dma((8,))] * 6,
         compiler_params=pltpu.CompilerParams(
             collective_id=cid, has_side_effects=True, vmem_limit_bytes=63 * 2**20
         ),
@@ -2422,14 +2470,18 @@
         remote(block, block, s_sem.at[n], recv_sem.at[n], sibling).wait_recv()
         return block
 
-    def up(z_at, source):
-        return remote(source, spot(z_at, 0, 0), up_sem.at[z_at], recv_sem.at[at(z_at, 0, 0)], above)
-
-    def down(z_at, source):
-        return remote(source, spot(z_at, 0, 0), down_sem.at[z_at], recv_sem.at[at(z_at, 0, 0)], below)
-
-    def over_a(z_at, source):
-        return remote(source, spot(z_at, 0, 0), a_sem.at[z_at], recv_sem.at[at(z_at, 1, 0)], peer_a)
+    def up(z_at, da, source):
+        n = z_at * 2 + da
+        target = recv_sem.at[at(z_at, da, 0)]
+        return remote(source, spot(z_at, da, 0), up_sem.at[n], target, above)
+
+    def down(z_at, da, source):
+        n = z_at * 2 + da
+        target = recv_sem.at[at(z_at, da, 0)]
+        return remote(source, spot(z_at, da, 0), down_sem.at[n], target, below)
+
+    def over_a(source):
+        return remote(source, spot(z, 0, 0), a_sem, recv_sem.at[at(z, 1, 0)], peer_a)
 
     def over_b(z_at, da, source):
         return remote(
@@ -2440,43 +2492,44 @@
         n = at(z_at, da, db)
         return remote(source, spot(z_at, da, db), s_sem.at[n], sib_sem.at[n], sibling)
 
-    def pass_z(k):
+    def along_z(da, source):
+        @pl.when(z < 3)
+        def _():
+            up(z, da, source).start()
+
+        @pl.when(z > 0)
+        def _():
+            down(z, da, source).start()
+
+    def pass_a():
+        block = arrived(z, 1, 0)
+        along_z(1, block)
+        over_b(z, 1, block).start()
+        to_sibling(z, 1, 0, block).start()
+
+    def pass_z(k, da):
         z_at = coming[k]
-        block = arrived(z_at, 0, 0)
+        block = arrived(z_at, da, 0)
 
         @pl.when((z_at > z) & (z > 0))
         def _():
-            down(z_at, block).start()
+            down(z_at, da, block).start()
 
         @pl.when((z_at < z) & (z < 3))
         def _():
-            up(z_at, block).start()
-
-        over_a(z_at, block).start()
-        over_b(z_at, 0, block).start()
-        to_sibling(z_at, 0, 0, block).start()
-
-    def pass_a(k):
-        block = arrived(coming[k], 1, 0)
-        over_b(coming[k], 1, block).start()
-        to_sibling(coming[k], 1, 0, block).start()
+            up(z_at, da, block).start()
+
+        over_b(z_at, da, block).start()
+        to_sibling(z_at, da, 0, block).start()
 
     def pass_b(k, da):
         block = arrived(coming[k], da, 1)
         to_sibling(coming[k], da, 1, block).start()
 
     own = pltpu.make_async_copy(grad_hbm, spot(z, 0, 0), load_sem.at[5])
+    over_a(grad_hbm).start()
+    along_z(0, grad_hbm)
     over_b(z, 0, grad_hbm).start()
-    over_a(z, grad_hbm).start()
-
-    @pl.when(z < 3)
-    def _():
-        up(z, grad_hbm).start()
-
-    @pl.when(z > 0)
-    def _():
-        down(z, grad_hbm).start()
-
     to_sibling(z, 0, 0, grad_hbm).start()
     own.start()
 
@@ -2502,8 +2555,8 @@
         inv_one_ref[span, :] = jnp.broadcast_to(inv, (inv.shape[0], 128))
 
     by_rows(32, norm_one)
-    pass_z(1)
-    pass_a(0)
+    pass_a()
+    pass_z(1, 0)
 
     def project(weights, bias_at):
         def one(i, carry):
@@ -2543,8 +2596,8 @@
             copy.start()
 
     pass_b(0, 0)
-    pass_z(2)
-    pass_a(1)
+    pass_z(2, 0)
+    pass_z(1, 1)
     loads[3].wait()
     project(wq, 0)
     rotate_into(q_ref)
@@ -2576,8 +2629,8 @@
         return carry
 
     lax.fori_loop(0, heads, local_head, 0)
-    pass_z(3)
-    pass_a(2)
+    pass_z(2, 1)
+    pass_z(3, 0)
     pass_b(0, 1)
     pass_b(1, 0)
 
@@ -2645,7 +2698,7 @@
     add_blocks(tp_mine.at[0], [tp_sib.at[0]], rows)
     out_x.start()
     part_of(1)
-    pass_a(3)
+    pass_z(3, 1)
     pass_b(1, 1)
     pass_b(2, 0)
     part_to_sibling(1).wait_recv()
@@ -2696,21 +2749,21 @@
     lax.fori_loop(0, 16, finish_sibling, 0)
 
     def finish_links(i, carry):
-        over_a(i, grad_hbm).wait_send()
-        over_b(i, 0, grad_hbm).wait_send()
-        over_b(i, 1, grad_hbm).wait_send()
-
-        @pl.when((z < 3) & (i <= z))
-        def _():
-            up(i, grad_hbm).wait_send()
-
-        @pl.when((z > 0) & (i >= z))
-        def _():
-            down(i, grad_hbm).wait_send()
+        for da in range(2):
+            over_b(i, da, grad_hbm).wait_send()
+
+            @pl.when((z < 3) & (i <= z))
+            def _(da=da):
+                up(i, da, grad_hbm).wait_send()
+
+            @pl.when((z > 0) & (i >= z))
+            def _(da=da):
+                down(i, da, grad_hbm).wait_send()
 
         return carry
 
     lax.fori_loop(0, 4, finish_links, 0)
+    over_a(grad_hbm).wait_send()
     own.wait()
     for copy in (t_x, t_s, t_f, out_x, part_to_sibling(0), part_to_sibling(1), first, second):
         copy.wait_send()
@@ -2766,7 +2819,7 @@
         ]
         + [dma((6,)), dma((3,)), dma((3,)), dma((2,)), dma((2,)), dma((3,)), dma((3,))]
         + [dma((2,)), dma((2,))]
-        + [dma((4,)), dma((4,)), dma((4,)), dma((8,)), dma((16,)), dma((16,)), dma((16,))],
+        + [dma((8,)), dma((8,)), dma, dma((8,)), dma((16,)), dma((16,)), dma((16,))],
         compiler_params=pltpu.CompilerParams(
             collective_id=cid, has_side_effects=True, vmem_limit_bytes=60 * 2**20
         ),

time: 658 us -> 612 us (0.930)
  Pallas kernels: 576 us -> 546 us
  starting transfers between devices: 19.8 us -> 3.93 us
    pallas_call x1, Pallas kernels: 306 us -> 286 us  [experts(): pl.pallas_call(functools.partial(experts_kernel, expert_width, shared_wid...]
    all_to_all x1, starting transfers between devices: 19.8 us -> 3.93 us  [dense_plan(): lax.all_to_all(shared_parts, 'ep', split_axis=0, concat_axis=0, tiled=True)]
    pallas_call x1, Pallas kernels: 104 us -> 90.3 us  [attend(): pl.pallas_call(attend_kernel, out_shape=[result(rows, cols, dtype=full),...]
  transfers between devices with their start and end apart: 1 -> 1, of which waited for: 0 -> 0; matrix products, arithmetic and copies ran while one was open for 4% -> 4% of each run, Pallas kernels for 26% -> 28%
where the time goes in v5:
time: 612 us; the launch traced here: 604 us
  Pallas kernels  546 us (89%)
  local copies, waits for them, and re-layouts  30.1 us (5%)
  other arithmetic  11.8 us (2%)
  blocking collectives  6.56 us (1%)
    pallas_call x1, Pallas kernels, experts(): pl.pallas_call(functools.partial(experts_kernel, expert_width, shared_wid...  286 us
    pallas_call x1, Pallas kernels, unwind(): pl.pallas_call(unwind_kernel, out_shape=[jax.ShapeDtypeStruct((rows, cols...  170 us
    pallas_call x1, Pallas kernels, attend(): pl.pallas_call(attend_kernel, out_shape=[result(rows, cols, dtype=full),...  90.3 us
  transfers between devices with their start and end apart: 1, of which 0 were waited for; matrix products, arithmetic and copies ran while one was open for 4% of the time, Pallas kernels for 28%

profile of v5, /device:TPU:9, one launch (start us, length us, event | category | flops | bytes accessed | tf_op | source)
XLA Modules:
  0.0 603.8 jit_solution(8422930275324872935)
XLA Ops:
  0.7 3.0 constant_dynamic-slice_fusion.1
  3.8 1.2 copy.74
  5.0 1.2 copy.73
  6.2 1.8 select_reduce_fusion
  8.4 1.4 convert_reduce_fusion
  10.4 1.0 fusion.3
  11.4 0.8 dynamic_slice.24
  12.2 0.6 fusion.4.extra_ref
  12.8 1.0 pad_maximum_fusion
  15.7 90.3 %attend.1 = (f32[512,512]{1,0:T(8,128)}, f32[512,512]{1,0:T(8,128)}, f32[512,128]{1,0:T(8,128)}, bf16[512,512]{1,0:T(8,128)(2,1)}, bf16[512,2048]{1,0:T(8,128)(2...) custom-call(f32[8,2048]{1,0:T(8,128)} %broadcast_in_dim.44.first_ref, ...), custom_call_target="tpu_custom_call" | custom-call | tf_op jit(solution)/shard_map/attend/pallas_call | solution.py:2789
  106.0 286.2 %experts.1 = (f32[528,512]{1,0:T(8,128)}, f32[512,512]{1,0:T(8,128)}, f32[512,128]{1,0:T(8,128)}, f32[3,352,2048]{2,1,0:T(8,128)}, bf16[8,3,176,256]{3,2,1,0:T(8...) custom-call(bf16[512,512]{1,0:T(8,128)(2,1)} %get-tuple-element.42.x, ...), custom_call_target="tpu_custom_call" | custom-call | tf_op jit(solution)/shard_map/experts/pallas_call | solution.py:1776
  392.1 3.9 all-to-all-start
  396.2 0.7 fusion.17
  397.3 0.7 fusion.8
  398.6 0.9 fusion.19
  399.5 2.9 multiply_reduce_fusion
  403.6 169.9 %unwind.1 = (bf16[512,512]{1,0:T(8,128)(2,1)}, f32[4,256,512]{2,1,0:T(8,128)}, f32[16,512]{1,0:T(8,128)}) custom-call(f32[512,512]{1,0:T(8,128)} %get-tuple-element.163.dn2_ref, f32[512,512]{1,0:T(8,128)} %get-tuple-element.47.unit_ref, f32[512,128]{1,0:T(8,128)} %get-tuple-element.48.inv_ref, f32[8,512]{1,0:T(8,128)} %broadcast_in_dim.45.second_ref, ...), custom_call_target="tpu_custom_call" | custom-call | tf_op jit(solution)/shard_map/unwind/pallas_call | solution.py:2310
  573.5 0.8 slice.84
  574.3 0.7 slice.83
  575.0 0.7 slice.89
  575.7 2.7 slice_bitcast_fusion.2
  578.4 1.0 copy.72
  579.4 6.6 %all_gather.3 = f32[11,2048]{1,0:T(8,128)S(1)} all-gather(f32[11,512]{1,0:T(8,128)S(1)} %pad_maximum_fusion.2), channel_id=1, replica_groups=mesh['ep'=8,'tp'=4] {'tp'}, dimensions={1}, use_global_device_ids=true | all-gather | bytes 112640 | tf_op jit(solution)/shard_map/all_gather | solution.py:3001
  586.0 0.6 fusion.18
  586.6 0.7 dynamic-slice_bitcast_fusion.1
  587.3 0.7 dynamic-slice_bitcast_fusion
  588.0 2.5 add_convert_fusion
  590.4 7.3 %fusion.15 = (f32[1,352,2048]{2,1,0:T(8,128)}, f32[1,2048,352]{1,2,0:T(8,128)}, f32[1,2048,352]{1,2,0:T(8,128)}) fusion(f32[3,352,2048]{2,1,0:T(8,128)} %get-tuple-element.62), kind=kLoop, calls=%fused_computation.65 | loop fusion | bytes 17301504 | tf_op jit(solution)/shard_map/slice | solution.py:3022
  598.3 1.5 fusion.16
  599.8 1.5 copy.70
  601.3 1.5 copy.71
  602.8 0.8 copy.76
  (50 shorter events, 5.7 us)
Async XLA Ops:
  0.7 5.5 copy-start.4
  0.7 5.5 copy-start.10
  3.7 6.7 %copy-start.6 = (bf16[2048]{0:T(1024)(128)(2,1)S(1)}, bf16[2048]{0:T(1024)(128)(2,1)}, u32[]{:S(2)}) copy-start(bf16[2048]{0:T(1024)(128)(2,1)} %param.36) | copy-start | bytes 12292
  3.7 8.4 %copy-start.3 = (bf16[2048,8]{0,1:T(8,128)(2,1)S(1)}, bf16[2048,8]{0,1:T(8,128)(2,1)}, u32[]{:S(2)}) copy-start(bf16[2048,8]{0,1:T(8,128)(2,1)} %param.32) | copy-start | bytes 98308
  3.7 10.1 %copy-start.7 = (f32[512]{0:T(512)S(1)}, f32[512]{0:T(512)}, u32[]{:S(2)}) copy-start(f32[512]{0:T(512)} %param.29) | copy-start | bytes 6148
  3.7 10.1 %copy-start.8 = (f32[512]{0:T(512)S(1)}, f32[512]{0:T(512)}, u32[]{:S(2)}) copy-start(f32[512]{0:T(512)} %param.28) | copy-start | bytes 6148
  3.8 10.1 %copy-start.9 = (f32[512]{0:T(512)S(1)}, f32[512]{0:T(512)}, u32[]{:S(2)}) copy-start(f32[512]{0:T(512)} %param.27) | copy-start | bytes 6148
  3.8 11.3 %copy-start.5 = (f32[2048]{0:T(1024)S(1)}, f32[2048]{0:T(1024)}, u32[]{:S(2)}) copy-start(f32[2048]{0:T(1024)} %param.23) | copy-start | bytes 24580
  392.1 4.9 copy-start.1
  392.1 6.2 %copy-start = (bf16[512,512]{1,0:T(8,128)(2,1)S(1)}, bf16[512,512]{1,0:T(8,128)(2,1)}, u32[]{:S(2)}) copy-start(bf16[512,512]{1,0:T(8,128)(2,1)} %get-tuple-element.42.x_ref) | copy-start | bytes 1572868
  392.1 205.6 %all-to-all-start = ((bf16[8,3,176,256]{3,2,1,0:T(8,128)(2,1)}), bf16[8,3,176,256]{3,2,1,0:T(8,128)(2,1)S(1)}, u32[]{:S(2)}, u32[]{:S(2)}) async-start(bf16[8,3,176,256]{3,2,1,0:T(8,128)(2,1)} %get-tuple-element.61), calls=%async_computation | async-start | bytes 4325376 | tf_op jit(solution)/shard_map/all_to_all | solution.py:2939
  599.8 3.1 copy-start.2

commit v6 on v5

--- a/solution.py
+++ b/solution.py
@@ -1090,8 +1090,9 @@
     shared_up_ref,
     expert_down_ref,
     shared_down_ref,
+    residual_ref,
     grad_ref,
-    ffn_ref,
+    mixed_ref,
     logit_ref,
     expert_grads_ref,
     shared_grads_ref,
@@ -1099,8 +1100,7 @@
     from_sib,
     from_b,
     from_a,
-    from_below,
-    from_above,
+    from_z,
     in_ref,
     down_ref,
     scalars,
@@ -1139,10 +1139,8 @@
     rb_recv,
     ra_send,
     ra_recv,
-    ru_send,
-    ru_recv,
-    rd_send,
-    rd_recv,
+    rz_send,
+    rz_recv,
 ):
     ep, tp, z, y, x, core = place()
     rows, cols = x_ref.shape
@@ -1171,8 +1169,8 @@
             z == 0, values[0], jnp.where(z == 1, values[1], jnp.where(z == 2, values[2], values[3]))
         )
 
-    coming = (z, choose(1, 0, 3, 2), choose(2, 2, 1, 1), choose(3, 3, 0, 0))
-    turns = (z, choose(1, 0, 3, 2), choose(3, 3, 0, 0), choose(2, 2, 1, 1))
+    coming = (z, choose(1, 2, 1, 2), choose(2, 0, 3, 1), choose(3, 3, 0, 0))
+    turns = (z, choose(1, 2, 1, 2), choose(3, 3, 0, 0), choose(2, 0, 3, 1))
 
     def arrived(z_at, da, db):
         block, n = spot(z_at, da, db), at(z_at, da, db)
@@ -1363,20 +1361,14 @@
             peer_a,
         )
 
-    def rs_up(k, z_at, half):
-        first, count = cuts[half]
-        n = z_at * 2 + half
-        span = pl.ds(first, count)
+    def rs_along_z(k, part):
+        span = pl.ds(*cuts[part])
         return remote(
-            mine.at[k, span], from_below.at[z_at, span], ru_send.at[n], ru_recv.at[n], above
-        )
-
-    def rs_down(k, z_at, half):
-        first, count = cuts[half]
-        n = z_at * 2 + half
-        span = pl.ds(first, count)
-        return remote(
-            mine.at[k, span], from_above.at[z_at, span], rd_send.at[n], rd_recv.at[n], below
+            mine.at[k, span],
+            from_z.at[z, span],
+            rz_send.at[k * 2 + part],
+            rz_recv.at[z * 2 + part],
+            (ep + 2 * (turns[k] - z), tp),
         )
 
     def fetch(source, i):
@@ -1439,33 +1431,21 @@
             copy.start()
         add_part(k, part, copies)
         if k > 0:
-
-            @pl.when(z == 0)
-            def _():
-                rs_up(k, z_at, part).start()
-
-            @pl.when(z == 3)
-            def _():
-                rs_down(k, z_at, part).start()
-
-    def chain(k, part):
-        z_at = turns[k]
-
-        @pl.when((z > 0) & (z < 3) & (z_at > z))
-        def _():
-            rs_up(k, z_at, part).wait_recv()
-            copy = fetch_part(from_below.at[z_at], part, 0)
-            copy.start()
-            add_part(k, part, [copy])
-            rs_up(k, z_at, part).start()
-
-        @pl.when((z > 0) & (z < 3) & (z_at < z))
-        def _():
-            rs_down(k, z_at, part).wait_recv()
-            copy = fetch_part(from_above.at[z_at], part, 0)
-            copy.start()
-            add_part(k, part, [copy])
-            rs_down(k, z_at, part).start()
+            rs_along_z(k, part).start()
+
+    def reduce_z(i, part):
+        source = (choose(3, 0, 3, 0), choose(2, 2, 1, 1), choose(1, 3, 0, 2))[i]
+        span = pl.ds(*cuts[part])
+        remote(
+            mine.at[0, span],
+            from_z.at[source, span],
+            rz_send.at[0],
+            rz_recv.at[source * 2 + part],
+            sibling,
+        ).wait_recv()
+        copy = fetch_part(from_z.at[source], part, 0)
+        copy.start()
+        add_part(0, part, [copy])
 
     tile = x_tile.shape[1]
 
@@ -1631,20 +1611,18 @@
     load_tile(all_ref, x_tile, 0, 3).start()
     tiles = shared_grads_ref.shape[0]
     services = {
-        (0, 0): lambda: fetch_sibling(0, 1),
-        (0, 1): lambda: reduce_sibling(0, 1),
-        (0, 2): lambda: chain(2, 0),
-        (1, 0): lambda: reduce_b(3, 0),
-        (1, 1): lambda: chain(2, 1),
-        (2, 0): lambda: chain(1, 0),
-        (2, 2): lambda: chain(1, 1),
-        (4, 0): lambda: reduce_b(3, 1),
-        (4, 2): lambda: reduce_a(3, 0),
-        (5, 1): lambda: reduce_b(0, 0),
-        (6, 0): lambda: chain(3, 0),
-        (6, 2): lambda: reduce_a(3, 1),
-        (7, 0): lambda: reduce_b(0, 1),
-        (7, 2): lambda: chain(3, 1),
+        (0, 0): (fetch_sibling, 0, 1),
+        (0, 1): (reduce_sibling, 0, 1),
+        (1, 0): (reduce_b, 3, 0),
+        (0, 2): (reduce_z, 0, 0),
+        (1, 1): (reduce_z, 0, 1),
+        (2, 0): (reduce_z, 1, 0),
+        (3, 0): (reduce_z, 1, 1),
+        (4, 0): (reduce_b, 3, 1),
+        (4, 2): (reduce_a, 3, 0),
+        (5, 1): (reduce_b, 0, 0),
+        (6, 2): (reduce_a, 3, 1),
+        (7, 0): (reduce_b, 0, 1),
     }
 
     def tile_step(t, carry):
@@ -1662,9 +1640,9 @@
                 if kind == 2:
                     load_tile(all_ref, x_tile, t + 1, 3).start()
 
-            for (at_tile, at_kind), service in services.items():
+            for (at_tile, at_kind), (service, *which) in services.items():
                 if at_kind == kind:
-                    pl.when(t == at_tile)(service)
+                    pl.when(t == at_tile)(functools.partial(service, *which))
         return carry
 
     lax.fori_loop(0, tiles, tile_step, 0)
@@ -1672,55 +1650,28 @@
         for copy in tile_stores(tiles - 1, kind):
             copy.wait()
 
-    reduce_a(0, 0)
-    reduce_a(0, 1)
-
-    for half in range(2):
-
-        @pl.when(z > 0)
-        def _(half=half):
-            rs_up(0, z, half).wait_recv()
-            fetch_part(from_below.at[z], half, 0).start()
-            fetch_part(from_below.at[z], half, 0).wait()
-
-        @pl.when(z < 3)
-        def _(half=half):
-            rs_down(0, z, half).wait_recv()
-            fetch_part(from_above.at[z], half, 1).start()
-            fetch_part(from_above.at[z], half, 1).wait()
-
-    def total(parts):
-        def body(i, carry):
-            for target, first in ((grad_ref, 0), (ffn_ref, out_at)):
-                span = pl.ds(pl.multiple_of(i * 16, 16), 16)
-                source = pl.ds(pl.multiple_of(first + i * 16, 16), 16)
-                value = mine[0, source, :].astype(jnp.float32)
-                for part in parts:
-                    value = value + landed[part, source, :].astype(jnp.float32)
-                target[span, :] = value
-            return carry
-
-        lax.fori_loop(0, rows // 16, body, 0)
-        value = mine[0, rows:out_at, :].astype(jnp.float32)
-        for part in parts:
-            value = value + landed[part, rows:out_at, :].astype(jnp.float32)
-        grad_ref[rows:, :] = value
-
-    @pl.when(z == 0)
-    def _():
-        total([1])
-
-    @pl.when(z == 3)
-    def _():
-        total([0])
-
-    @pl.when((z > 0) & (z < 3))
-    def _():
-        total([0, 1])
+    for part in range(2):
+        reduce_a(0, part)
+        reduce_z(2, part)
+
+    def total(i, carry):
+        span = pl.ds(pl.multiple_of(i * 64, 64), 64)
+        out_span = pl.ds(pl.multiple_of(out_at + i * 64, 16), 64)
+        grad_ref[span, :] = mine[0, span, :].astype(jnp.float32)
+        mixed_ref[span, :] = (
+            residual_ref[span, :] + mine[0, out_span, :].astype(jnp.float32)
+        ).astype(jnp.bfloat16)
+        return carry
+
+    lax.fori_loop(0, rows // 64, total, 0)
+    grad_ref[rows:, :] = mine[0, rows:out_at, :].astype(jnp.float32)
 
     for i in range(1, sources):
         kept_to(i).wait_send()
     staged_free(0, 1)
+    for k in range(1, 4):
+        for part in range(2):
+            rs_along_z(k, part).wait_send()
     for k in (0, 2, 3):
         for part in range(2):
             rs_over_a(k, part).wait_send()
@@ -1743,22 +1694,12 @@
         def _():
             down(i, x_ref).wait_send()
 
-        for half in range(2):
-
-            @pl.when(i > z)
-            def _(half=half):
-                rs_up(0, i, half).wait_send()
-
-            @pl.when(i < z)
-            def _(half=half):
-                rs_down(0, i, half).wait_send()
-
         return carry
 
     lax.fori_loop(0, 4, finish, 0)
 
 
-def experts(x_cols, grads_all, kept_rows, weights, expert_total, cid):
+def experts(x_cols, grads_all, kept_rows, weights, residual, expert_total, cid):
     rows, cols = x_cols.shape
     total, model_dim = grads_all.shape
     sources = total // rows
@@ -1777,7 +1718,7 @@
         functools.partial(experts_kernel, expert_width, shared_width, expert_total),
         out_shape=[
             jax.ShapeDtypeStruct((rows + 16, cols), jnp.float32),
-            jax.ShapeDtypeStruct((rows, cols), jnp.float32),
+            jax.ShapeDtypeStruct((rows, cols), low),
             jax.ShapeDtypeStruct((rows, 128), jnp.float32),
             jax.ShapeDtypeStruct((3, expert_width, model_dim), jnp.float32),
             jax.ShapeDtypeStruct((sources, 3, shared_width, tile), low),
@@ -1786,10 +1727,9 @@
             landing(8),
             landing(4),
             landing(4),
-            landing(4),
         ],
-        in_specs=[hbm] * 10,
-        out_specs=[vmem, vmem, vmem] + [hbm] * 8,
+        in_specs=[hbm] * 10 + [vmem],
+        out_specs=[vmem, vmem, vmem] + [hbm] * 7,
         scratch_shapes=[
             pltpu.VMEM((2 * width, model_dim), low),
             pltpu.VMEM((width, model_dim), low),
@@ -1813,12 +1753,12 @@
         + [dma((4,)), dma((4,)), dma((4,)), dma((8,)), dma((16,)), dma((16,)), dma((16,)), dma]
         + [dma((4,)), dma((2,)), dma((6,)), dma((8,)), dma((7,)), dma((7,))]
         + [dma((16,))] * 4
-        + [dma((8,))] * 6,
+        + [dma((8,))] * 4,
         compiler_params=pltpu.CompilerParams(
             collective_id=cid, has_side_effects=True, vmem_limit_bytes=63 * 2**20
         ),
         name="experts",
-    )(x_cols, grads_all, kept_rows, *weights)
+    )(x_cols, grads_all, kept_rows, *weights, residual)
 
 
 def row_of(columns):
@@ -1878,6 +1818,8 @@
     from_y,
     from_below,
     from_above,
+    from_below_2,
+    from_above_2,
     tp_staged,
     tp_mine,
     tp_sib,
@@ -1887,6 +1829,7 @@
     row_sib,
     row_x,
     smalls,
+    quarters,
     load_sem,
     g_send,
     g_recv,
@@ -1904,6 +1847,12 @@
     tp_recv,
     small_send,
     small_recv,
+    s_send,
+    s_recv,
+    up2_send,
+    up2_recv,
+    down2_send,
+    down2_recv,
 ):
     ep, tp, z, y, x, core = place()
     rows, cols = unit_ref.shape
@@ -2010,6 +1959,82 @@
         lax.fori_loop(0, 4, other, 0)
         lax.fori_loop(0, 4, ours, 0)
 
+    def blocks_along_z(left, right):
+        def one(i, carry):
+            z_at = lax.rem(i * 3, 4)
+            cut = pl.ds(pl.multiple_of((z_at * 2 + 1 - y) * block, block), block)
+            staged[4 + z_at] = inner_rows(left[:, cut], right[...]).astype(low)
+            cut = pl.ds(pl.multiple_of((z_at * 2 + y) * block, block), block)
+            mine[4 + z_at] = inner_rows(left[:, cut], right[...]).astype(low)
+
+            @pl.when((z == 0) & (z_at > 0))
+            def _():
+                up_2(z_at).start()
+                up(1, z_at).start()
+
+            @pl.when((z == 3) & (z_at < 3))
+            def _():
+                down_2(z_at).start()
+                down(1, z_at).start()
+
+            return carry
+
+        lax.fori_loop(0, 4, one, 0)
+
+    def up_2(z_at):
+        return remote(
+            staged.at[4 + z_at], from_below_2.at[z_at], up2_send.at[z_at], up2_recv.at[z_at], above
+        )
+
+    def down_2(z_at):
+        return remote(
+            staged.at[4 + z_at],
+            from_above_2.at[z_at],
+            down2_send.at[z_at],
+            down2_recv.at[z_at],
+            below,
+        )
+
+    def chain_2():
+        def rise(z_at):
+            up_2(z_at).wait_recv()
+            add_blocks(staged.at[4 + z_at], [from_below_2.at[z_at]], block)
+            up_2(z_at).start()
+
+        def fall(z_at):
+            down_2(z_at).wait_recv()
+            add_blocks(staged.at[4 + z_at], [from_above_2.at[z_at]], block)
+            down_2(z_at).start()
+
+        @pl.when(z == 1)
+        def _():
+            rise(3)
+            rise(2)
+            fall(0)
+
+        @pl.when(z == 2)
+        def _():
+            fall(0)
+            fall(1)
+            rise(3)
+
+    def other_y_along_z():
+        @pl.when(z > 0)
+        def _():
+            up_2(z).wait_recv()
+            add_blocks(staged.at[4 + z], [from_below_2.at[z]], block)
+
+        @pl.when(z < 3)
+        def _():
+            down_2(z).wait_recv()
+            add_blocks(staged.at[4 + z], [from_above_2.at[z]], block)
+
+        over_y(1, z).start()
+
+    def own_first_along_z():
+        over_y(1, z).wait_recv()
+        add_blocks(mine.at[4 + z], [from_y.at[4 + z]], block)
+
     def up(kind, z_at):
         n = kind * 4 + z_at
         return remote(mine.at[n], from_below.at[n], up_send.at[n], up_recv.at[n], above)
@@ -2164,7 +2189,7 @@
 
     rotate_back(dq, 0, score_scale)
     loads[1].wait()
-    weight_blocks(1, n1, lin_grads.at[0])
+    blocks_along_z(n1, lin_grads.at[0])
     chain(0)
 
     @pl.when(y == 0)
@@ -2182,7 +2207,6 @@
     lin_grads[2] = dv[...].astype(low)
     weight_blocks(2, n1, lin_grads.at[1])
     weight_blocks(3, n1, lin_grads.at[2])
-    y_stage(1)
     for copy in loads[2:]:
         copy.wait()
 
@@ -2208,7 +2232,7 @@
     add_blocks(tp_mine.at[0], [tp_sib.at[0]], rows)
     out_x.start()
     part_of(1)
-    chain(1)
+    chain_2()
     to_sibling(1).wait_recv()
     out_x.wait_recv()
 
@@ -2253,22 +2277,36 @@
 
     for i in range(1, sources):
         small_to(i).start()
+    other_y_along_z()
+    chain(1)
     y_stage(2)
     final(0)
     chain(2)
     y_stage(3)
-    final(1)
     chain(3)
     for i in range(1, sources):
         small_to(i).wait_recv()
     total = smalls[0]
     for i in range(1, sources):
         total = total + smalls[i]
-    sums_ref[...] = total
+    quarters[tp] = total
+    s_x = remote(quarters.at[tp], quarters.at[tp], s_send.at[0], s_recv.at[0], across)
+    s_s = remote(quarters.at[tp], quarters.at[tp], s_send.at[1], s_recv.at[1], sibling)
+    s_x.start()
+    s_s.start()
     final(2)
+    own_first_along_z()
+    s_x.wait_recv()
+    other = quarters.at[tp + 2 - 4 * x]
+    s_f = remote(other, other, s_send.at[2], s_recv.at[2], sibling)
+    s_f.start()
     final(3)
-
-    for copy in (g_x, g_s, g_f, out_x, to_sibling(0), to_sibling(1)):
+    final(1)
+    s_s.wait_recv()
+    s_f.wait_recv()
+    sums_ref[...] = quarters[...]
+
+    for copy in (g_x, g_s, g_f, s_x, s_s, s_f, out_x, to_sibling(0), to_sibling(1)):
         copy.wait_send()
 
     @pl.when(y == 1)
@@ -2280,8 +2318,12 @@
         small_to(i).wait_send()
 
     def finish(n, carry):
-        remote(staged.at[0], from_y.at[0], y_send.at[n], y_recv.at[n], beside).wait_send()
         z_at = lax.rem(n, 4)
+
+        @pl.when((n < 4) | (n >= 8) | (n == 4 + z))
+        def _():
+            remote(staged.at[0], from_y.at[0], y_send.at[n], y_recv.at[n], beside).wait_send()
+
 
         @pl.when(z_at > z)
         def _():
@@ -2294,6 +2336,19 @@
         return carry
 
     lax.fori_loop(0, 16, finish, 0)
+
+    def finish_2(z_at, carry):
+        @pl.when(z_at > z)
+        def _():
+            up_2(z_at).wait_send()
+
+        @pl.when(z_at < z)
+        def _():
+            down_2(z_at).wait_send()
+
+        return carry
+
+    lax.fori_loop(0, 4, finish_2, 0)
 
 
 def unwind(vmem_args, hbm_args, cid):
@@ -2312,7 +2367,7 @@
         out_shape=[
             jax.ShapeDtypeStruct((rows, cols), low),
             jax.ShapeDtypeStruct((4, block, cols), full),
-            jax.ShapeDtypeStruct((16, cols), full),
+            jax.ShapeDtypeStruct((4, 16, cols), full),
         ],
         in_specs=[vmem] * len(vmem_args) + [hbm] * len(hbm_args),
         out_specs=[vmem] * 3,
@@ -2332,6 +2387,7 @@
             buffers(rows, cols),
         ]
         + [buffers(16, block, cols)] * 5
+        + [buffers(4, block, cols)] * 2
         + [
             buffers(2, rows, cols),
             buffers(2, rows, cols),
@@ -2342,10 +2398,12 @@
             buffers(2, 8, rows, dtype=full),
             buffers(2, 8, rows, dtype=full),
             buffers(sources, 16, cols, dtype=full),
+            buffers(4, 16, cols, dtype=full),
         ]
         + [dma((5,)), dma((3,)), dma((3,)), dma((4,)), dma((4,)), dma((2,)), dma((2,))]
         + [dma((16,))] * 6
-        + [dma((3,)), dma((3,)), dma((7,)), dma((7,))],
+        + [dma((3,)), dma((3,)), dma((7,)), dma((7,)), dma((3,)), dma((3,))]
+        + [dma((4,))] * 4,
         compiler_params=pltpu.CompilerParams(
             collective_id=cid, has_side_effects=True, vmem_limit_bytes=60 * 2**20
         ),
@@ -2919,7 +2977,7 @@
     extra_rows = jnp.concatenate([router_weight.T, switch_vector[None, :]], axis=0)
     extra_rows = jnp.pad(extra_rows, ((0, 16 - extra_rows.shape[0]), (0, 0)))
     kept_rows = jnp.pad(kept_own, ((0, 16 - expert_total), (0, 0))).astype(jnp.bfloat16)
-    reduced, ffn_cols, logit_tile, expert_grads, shared_parts, *_ = experts(
+    reduced, layer_out, logit_tile, expert_grads, shared_parts, *_ = experts(
         normed_cols,
         grads_all,
         kept_rows,
@@ -2932,10 +2990,10 @@
             expert_down_weight[0],
             shared_down_weight,
         ],
+        hidden_cols,
         expert_total,
         4,
     )
-    layer_out = (hidden_cols + ffn_cols).astype(jnp.bfloat16)
     shared_parts = lax.all_to_all(shared_parts, "ep", split_axis=0, concat_axis=0, tiled=True)
     shared_parts = shared_parts.transpose(1, 0, 2, 3).reshape(3, sources * shared_width, -1)
     shared_parts = shared_parts.astype(jnp.float32)
@@ -2995,11 +3053,15 @@
     share = model_dim // sources
     bias_width = HD // sources
     bias_sums = lax.dynamic_slice_in_dim(
-        sums[1:4].reshape(3, head_count, HD), ep * bias_width, bias_width, 2
-    )
-    spread = jnp.concatenate([sums[:1], sums[4 : 4 + small_rows]], axis=0)
-    spread = lax.all_gather(spread, "tp", axis=1, tiled=True)
-    spread = lax.dynamic_slice_in_dim(spread, ep * share, share, 1)
+        lax.dynamic_index_in_dim(sums, tp, 0, keepdims=False)[1:4].reshape(3, head_count, HD),
+        ep * bias_width,
+        bias_width,
+        2,
+    )
+    per_quarter = col_width // share
+    spread = lax.dynamic_index_in_dim(sums, ep // per_quarter, 0, keepdims=False)
+    spread = lax.dynamic_slice_in_dim(spread, ep % per_quarter * share, share, 1)
+    spread = jnp.concatenate([spread[:1], spread[4 : 4 + small_rows]], axis=0)
     return (
         layer_out,
         tokens_grad,

time: 612 us -> 586 us (0.958)
  Pallas kernels: 546 us -> 524 us
  blocking collectives: 6.56 us -> 0 us
    pallas_call x1, Pallas kernels: 170 us -> 152 us  [unwind(): pl.pallas_call(unwind_kernel, out_shape=[jax.ShapeDtypeStruct((rows, cols...]
    all_gather x1 -> x0, blocking collectives: 6.56 us -> none  [dense_plan(): spread = lax.all_gather(spread, 'tp', axis=1, tiled=True)]
  transfers between devices with their start and end apart: 1 -> 1, of which waited for: 0 -> 0; matrix products, arithmetic and copies ran while one was open for 4% -> 4% of each run, Pallas kernels for 28% -> 26%
where the time goes in v6:
time: 586 us; the launch traced here: 575 us
  Pallas kernels  524 us (89%)
  local copies, waits for them, and re-layouts  30.9 us (5%)
  other arithmetic  9.33 us (2%)
    pallas_call x1, Pallas kernels, experts(): pl.pallas_call(functools.partial(experts_kernel, expert_width, shared_wid...  282 us
    pallas_call x1, Pallas kernels, unwind(): pl.pallas_call(unwind_kernel, out_shape=[jax.ShapeDtypeStruct((rows, cols...  152 us
    pallas_call x1, Pallas kernels, attend(): pl.pallas_call(attend_kernel, out_shape=[result(rows, cols, dtype=full),...  90.4 us
  transfers between devices with their start and end apart: 1, of which 0 were waited for; matrix products, arithmetic and copies ran while one was open for 4% of the time, Pallas kernels for 26%

profile of v6, /device:TPU:9, one launch (start us, length us, event | category | flops | bytes accessed | tf_op | source)
XLA Modules:
  0.0 574.5 jit_solution(17576627263375891795)
XLA Ops:
  0.7 2.9 constant_dynamic-slice_fusion.2
  3.8 1.2 copy.74
  5.0 1.2 copy.73
  6.2 1.8 select_reduce_fusion
  8.4 1.4 convert_reduce_fusion
  10.4 1.0 fusion.3
  11.4 0.8 dynamic_slice.29
  12.1 0.6 fusion.4.extra_ref
  12.8 1.0 pad_maximum_fusion
  13.8 0.6 select_maximum_fusion.2.bias_ref
  15.0 0.6 broadcast_in_dim.44.first_ref
  15.7 90.4 %attend.1 = (f32[512,512]{1,0:T(8,128)}, f32[512,512]{1,0:T(8,128)}, f32[512,128]{1,0:T(8,128)}, bf16[512,512]{1,0:T(8,128)(2,1)}, bf16[512,2048]{1,0:T(8,128)(2...) custom-call(f32[8,2048]{1,0:T(8,128)} %broadcast_in_dim.44.first_ref, ...), custom_call_target="tpu_custom_call" | custom-call | tf_op jit(solution)/shard_map/attend/pallas_call | solution.py:2847
  106.0 282.1 %experts.1 = (f32[528,512]{1,0:T(8,128)}, bf16[512,512]{1,0:T(8,128)(2,1)}, f32[512,128]{1,0:T(8,128)}, f32[3,352,2048]{2,1,0:T(8,128)}, bf16[8,3,176,256]{3,2,1...) custom-call(bf16[512,512]{1,0:T(8,128)(2,1)} %get-tuple-element.41.x, ...), custom_call_target="tpu_custom_call" | custom-call | tf_op jit(solution)/shard_map/experts/pallas_call | solution.py:1717
  388.2 5.0 all-to-all-start
  393.3 0.7 fusion.17
  394.4 0.7 fusion.8
  395.7 0.9 fusion.19
  396.6 2.9 multiply_reduce_fusion
  399.5 0.6 select_maximum_fusion.small_ref
  400.8 151.6 %unwind.1 = (bf16[512,512]{1,0:T(8,128)(2,1)}, f32[4,256,512]{2,1,0:T(8,128)}, f32[4,16,512]{2,1,0:T(8,128)}) custom-call(f32[512,512]{1,0:T(8,128)} %get-tuple-element.163.dn2_ref, f32[512,512]{1,0:T(8,128)} %get-tuple-element.47.unit_ref, f32[512,128]{1,0:T(8,128)} %get-tuple-element.48.inv_ref, f32[8,512]{1,0:T(8,128)} %broadcast_in_dim.45.second_ref, ...), custom_call_target="tpu_custom_call" | custom-call | tf_op jit(solution)/shard_map/unwind/pallas_call | solution.py:2365
  552.4 2.7 slice_bitcast_fusion.2
  555.1 1.0 copy.72
  556.1 0.7 constant_dynamic-slice_fusion.1
  556.8 1.5 fusion.18
  558.3 0.7 dynamic-slice_bitcast_fusion.1
  558.9 1.4 dynamic-slice_bitcast_fusion
  560.4 7.3 %fusion.15 = (f32[1,352,2048]{2,1,0:T(8,128)}, f32[1,2048,352]{1,2,0:T(8,128)}, f32[1,2048,352]{1,2,0:T(8,128)}) fusion(f32[3,352,2048]{2,1,0:T(8,128)} %get-tuple-element.62), kind=kLoop, calls=%fused_computation.64 | loop fusion | bytes 17301504 | tf_op jit(solution)/shard_map/slice | solution.py:3084
  568.2 1.5 fusion.16
  569.7 1.5 copy.70
  571.2 1.5 copy.71
  572.8 0.8 copy.77
  573.6 0.8 copy.78
  (48 shorter events, 3.8 us)
Async XLA Ops:
  0.7 5.5 copy-start.5
  0.7 5.5 copy-start.11
  3.7 6.7 %copy-start.7 = (bf16[2048]{0:T(1024)(128)(2,1)S(1)}, bf16[2048]{0:T(1024)(128)(2,1)}, u32[]{:S(2)}) copy-start(bf16[2048]{0:T(1024)(128)(2,1)} %param.36) | copy-start | bytes 12292
  3.7 8.4 %copy-start.4 = (bf16[2048,8]{0,1:T(8,128)(2,1)S(1)}, bf16[2048,8]{0,1:T(8,128)(2,1)}, u32[]{:S(2)}) copy-start(bf16[2048,8]{0,1:T(8,128)(2,1)} %param.32) | copy-start | bytes 98308
  3.7 10.1 %copy-start.8 = (f32[512]{0:T(512)S(1)}, f32[512]{0:T(512)}, u32[]{:S(2)}) copy-start(f32[512]{0:T(512)} %param.29) | copy-start | bytes 6148
  3.7 10.1 %copy-start.9 = (f32[512]{0:T(512)S(1)}, f32[512]{0:T(512)}, u32[]{:S(2)}) copy-start(f32[512]{0:T(512)} %param.28) | copy-start | bytes 6148
  3.7 10.1 %copy-start.10 = (f32[512]{0:T(512)S(1)}, f32[512]{0:T(512)}, u32[]{:S(2)}) copy-start(f32[512]{0:T(512)} %param.27) | copy-start | bytes 6148
  3.7 11.3 %copy-start.6 = (f32[2048]{0:T(1024)S(1)}, f32[2048]{0:T(1024)}, u32[]{:S(2)}) copy-start(f32[2048]{0:T(1024)} %param.23) | copy-start | bytes 24580
  388.2 6.0 %copy-start.1 = (f32[512,128]{1,0:T(8,128)S(1)}, f32[512,128]{1,0:T(8,128)}, u32[]{:S(2)}) copy-start(f32[512,128]{1,0:T(8,128)} %get-tuple-element.46) | copy-start | bytes 786436
  388.2 7.3 %copy-start = (bf16[512,512]{1,0:T(8,128)(2,1)S(1)}, bf16[512,512]{1,0:T(8,128)(2,1)}, u32[]{:S(2)}) copy-start(bf16[512,512]{1,0:T(8,128)(2,1)} %get-tuple-element.41.x_ref) | copy-start | bytes 1572868
  388.2 179.5 %all-to-all-start = ((bf16[8,3,176,256]{3,2,1,0:T(8,128)(2,1)}), bf16[8,3,176,256]{3,2,1,0:T(8,128)(2,1)S(1)}, u32[]{:S(2)}, u32[]{:S(2)}) async-start(bf16[8,3,176,256]{3,2,1,0:T(8,128)(2,1)} %get-tuple-element.61), calls=%async_computation | async-start | bytes 4325376 | tf_op jit(solution)/shard_map/all_to_all | solution.py:2997
  569.7 3.1 copy-start.2
  571.2 2.3 copy-start.3

commit v7 on v6

--- a/solution.py
+++ b/solution.py
@@ -1515,15 +1515,25 @@
             expert_width,
         ),
         (expert_gate_ref, in_ref, 0),
-        (shared_gate_ref, in_ref, expert_width),
         (extra_ref, in_ref, filled),
         (expert_up_ref, in_ref, width),
-        (shared_up_ref, in_ref, width + expert_width),
     ]
     weight_copies = [
         pltpu.make_async_copy(piece, target.at[pl.ds(at_row, piece.shape[0]), :], weight_sem.at[i])
         for i, (piece, target, at_row) in enumerate(pieces)
     ]
+    model_dim = in_ref.shape[1]
+    window = (shared_width // 128 + 2) * 128
+    first_tile = lax.min(ep * shared_width // 128, (shared_gate_ref.shape[1] - window) // 128)
+    offset = ep * shared_width - first_tile * 128
+    for i, source in enumerate((shared_gate_ref, shared_up_ref)):
+        weight_copies.append(
+            pltpu.make_async_copy(
+                source.at[:, pl.ds(pl.multiple_of(first_tile * 128, 128), window)],
+                both_all.at[pl.ds(i * model_dim, model_dim), pl.ds(0, window)],
+                weight_sem.at[5 + i],
+            )
+        )
     for copy in weight_copies:
         copy.start()
     for target, first, last_row in (
@@ -1534,6 +1544,22 @@
         target[first:last_row, :] = jnp.zeros((last_row - first, target.shape[1]), target.dtype)
     for copy in weight_copies:
         copy.wait()
+    picked = (
+        lax.broadcasted_iota(jnp.int32, (shared_width, window), 1)
+        == lax.broadcasted_iota(jnp.int32, (shared_width, window), 0) + offset
+    ).astype(jnp.bfloat16)
+
+    def pick_rows(i, carry):
+        cut = pl.ds(pl.multiple_of(i * 512, 512), 512)
+        for j in range(2):
+            held = pl.ds(pl.multiple_of(j * model_dim + i * 512, 512), 512)
+            at_row = j * width + expert_width
+            in_ref[at_row : at_row + shared_width, cut] = times_transpose(
+                picked, both_all[held, :window]
+            ).astype(jnp.bfloat16)
+        return carry
+
+    lax.fori_loop(0, model_dim // 512, pick_rows, 0)
     load_g(0, 0).wait()
     project_grad()
     own_kept.wait()
@@ -1703,7 +1729,7 @@
     rows, cols = x_cols.shape
     total, model_dim = grads_all.shape
     sources = total // rows
-    expert_width, shared_width = weights[0].shape[0], weights[1].shape[0]
+    expert_width, shared_width = weights[0].shape[0], weights[1].shape[1] // sources
     filled = expert_width + shared_width
     width = -(-(filled + expert_total + 1) // 128) * 128
     tall = 2 * rows + 16
@@ -2942,14 +2968,11 @@
 
     kept_own = kept_choice(expert_ids, pair_order, expert_total, capacity)
 
-    def tall(vector):
-        return jnp.broadcast_to(vector[None, :], (8, vector.shape[0]))
-
     cosine, sine_part = rope_tables(tok_count, HD, place_in_seq * tok_count)
     cos_wide = jnp.concatenate([cosine[:, 0], cosine[:, 0]], axis=1)
     sin_wide = jnp.concatenate([-sine_part[:, 0], sine_part[:, 0]], axis=1)
     second_cols = own_cols(second_gain)
-    biases = jnp.pad(jnp.stack([query_bias, key_bias, value_bias]), ((0, 5), (0, 0)))
+    biases = jnp.stack([query_bias, key_bias, value_bias])
     (
         hidden_cols,
         unit_two,
@@ -2966,13 +2989,10 @@
         log_rows,
         grads_all,
     ) = attend(
-        [tall(first_gain), biases, tall(second_cols), cos_wide, sin_wide],
+        [first_gain[None], biases, second_cols[None], cos_wide, sin_wide],
         [tokens, out_grad, query_weight, key_weight, value_weight, output_weight],
         2,
     )
-
-    def shared_rows(weight):
-        return lax.dynamic_slice_in_dim(weight, ep * shared_width, shared_width, 1).T
 
     extra_rows = jnp.concatenate([router_weight.T, switch_vector[None, :]], axis=0)
     extra_rows = jnp.pad(extra_rows, ((0, 16 - extra_rows.shape[0]), (0, 0)))
@@ -2983,10 +3003,10 @@
         kept_rows,
         [
             expert_gate_weight[0].T,
-            shared_rows(shared_gate_weight),
+            shared_gate_weight,
             extra_rows,
             expert_up_weight[0].T,
-            shared_rows(shared_up_weight),
+            shared_up_weight,
             expert_down_weight[0],
             shared_down_weight,
         ],
@@ -3031,11 +3051,11 @@
             normed_grad,
             unit_two,
             inv_two,
-            tall(second_cols),
+            second_cols[None],
             out_grad,
             tokens,
             inv_one,
-            tall(own_cols(first_gain)),
+            own_cols(first_gain)[None],
             small,
             queries,
             keys_rot,

time: 586 us -> 585 us (level)
  transfers between devices with their start and end apart: 1 -> 1, of which waited for: 0 -> 0; matrix products, arithmetic and copies ran while one was open for 4% -> 4% of each run, Pallas kernels for 26% -> 27%
where the time goes in v7:
time: 585 us; the launch traced here: 574 us
  Pallas kernels  524 us (90%)
  local copies, waits for them, and re-layouts  26.2 us (4%)
  other arithmetic  12.9 us (2%)
    pallas_call x1, Pallas kernels, experts(): pl.pallas_call(functools.partial(experts_kernel, expert_width, shared_wid...  282 us
    pallas_call x1, Pallas kernels, unwind(): pl.pallas_call(unwind_kernel, out_shape=[jax.ShapeDtypeStruct((rows, cols...  152 us
    pallas_call x1, Pallas kernels, attend(): pl.pallas_call(attend_kernel, out_shape=[result(rows, cols, dtype=full),...  90.4 us
  transfers between devices with their start and end apart: 1, of which 0 were waited for; matrix products, arithmetic and copies ran while one was open for 4% of the time, Pallas kernels for 27%

profile of v7, /device:TPU:9, one launch (start us, length us, event | category | flops | bytes accessed | tf_op | source)
XLA Modules:
  0.0 573.6 jit_solution(6973245035484326630)
XLA Ops:
  0.7 0.7 fusion.5
  1.5 2.4 select_reduce_fusion
  4.3 0.7 select_reduce_fusion.1
  5.0 1.4 convert_reduce_fusion
  7.0 0.7 broadcast_in_dim.74
  7.7 1.0 fusion.3
  8.7 1.3 dynamic_slice.23
  10.0 1.4 fusion.4.extra_ref
  11.4 1.0 pad_maximum_fusion
  13.1 90.4 %attend.1 = (f32[512,512]{1,0:T(8,128)}, f32[512,512]{1,0:T(8,128)}, f32[512,128]{1,0:T(8,128)}, bf16[512,512]{1,0:T(8,128)(2,1)}, bf16[512,2048]{1,0:T(8,128)(2...) custom-call(f32[1,2048]{1,0:T(1,128)} %bitcast.93, ...), custom_call_target="tpu_custom_call" | custom-call | tf_op jit(solution)/shard_map/attend/pallas_call | solution.py:2873
  103.4 281.6 %experts.1 = (f32[528,512]{1,0:T(8,128)}, bf16[512,512]{1,0:T(8,128)(2,1)}, f32[512,128]{1,0:T(8,128)}, f32[3,352,2048]{2,1,0:T(8,128)}, bf16[8,3,176,256]{3,2,1...) custom-call(bf16[512,512]{1,0:T(8,128)(2,1)} %get-tuple-element.41.x, ...), custom_call_target="tpu_custom_call" | custom-call | tf_op jit(solution)/shard_map/experts/pallas_call | solution.py:1743
  385.1 5.1 all-to-all-start
  390.2 1.3 dynamic_slice.26
  391.5 0.7 fusion.17
  392.5 0.8 dynamic-slice_convert_fusion
  393.3 0.7 fusion.8
  394.6 0.9 fusion.19
  395.5 3.0 multiply_reduce_fusion
  398.4 0.6 select_maximum_fusion.small_ref
  399.1 152.4 %unwind.1 = (bf16[512,512]{1,0:T(8,128)(2,1)}, f32[4,256,512]{2,1,0:T(8,128)}, f32[4,16,512]{2,1,0:T(8,128)}) custom-call(f32[512,512]{1,0:T(8,128)} %get-tuple-element.163.dn2_ref, f32[512,512]{1,0:T(8,128)} %get-tuple-element.47.unit_ref, f32[512,128]{1,0:T(8,128)} %get-tuple-element.48.inv_ref, f32[1,512]{1,0:T(1,128)} %bitcast.92, ...), custom_call_target="tpu_custom_call" | custom-call | tf_op jit(solution)/shard_map/unwind/pallas_call | solution.py:2391
  551.5 2.7 slice_bitcast_fusion.2
  554.1 1.0 copy.64
  555.1 0.7 constant_dynamic-slice_fusion.1
  555.9 1.5 fusion.18
  557.4 0.7 dynamic-slice_bitcast_fusion.1
  558.0 1.4 dynamic-slice_bitcast_fusion
  559.4 7.3 %fusion.15 = (f32[1,352,2048]{2,1,0:T(8,128)}, f32[1,2048,352]{1,2,0:T(8,128)}, f32[1,2048,352]{1,2,0:T(8,128)}) fusion(f32[3,352,2048]{2,1,0:T(8,128)} %get-tuple-element.62), kind=kLoop, calls=%fused_computation.60 | loop fusion | bytes 17301504 | tf_op jit(solution)/shard_map/slice | solution.py:3104
  567.3 1.5 fusion.16
  568.8 1.5 copy.62
  570.3 1.5 copy.63
  571.8 0.8 copy.67
  572.6 0.8 copy.68
  (32 shorter events, 3.0 us)
Async XLA Ops:
  0.7 11.8 %copy-start.6 = (f32[512]{0:T(512)S(1)}, f32[512]{0:T(512)}, u32[]{:S(2)}) copy-start(f32[512]{0:T(512)} %param.27) | copy-start | bytes 6148
  0.7 11.8 %copy-start.5 = (f32[512]{0:T(512)S(1)}, f32[512]{0:T(512)}, u32[]{:S(2)}) copy-start(f32[512]{0:T(512)} %param.28) | copy-start | bytes 6148
  0.7 11.8 %copy-start.4 = (f32[512]{0:T(512)S(1)}, f32[512]{0:T(512)}, u32[]{:S(2)}) copy-start(f32[512]{0:T(512)} %param.29) | copy-start | bytes 6148
  385.1 7.3 %copy-start.1 = (f32[512,128]{1,0:T(8,128)S(1)}, f32[512,128]{1,0:T(8,128)}, u32[]{:S(2)}) copy-start(f32[512,128]{1,0:T(8,128)} %get-tuple-element.46) | copy-start | bytes 786436
  385.1 9.3 %copy-start = (bf16[512,512]{1,0:T(8,128)(2,1)S(1)}, bf16[512,512]{1,0:T(8,128)(2,1)}, u32[]{:S(2)}) copy-start(bf16[512,512]{1,0:T(8,128)(2,1)} %get-tuple-element.41.x_ref) | copy-start | bytes 1572868
  385.1 181.7 %all-to-all-start = ((bf16[8,3,176,256]{3,2,1,0:T(8,128)(2,1)}), bf16[8,3,176,256]{3,2,1,0:T(8,128)(2,1)S(1)}, u32[]{:S(2)}, u32[]{:S(2)}) async-start(bf16[8,3,176,256]{3,2,1,0:T(8,128)(2,1)} %get-tuple-element.61), calls=%async_computation | async-start | bytes 4325376 | tf_op jit(solution)/shard_map/all_to_all | solution.py:3017
  568.7 3.1 copy-start.2
  570.3 2.3 copy-start.3

commit v8 on v7

--- a/solution.py
+++ b/solution.py
@@ -448,7 +448,6 @@
 
 
 MESH = pl.DeviceIdType.MESH
-Z_ORDER = (0, 3, 1, 2)
 
 
 def place():
@@ -501,103 +500,6 @@
     lax.fori_loop(0, rows // step, body, 0)
 
 
-def gather_tp_kernel(x_ref, o_ref, send_sem, recv_sem, own_sem):
-    ep, tp, _, _, x, core = place()
-    cols = x_ref.shape[1]
-    sibling = (ep, tp + 1 - 2 * core)
-    across = (ep, tp + 2 - 4 * x)
-    greet([sibling, across])
-    mine = o_ref.at[:, pl.ds(pl.multiple_of(tp * cols, cols), cols)]
-    theirs = o_ref.at[:, pl.ds(pl.multiple_of((tp + 2 - 4 * x) * cols, cols), cols)]
-    out_x = remote(x_ref, mine, send_sem.at[0], recv_sem.at[0], across)
-    out_s = remote(x_ref, mine, send_sem.at[1], recv_sem.at[1], sibling)
-    own = pltpu.make_async_copy(x_ref, mine, own_sem)
-    out_x.start()
-    out_s.start()
-    own.start()
-    remote(x_ref, theirs, send_sem.at[0], recv_sem.at[0], across).wait_recv()
-    passing = remote(theirs, theirs, send_sem.at[2], recv_sem.at[2], sibling)
-    passing.start()
-    out_s.wait_recv()
-    passing.wait_recv()
-    own.wait()
-    out_x.wait_send()
-    out_s.wait_send()
-    passing.wait_send()
-
-
-def gather_tp(value, cid):
-    rows, cols = value.shape
-    return pl.pallas_call(
-        gather_tp_kernel,
-        out_shape=jax.ShapeDtypeStruct((rows, 4 * cols), value.dtype),
-        in_specs=[pl.BlockSpec(memory_space=pl.ANY)],
-        out_specs=pl.BlockSpec(memory_space=pl.ANY),
-        scratch_shapes=[
-            pltpu.SemaphoreType.DMA((3,)),
-            pltpu.SemaphoreType.DMA((3,)),
-            pltpu.SemaphoreType.DMA,
-        ],
-        compiler_params=pltpu.CompilerParams(collective_id=cid, has_side_effects=True),
-        name="gather_tp",
-    )(value)
-
-
-def scatter_tp_kernel(p_ref, o_ref, mine, from_sib, from_x, own_sem, send_sem, recv_sem):
-    ep, tp, _, _, x, core = place()
-    rows, cols = o_ref.shape
-    sibling = (ep, tp + 1 - 2 * core)
-    across = (ep, tp + 2 - 4 * x)
-    greet([sibling, across])
-
-    def part(x_at, core_at):
-        return p_ref.at[:, pl.ds(pl.multiple_of((x_at * 2 + core_at) * cols, cols), cols)]
-
-    sends, owns = [], []
-    for i, x_at in enumerate((1 - x, x)):
-        owns.append(pltpu.make_async_copy(part(x_at, core), mine.at[i], own_sem.at[i]))
-        sends.append(
-            remote(part(x_at, 1 - core), from_sib.at[i], send_sem.at[i], recv_sem.at[i], sibling)
-        )
-        sends[-1].start()
-        owns[-1].start()
-    owns[0].wait()
-    sends[0].wait_recv()
-    add_blocks(mine.at[0], [from_sib.at[0]], rows)
-    out_x = remote(mine.at[0], from_x, send_sem.at[2], recv_sem.at[2], across)
-    out_x.start()
-    owns[1].wait()
-    sends[1].wait_recv()
-    out_x.wait_recv()
-    o_ref[...] = jnp.zeros_like(o_ref)
-    add_blocks(o_ref, [mine.at[1], from_sib.at[1], from_x], rows)
-    out_x.wait_send()
-    sends[0].wait_send()
-    sends[1].wait_send()
-
-
-def scatter_tp(value, cid):
-    rows, cols = value.shape[0], value.shape[1] // 4
-    return pl.pallas_call(
-        scatter_tp_kernel,
-        out_shape=jax.ShapeDtypeStruct((rows, cols), jnp.float32),
-        in_specs=[pl.BlockSpec(memory_space=pl.ANY)],
-        out_specs=pl.BlockSpec(memory_space=pltpu.VMEM),
-        scratch_shapes=[
-            pltpu.VMEM((2, rows, cols), value.dtype),
-            pltpu.VMEM((2, rows, cols), value.dtype),
-            pltpu.VMEM((rows, cols), value.dtype),
-            pltpu.SemaphoreType.DMA((2,)),
-            pltpu.SemaphoreType.DMA((3,)),
-            pltpu.SemaphoreType.DMA((3,)),
-        ],
-        compiler_params=pltpu.CompilerParams(
-            collective_id=cid, has_side_effects=True, vmem_limit_bytes=32 * 2**20
-        ),
-        name="scatter_tp",
-    )(value)
-
-
 def lane_peers():
     ep, tp, z, y, x, core = place()
     to_y, to_x = 1 - 2 * y, 1 - 2 * x
@@ -613,467 +515,6 @@
     y_at = y + (1 - 2 * y) * ((1 - core_at) * da + core_at * db)
     x_at = x + (1 - 2 * x) * (core_at * da + (1 - core_at) * db)
     return z_at * 2 + y_at, x_at * 2 + core_at
-
-
-def gather_all_kernel(x_ref, o_ref, up_sem, down_sem, a_sem, b_sem, s_sem, recv_sem, sib_sem, own_sem):
-    ep, tp, z, y, x, core = place()
-    rows, cols = x_ref.shape
-    peer_a, peer_b, sibling, above, below = lane_peers()
-    greet([peer_a, peer_b, sibling], True)
-
-    def spot(z_at, da, db):
-        group, quarter = lane_spot(z_at, da, db, core)
-        return o_ref.at[
-            pl.ds(pl.multiple_of(group * rows, rows), rows),
-            pl.ds(pl.multiple_of(quarter * cols, cols), cols),
-        ]
-
-    def at(z_at, da, db):
-        return z_at * 4 + da * 2 + db
-
-    def arrived(z_at, da, db):
-        block = spot(z_at, da, db)
-        remote(block, block, s_sem.at[at(z_at, da, db)], recv_sem.at[at(z_at, da, db)], sibling).wait_recv()
-
-    def up(z_at, source):
-        return remote(source, spot(z_at, 0, 0), up_sem.at[z_at], recv_sem.at[at(z_at, 0, 0)], above)
-
-    def down(z_at, source):
-        return remote(source, spot(z_at, 0, 0), down_sem.at[z_at], recv_sem.at[at(z_at, 0, 0)], below)
-
-    def over_a(z_at, source):
-        return remote(source, spot(z_at, 0, 0), a_sem.at[z_at], recv_sem.at[at(z_at, 1, 0)], peer_a)
-
-    def over_b(z_at, da, source):
-        return remote(
-            source, spot(z_at, da, 0), b_sem.at[z_at * 2 + da], recv_sem.at[at(z_at, da, 1)], peer_b
-        )
-
-    def to_sibling(z_at, da, db, source):
-        n = at(z_at, da, db)
-        return remote(source, spot(z_at, da, db), s_sem.at[n], sib_sem.at[n], sibling)
-
-    own = pltpu.make_async_copy(x_ref, spot(z, 0, 0), own_sem)
-    over_b(z, 0, x_ref).start()
-    over_a(z, x_ref).start()
-
-    @pl.when(z < 3)
-    def _():
-        up(z, x_ref).start()
-
-    @pl.when(z > 0)
-    def _():
-        down(z, x_ref).start()
-
-    to_sibling(z, 0, 0, x_ref).start()
-    own.start()
-
-    def from_a(z_at):
-        arrived(z_at, 1, 0)
-        block = spot(z_at, 1, 0)
-        over_b(z_at, 1, block).start()
-        to_sibling(z_at, 1, 0, block).start()
-
-    def from_z(z_at, onward):
-        arrived(z_at, 0, 0)
-        block = spot(z_at, 0, 0)
-        onward(block)
-        over_a(z_at, block).start()
-        over_b(z_at, 0, block).start()
-        to_sibling(z_at, 0, 0, block).start()
-
-    def from_below(z_at):
-        def onward(block):
-            @pl.when(z < 3)
-            def _():
-                up(z_at, block).start()
-
-        from_z(z_at, onward)
-
-    def from_above(z_at):
-        def onward(block):
-            @pl.when(z > 0)
-            def _():
-                down(z_at, block).start()
-
-        from_z(z_at, onward)
-
-    for d in range(1, 4):
-
-        @pl.when(z >= d)
-        def _(d=d):
-            from_below(z - d)
-
-        @pl.when(z + d <= 3)
-        def _(d=d):
-            from_above(z + d)
-
-        if d == 1:
-            from_a(z)
-        else:
-
-            @pl.when(z >= d - 1)
-            def _(d=d):
-                from_a(z - d + 1)
-
-            @pl.when(z + d - 1 <= 3)
-            def _(d=d):
-                from_a(z + d - 1)
-
-    @pl.when(z >= 3)
-    def _():
-        from_a(z - 3)
-
-    @pl.when(z + 3 <= 3)
-    def _():
-        from_a(z + 3)
-
-    def from_b(z_at, da):
-        arrived(z_at, da, 1)
-        to_sibling(z_at, da, 1, spot(z_at, da, 1)).start()
-
-    for da in range(2):
-        from_b(z, da)
-    for d in range(1, 4):
-        for da in range(2):
-
-            @pl.when(z >= d)
-            def _(d=d, da=da):
-                from_b(z - d, da)
-
-            @pl.when(z + d <= 3)
-            def _(d=d, da=da):
-                from_b(z + d, da)
-
-    def finish_sibling(i, carry):
-        block = spot(0, 0, 0)
-        copy = remote(block, block, s_sem.at[i], sib_sem.at[i], sibling)
-        copy.wait_recv()
-        copy.wait_send()
-        return carry
-
-    lax.fori_loop(0, 16, finish_sibling, 0)
-
-    def finish_links(i, carry):
-        over_a(i, x_ref).wait_send()
-        over_b(i, 0, x_ref).wait_send()
-        over_b(i, 1, x_ref).wait_send()
-
-        @pl.when((z < 3) & (i <= z))
-        def _():
-            up(i, x_ref).wait_send()
-
-        @pl.when((z > 0) & (i >= z))
-        def _():
-            down(i, x_ref).wait_send()
-
-        return carry
-
-    lax.fori_loop(0, 4, finish_links, 0)
-    own.wait()
-
-
-def gather_all(value, cid):
-    rows, cols = value.shape
-    return pl.pallas_call(
-        gather_all_kernel,
-        out_shape=jax.ShapeDtypeStruct((8 * rows, 4 * cols), value.dtype),
-        in_specs=[pl.BlockSpec(memory_space=pl.ANY)],
-        out_specs=pl.BlockSpec(memory_space=pl.ANY),
-        scratch_shapes=[
-            pltpu.SemaphoreType.DMA((4,)),
-            pltpu.SemaphoreType.DMA((4,)),
-            pltpu.SemaphoreType.DMA((4,)),
-            pltpu.SemaphoreType.DMA((8,)),
-            pltpu.SemaphoreType.DMA((16,)),
-            pltpu.SemaphoreType.DMA((16,)),
-            pltpu.SemaphoreType.DMA((16,)),
-            pltpu.SemaphoreType.DMA,
-        ],
-        compiler_params=pltpu.CompilerParams(collective_id=cid, has_side_effects=True),
-        name="gather_all",
-    )(value)
-
-
-def z_chain(blocks, totals, from_below, from_above, up_send, up_recv, down_send, down_recv, rows, final):
-    ep, tp, z, _, _, _ = place()
-    above, below = (ep + 2, tp), (ep - 2, tp)
-
-    def up(z_at):
-        return remote(totals(z_at), from_below.at[z_at], up_send.at[z_at], up_recv.at[z_at], above)
-
-    def down(z_at):
-        return remote(totals(z_at), from_above.at[z_at], down_send.at[z_at], down_recv.at[z_at], below)
-
-    for z_at in Z_ORDER:
-        blocks(z_at)
-
-        @pl.when(z_at > z)
-        def _(z_at=z_at):
-            @pl.when(z > 0)
-            def _():
-                up(z_at).wait_recv()
-                add_blocks(totals(z_at), [from_below.at[z_at]], rows)
-
-            up(z_at).start()
-
-        @pl.when(z_at < z)
-        def _(z_at=z_at):
-            @pl.when(z < 3)
-            def _():
-                down(z_at).wait_recv()
-                add_blocks(totals(z_at), [from_above.at[z_at]], rows)
-
-            down(z_at).start()
-
-    for z_at in range(4):
-
-        @pl.when(z_at == z)
-        def _(z_at=z_at):
-            @pl.when(z > 0)
-            def _():
-                up(z_at).wait_recv()
-
-            @pl.when(z < 3)
-            def _():
-                down(z_at).wait_recv()
-
-            @pl.when(z == 0)
-            def _():
-                final(z_at, [from_above.at[z_at]])
-
-            @pl.when(z == 3)
-            def _():
-                final(z_at, [from_below.at[z_at]])
-
-            @pl.when((z > 0) & (z < 3))
-            def _():
-                final(z_at, [from_below.at[z_at], from_above.at[z_at]])
-
-    for z_at in range(4):
-
-        @pl.when(z_at > z)
-        def _(z_at=z_at):
-            up(z_at).wait_send()
-
-        @pl.when(z_at < z)
-        def _(z_at=z_at):
-            down(z_at).wait_send()
-
-
-def scatter_all_kernel(
-    p_ref,
-    o_ref,
-    mine,
-    from_sib,
-    from_b,
-    from_a,
-    from_below,
-    from_above,
-    own_sem,
-    s_send,
-    s_recv,
-    b_send,
-    b_recv,
-    a_send,
-    a_recv,
-    up_send,
-    up_recv,
-    down_send,
-    down_recv,
-):
-    ep, tp, z, y, x, core = place()
-    rows, cols = o_ref.shape
-    peer_a, peer_b, sibling, above, below = lane_peers()
-    greet([peer_a, peer_b, sibling], True)
-
-    def part(z_at, da, db, core_at):
-        group, quarter = lane_spot(z_at, da, db, core_at)
-        return p_ref.at[
-            pl.ds(pl.multiple_of(group * rows, rows), rows),
-            pl.ds(pl.multiple_of(quarter * cols, cols), cols),
-        ]
-
-    def at(z_at, da, db):
-        return z_at * 4 + da * 2 + db
-
-    def own(z_at, da, db):
-        n = at(z_at, da, db)
-        return pltpu.make_async_copy(part(z_at, da, db, core), mine.at[n], own_sem.at[n])
-
-    def to_sibling(z_at, da, db):
-        n = at(z_at, da, db)
-        return remote(
-            part(z_at, da, db, 1 - core), from_sib.at[n], s_send.at[n], s_recv.at[n], sibling
-        )
-
-    for da, db in ((1, 1), (0, 1), (1, 0), (0, 0)):
-        for z_at in Z_ORDER:
-            to_sibling(z_at, da, db).start()
-            own(z_at, da, db).start()
-
-    def here(z_at, da, db):
-        own(z_at, da, db).wait()
-        to_sibling(z_at, da, db).wait_recv()
-        return mine.at[at(z_at, da, db)], from_sib.at[at(z_at, da, db)]
-
-    def over_b(z_at, da):
-        n = z_at * 2 + da
-        return remote(mine.at[at(z_at, da, 1)], from_b.at[n], b_send.at[n], b_recv.at[n], peer_b)
-
-    def over_a(z_at):
-        return remote(mine.at[at(z_at, 1, 0)], from_a.at[z_at], a_send.at[z_at], a_recv.at[z_at], peer_a)
-
-    for da in (1, 0):
-        for z_at in Z_ORDER:
-            own_part, sib_part = here(z_at, da, 1)
-            add_blocks(own_part, [sib_part], rows)
-            over_b(z_at, da).start()
-    for z_at in Z_ORDER:
-        own_part, sib_part = here(z_at, 1, 0)
-        over_b(z_at, 1).wait_recv()
-        add_blocks(own_part, [sib_part, from_b.at[z_at * 2 + 1]], rows)
-        over_a(z_at).start()
-
-    def blocks(z_at):
-        own_part, sib_part = here(z_at, 0, 0)
-        over_b(z_at, 0).wait_recv()
-        over_a(z_at).wait_recv()
-        add_blocks(own_part, [sib_part, from_b.at[z_at * 2], from_a.at[z_at]], rows)
-
-    def final(z_at, others):
-        o_ref[...] = jnp.zeros_like(o_ref)
-        add_blocks(o_ref, [mine.at[at(z_at, 0, 0)], *others], rows)
-
-    z_chain(
-        blocks,
-        lambda z_at: mine.at[at(z_at, 0, 0)],
-        from_below,
-        from_above,
-        up_send,
-        up_recv,
-        down_send,
-        down_recv,
-        rows,
-        final,
-    )
-    for z_at in range(4):
-        over_a(z_at).wait_send()
-        for da in range(2):
-            over_b(z_at, da).wait_send()
-            for db in range(2):
-                to_sibling(z_at, da, db).wait_send()
-
-
-def scatter_all(value, cid):
-    rows, cols = value.shape[0] // 8, value.shape[1] // 4
-    dma = pltpu.SemaphoreType.DMA
-
-    def held(count):
-        return pltpu.VMEM((count, rows, cols), value.dtype)
-
-    return pl.pallas_call(
-        scatter_all_kernel,
-        out_shape=jax.ShapeDtypeStruct((rows, cols), jnp.float32),
-        in_specs=[pl.BlockSpec(memory_space=pl.ANY)],
-        out_specs=pl.BlockSpec(memory_space=pltpu.VMEM),
-        scratch_shapes=[held(16), held(16), held(8), held(4), held(4), held(4)]
-        + [dma((16,)), dma((16,)), dma((16,)), dma((8,)), dma((8,))]
-        + [dma((4,))] * 6,
-        compiler_params=pltpu.CompilerParams(
-            collective_id=cid, has_side_effects=True, vmem_limit_bytes=48 * 2**20
-        ),
-        name="scatter_all",
-    )(value)
-
-
-def scatter_ep_kernel(
-    p_ref, e_ref, o_ref, mine, from_y, from_below, from_above, own_sem, y_send, y_recv, up_send, up_recv, down_send, down_recv
-):
-    ep, tp, z, y, _, _ = place()
-    rows, extra = p_ref.shape[0] // 8, e_ref.shape[0]
-    tall = rows + extra
-    across = (ep + 1 - 2 * y, tp)
-    greet([across], True)
-
-    def part(z_at, y_at):
-        return p_ref.at[pl.ds(pl.multiple_of((z_at * 2 + y_at) * rows, rows), rows), :]
-
-    def own(z_at):
-        return (
-            pltpu.make_async_copy(part(z_at, y), mine.at[z_at, pl.ds(0, rows)], own_sem.at[z_at]),
-            pltpu.make_async_copy(e_ref, mine.at[z_at, pl.ds(rows, extra)], own_sem.at[4 + z_at]),
-        )
-
-    def over_y(z_at):
-        return (
-            remote(
-                part(z_at, 1 - y),
-                from_y.at[z_at, pl.ds(0, rows)],
-                y_send.at[z_at],
-                y_recv.at[z_at],
-                across,
-            ),
-            remote(
-                e_ref,
-                from_y.at[z_at, pl.ds(rows, extra)],
-                y_send.at[4 + z_at],
-                y_recv.at[4 + z_at],
-                across,
-            ),
-        )
-
-    for z_at in Z_ORDER:
-        for copy in over_y(z_at) + own(z_at):
-            copy.start()
-
-    def blocks(z_at):
-        for copy in own(z_at):
-            copy.wait()
-        for copy in over_y(z_at):
-            copy.wait_recv()
-        add_blocks(mine.at[z_at], [from_y.at[z_at]], tall)
-
-    def final(z_at, others):
-        o_ref[...] = jnp.zeros_like(o_ref)
-        add_blocks(o_ref, [mine.at[z_at], *others], tall)
-
-    z_chain(
-        blocks,
-        lambda z_at: mine.at[z_at],
-        from_below,
-        from_above,
-        up_send,
-        up_recv,
-        down_send,
-        down_recv,
-        tall,
-        final,
-    )
-    for z_at in range(4):
-        for copy in over_y(z_at):
-            copy.wait_send()
-
-
-def scatter_ep(value, extra, cid):
-    rows, cols = value.shape[0] // 8, value.shape[1]
-    tall = rows + extra.shape[0]
-    dma = pltpu.SemaphoreType.DMA
-
-    def held():
-        return pltpu.VMEM((4, tall, cols), value.dtype)
-
-    return pl.pallas_call(
-        scatter_ep_kernel,
-        out_shape=jax.ShapeDtypeStruct((tall, cols), jnp.float32),
-        in_specs=[pl.BlockSpec(memory_space=pl.ANY)] * 2,
-        out_specs=pl.BlockSpec(memory_space=pltpu.VMEM),
-        scratch_shapes=[held(), held(), held(), held()] + [dma((8,))] * 3 + [dma((4,))] * 4,
-        compiler_params=pltpu.CompilerParams(
-            collective_id=cid, has_side_effects=True, vmem_limit_bytes=40 * 2**20
-        ),
-        name="scatter_ep",
-    )(value, extra)
 
 
 def experts_kernel(
@@ -1094,7 +535,9 @@
     grad_ref,
     mixed_ref,
     logit_ref,
-    expert_grads_ref,
+    down_grad_ref,
+    gate_grad_ref,
+    up_grad_ref,
     shared_grads_ref,
     all_ref,
     from_sib,
@@ -1458,7 +901,7 @@
         return (
             pltpu.make_async_copy(
                 tile_out.at[kind, pl.ds(0, expert_width)],
-                expert_grads_ref.at[kind, :, cut],
+                (down_grad_ref, gate_grad_ref, up_grad_ref)[kind].at[:, cut],
                 store_sem.at[kind],
             ),
             pltpu.make_async_copy(
@@ -1746,7 +1189,9 @@
             jax.ShapeDtypeStruct((rows + 16, cols), jnp.float32),
             jax.ShapeDtypeStruct((rows, cols), low),
             jax.ShapeDtypeStruct((rows, 128), jnp.float32),
-            jax.ShapeDtypeStruct((3, expert_width, model_dim), jnp.float32),
+            jax.ShapeDtypeStruct((expert_width, model_dim), jnp.float32),
+            jax.ShapeDtypeStruct((expert_width, model_dim), jnp.float32),
+            jax.ShapeDtypeStruct((expert_width, model_dim), jnp.float32),
             jax.ShapeDtypeStruct((sources, 3, shared_width, tile), low),
             jax.ShapeDtypeStruct((total, model_dim), low),
             landing(16),
@@ -1755,7 +1200,7 @@
             landing(4),
         ],
         in_specs=[hbm] * 10 + [vmem],
-        out_specs=[vmem, vmem, vmem] + [hbm] * 7,
+        out_specs=[vmem, vmem, vmem] + [hbm] * 9,
         scratch_shapes=[
             pltpu.VMEM((2 * width, model_dim), low),
             pltpu.VMEM((width, model_dim), low),
@@ -2997,7 +2442,7 @@
     extra_rows = jnp.concatenate([router_weight.T, switch_vector[None, :]], axis=0)
     extra_rows = jnp.pad(extra_rows, ((0, 16 - extra_rows.shape[0]), (0, 0)))
     kept_rows = jnp.pad(kept_own, ((0, 16 - expert_total), (0, 0))).astype(jnp.bfloat16)
-    reduced, layer_out, logit_tile, expert_grads, shared_parts, *_ = experts(
+    reduced, layer_out, logit_tile, down_grad, gate_grad, up_grad, shared_parts, *_ = experts(
         normed_cols,
         grads_all,
         kept_rows,
@@ -3099,9 +2544,9 @@
         shared_up_grad,
         shared_down_grad,
         spread[2],
-        expert_grads[1].T[None],
-        expert_grads[2].T[None],
-        expert_grads[0][None],
+        gate_grad.T[None],
+        up_grad.T[None],
+        down_grad[None],
     )
 
 

time: 585 us -> 585 us (level)
    unnamed x17 -> x26, local copies, waits for them, and re-layouts: 2.61 us -> 10.9 us
    slice x1 -> x0, local copies, waits for them, and re-layouts: 7.34 us -> none  [dense_plan(): expert_grads[0][None]]
  transfers between devices with their start and end apart: 1 -> 1, of which waited for: 0 -> 0; matrix products, arithmetic and copies ran while one was open for 4% -> 3% of each run, Pallas kernels for 27% -> 27%
where the time goes in v8:
time: 585 us; the launch traced here: 574 us
  Pallas kernels  524 us (90%)
  local copies, waits for them, and re-layouts  27.2 us (5%)
  other arithmetic  12.9 us (2%)
    pallas_call x1, Pallas kernels, experts(): pl.pallas_call(functools.partial(experts_kernel, expert_width, shared_wid...  282 us
    pallas_call x1, Pallas kernels, unwind(): pl.pallas_call(unwind_kernel, out_shape=[jax.ShapeDtypeStruct((rows, cols...  152 us
    pallas_call x1, Pallas kernels, attend(): pl.pallas_call(attend_kernel, out_shape=[result(rows, cols, dtype=full),...  90.4 us
  transfers between devices with their start and end apart: 1, of which 0 were waited for; matrix products, arithmetic and copies ran while one was open for 3% of the time, Pallas kernels for 27%

profile of v8, /device:TPU:9, one launch (start us, length us, event | category | flops | bytes accessed | tf_op | source)
XLA Modules:
  0.0 574.4 jit_solution(4042023053592490853)
XLA Ops:
  0.7 0.7 fusion.5
  1.5 2.4 select_reduce_fusion
  4.3 0.7 select_reduce_fusion.1
  5.0 1.4 convert_reduce_fusion
  7.7 1.0 fusion.3
  8.7 1.3 dynamic_slice.23
  10.0 1.4 fusion.4.extra_ref
  11.4 1.0 pad_maximum_fusion
  13.1 90.4 %attend.1 = (f32[512,512]{1,0:T(8,128)}, f32[512,512]{1,0:T(8,128)}, f32[512,128]{1,0:T(8,128)}, bf16[512,512]{1,0:T(8,128)(2,1)}, bf16[512,2048]{1,0:T(8,128)(2...) custom-call(f32[1,2048]{1,0:T(1,128)} %bitcast.91, ...), custom_call_target="tpu_custom_call" | custom-call | tf_op jit(solution)/shard_map/attend/pallas_call | solution.py:2318
  103.4 281.7 %experts.1 = (f32[528,512]{1,0:T(8,128)}, bf16[512,512]{1,0:T(8,128)(2,1)}, f32[512,128]{1,0:T(8,128)}, f32[352,2048]{1,0:T(8,128)}, f32[352,2048]{1,0:T(8,128)}...) custom-call(bf16[512,512]{1,0:T(8,128)(2,1)} %get-tuple-element.43.x, ...), custom_call_target="tpu_custom_call" | custom-call | tf_op jit(solution)/shard_map/experts/pallas_call | solution.py:1186
  385.1 5.1 all-to-all-start
  390.2 1.3 dynamic_slice.26
  391.5 0.7 fusion.16
  392.6 0.8 dynamic-slice_convert_fusion
  393.5 0.7 fusion.8
  394.7 0.9 fusion.18
  395.6 2.6 multiply_reduce_fusion
  398.9 152.3 %unwind.1 = (bf16[512,512]{1,0:T(8,128)(2,1)}, f32[4,256,512]{2,1,0:T(8,128)}, f32[4,16,512]{2,1,0:T(8,128)}) custom-call(f32[512,512]{1,0:T(8,128)} %get-tuple-element.164.dn2_ref, f32[512,512]{1,0:T(8,128)} %get-tuple-element.49.unit_ref, f32[512,128]{1,0:T(8,128)} %get-tuple-element.50.inv_ref, f32[1,512]{1,0:T(1,128)} %bitcast.90, ...), custom_call_target="tpu_custom_call" | custom-call | tf_op jit(solution)/shard_map/unwind/pallas_call | solution.py:1836
  551.2 2.7 slice_bitcast_fusion
  553.9 1.0 copy.64
  554.9 0.7 constant_dynamic-slice_fusion.1
  555.7 1.5 fusion.17
  557.8 1.4 dynamic-slice_bitcast_fusion
  559.7 1.5 fusion.15
  561.2 1.5 copy.62
  562.7 1.5 copy.63
  564.3 0.8 copy.70
  565.1 0.8 copy.71
  565.9 3.9 copy.72
  569.7 1.6 copy.73
  571.3 1.3 copy-done.2
  572.6 1.6 copy.74
  (40 shorter events, 5.0 us)
Async XLA Ops:
  0.7 11.8 %copy-start.9 = (f32[512]{0:T(512)S(1)}, f32[512]{0:T(512)}, u32[]{:S(2)}) copy-start(f32[512]{0:T(512)} %param.27) | copy-start | bytes 6148
  0.7 11.8 %copy-start.8 = (f32[512]{0:T(512)S(1)}, f32[512]{0:T(512)}, u32[]{:S(2)}) copy-start(f32[512]{0:T(512)} %param.28) | copy-start | bytes 6148
  0.7 11.8 %copy-start.7 = (f32[512]{0:T(512)S(1)}, f32[512]{0:T(512)}, u32[]{:S(2)}) copy-start(f32[512]{0:T(512)} %param.29) | copy-start | bytes 6148
  385.1 7.3 %copy-start.4 = (f32[512,128]{1,0:T(8,128)S(1)}, f32[512,128]{1,0:T(8,128)}, u32[]{:S(2)}) copy-start(f32[512,128]{1,0:T(8,128)} %get-tuple-element.48) | copy-start | bytes 786436
  385.1 9.4 %copy-start = (bf16[512,512]{1,0:T(8,128)(2,1)S(1)}, bf16[512,512]{1,0:T(8,128)(2,1)}, u32[]{:S(2)}) copy-start(bf16[512,512]{1,0:T(8,128)(2,1)} %get-tuple-element.43.x_ref) | copy-start | bytes 1572868
  385.1 174.1 %all-to-all-start = ((bf16[8,3,176,256]{3,2,1,0:T(8,128)(2,1)}), bf16[8,3,176,256]{3,2,1,0:T(8,128)(2,1)S(1)}, u32[]{:S(2)}, u32[]{:S(2)}) async-start(bf16[8,3,176,256]{3,2,1,0:T(8,128)(2,1)} %get-tuple-element.63), calls=%async_computation | async-start | bytes 4325376 | tf_op jit(solution)/shard_map/all_to_all | solution.py:2462
  392.6 3.1 copy-start.1
  562.7 1.5 copy-start.5
  562.7 2.3 copy-start.6
  565.9 3.9 copy-start.3
  569.7 2.9 copy-start.2
